TPU v7x, 32 devices: a whole 2x2x4 slice. The times are simulated.
32 devices in a mesh: ctx: 8 (over z, y), head: 4 (over x, core).
Axes of the slice: x: 2, y: 2, z: 4, core: 2. Of those that a mesh axis runs over, the one named last changes fastest.
Arguments:
- inputs: bfloat16 [2048, 2048], P('ctx', 'head'), may hold values from -6 to 6
- cotangent: bfloat16 [2048, 2048], P('ctx', 'head'), may hold values from -6 to 6
- w_query: float32 [2048, 2048], P('ctx', 'head'), may hold values from -0.125 to 0.125
- w_key: float32 [2048, 2048], P('ctx', 'head'), may hold values from -0.125 to 0.125
- w_value: float32 [2048, 2048], P('ctx', 'head'), may hold values from -0.125 to 0.125
- w_out: float32 [2048, 2048], P('head', 'ctx'), may hold values from -0.125 to 0.125
- w_gate: float32 [2048, 8192], P('ctx', 'head'), may hold values from -0.125 to 0.125
- w_up: float32 [2048, 8192], P('ctx', 'head'), may hold values from -0.125 to 0.125
- w_down: float32 [8192, 2048], P('head', 'ctx'), may hold values from -0.0625 to 0.0625
- query_gain: float32 [2048], P('head'), may hold values from 0.8 to 2
- key_gain: float32 [2048], P('head'), may hold values from 0.8 to 2
- attn_gain: float32 [2048], P('head'), may hold values from 0.5 to 1.5
- ffn_gain: float32 [2048], P('head'), may hold values from 0.5 to 1.5
- lengths: int32 [4], replicated, may hold values from 1 to 1824, 2048 in all
- block_order: int32 [64], replicated, may hold values from 0 to 63, as said below
Outputs:
- outputs: bfloat16 [2048, 2048], P('ctx', 'head')
- input_grad: bfloat16 [2048, 2048], P('ctx', 'head')
- grad_query: float32 [2048, 2048], P('ctx', 'head')
- grad_key: float32 [2048, 2048], P('ctx', 'head')
- grad_value: float32 [2048, 2048], P('ctx', 'head')
- grad_out: float32 [2048, 2048], P('head', 'ctx')
- grad_gate: float32 [2048, 8192], P('ctx', 'head')
- grad_up: float32 [2048, 8192], P('ctx', 'head')
- grad_down: float32 [8192, 2048], P('head', 'ctx')
- query_gain_grad: float32 [2048], P('head')
- key_gain_grad: float32 [2048], P('head')
- attn_gain_grad: float32 [2048], P('head')
- ffn_gain_grad: float32 [2048], P('head')
Inputs may be any that keep to these rules, and one draw needn't show every extreme that they name: `block_order`: every value appears once. Entries j * 8 to (j + 1) * 8 - 1 (the blocks stored on index j of ctx) take every remainder modulo 2048 / 256 exactly once. `lengths`: they sum to 2048; the longest has exactly 1824 tokens.
All inputs are finite; a program needn't handle non-finite values.
Results may differ from a plain program's by a relative error of at most 0.025.
Values may be sent and summed in bfloat16 or wider, within the bound.
A program may use at most 192 MiB of HBM per device.

v0:
```python
import math

import jax
import jax.numpy as jnp
from jax import lax
from jax.sharding import PartitionSpec as P

D = 2048
HD = 128


EPSILON = 1e-06
ROPE_THETA = 500000.0
MASKED = -1e30


def full_rows(piece):
    return lax.all_gather(piece, "head", axis=1, tiled=True)


def head_sums(term):
    return lax.psum_scatter(
        term.astype(jnp.bfloat16), "head", scatter_dimension=1, tiled=True
    ).astype(jnp.float32)


def row_single(term):
    return lax.psum(term, "head")


def row_pair(first, second):
    return lax.psum((first, second), "head")


def gather_weights(w_query, w_key, w_value, w_out, w_gate, w_up, w_down):
    row_parts = (
        lax.all_gather(w_query.astype(jnp.bfloat16), "ctx", axis=0, tiled=True),
        lax.all_gather(w_key.astype(jnp.bfloat16), "ctx", axis=0, tiled=True),
        lax.all_gather(w_value.astype(jnp.bfloat16), "ctx", axis=0, tiled=True),
        lax.all_gather(w_gate.astype(jnp.bfloat16), "ctx", axis=0, tiled=True),
        lax.all_gather(w_up.astype(jnp.bfloat16), "ctx", axis=0, tiled=True),
    )
    col_parts = (
        lax.all_gather(w_out.astype(jnp.bfloat16), "ctx", axis=1, tiled=True),
        lax.all_gather(w_down.astype(jnp.bfloat16), "ctx", axis=1, tiled=True),
    )
    return tuple(row_parts) + tuple(col_parts)


def sequence_tables(logical, lengths):
    seq_ends = jnp.cumsum(lengths)
    seq_starts = seq_ends - lengths
    number = jnp.sum((logical[:, None] >= seq_ends[None, :]).astype(jnp.int32), axis=1)
    member = number[:, None] == jnp.arange(lengths.shape[0], dtype=jnp.int32)[None, :]
    offset = logical - jnp.sum(jnp.where(member, seq_starts[None, :], 0), axis=1)
    return (number, offset)


def rotate(values, offset):
    half_dim = HD // 2
    inverse = jnp.power(ROPE_THETA, -jnp.arange(half_dim, dtype=jnp.float32) * 2.0 / HD)
    angles = offset.astype(jnp.float32)[:, None] * inverse[None, :]
    cosine = jnp.cos(angles)[:, None, :]
    sine_part = jnp.sin(angles)[:, None, :]
    first_half = values[..., :half_dim]
    second_half = values[..., half_dim:]
    return jnp.concatenate(
        [
            first_half * cosine - second_half * sine_part,
            second_half * cosine + first_half * sine_part,
        ],
        axis=-1,
    )


def norm_backward(grad_in, values, factor, gain):
    gain_term = jnp.sum(grad_in * values * factor[:, None], axis=0)
    weighted = grad_in * gain
    row_dot = row_single(jnp.sum(weighted * values, axis=1))
    grad_values = (
        factor[:, None] * weighted - values * (factor * factor * factor * row_dot / D)[:, None]
    )
    return (grad_values, gain_term)


def on_device(
    inputs,
    cotangent,
    w_query,
    w_key,
    w_value,
    w_out,
    w_gate,
    w_up,
    w_down,
    query_gain,
    key_gain,
    attn_gain,
    ffn_gain,
    lengths,
    block_order,
):
    shards = lax.axis_size("ctx")
    position = lax.axis_index("ctx")
    tok_rows, width_part = inputs.shape
    block_rows = tok_rows // shards
    total_tokens = tok_rows * shards
    local_heads = width_part // HD
    scaling = 1.0 / math.sqrt(HD)
    shard_range = jnp.arange(shards, dtype=jnp.int32)
    order_table = block_order.reshape(shards, shards)
    target = order_table % shards
    choose = target[:, :, None] == shard_range[None, None, :]
    stream = jnp.sum(jnp.where(choose, order_table[:, :, None], 0), axis=1)
    stream_blocks = jnp.transpose(stream).reshape(-1)
    logical = (
        stream_blocks[:, None] * block_rows + jnp.arange(block_rows, dtype=jnp.int32)[None, :]
    ).reshape(-1)
    own_target = lax.dynamic_index_in_dim(target, position, 0, keepdims=False)
    send_order = jnp.sum(
        jnp.where(own_target[:, None] == shard_range[None, :], shard_range[:, None], 0), axis=0
    )

    def deal_out(values):
        return values.reshape(shards, block_rows, width_part)[send_order].reshape(
            tok_rows, width_part
        )

    def undeal(values):
        return values.reshape(shards, block_rows, width_part)[own_target].reshape(
            tok_rows, width_part
        )

    local_in, local_cot = (
        lax.all_to_all(deal_out(inputs), "ctx", split_axis=0, concat_axis=0, tiled=True),
        lax.all_to_all(deal_out(cotangent), "ctx", split_axis=0, concat_axis=0, tiled=True),
    )
    number_all, offset_all = sequence_tables(logical, lengths)
    number_own = lax.dynamic_slice_in_dim(number_all, position * tok_rows, tok_rows)
    offset_own = lax.dynamic_slice_in_dim(offset_all, position * tok_rows, tok_rows)
    logical_own = lax.dynamic_slice_in_dim(logical, position * tok_rows, tok_rows)
    query_full, key_full, value_full, gate_full, up_full, out_full, down_full = gather_weights(
        w_query, w_key, w_value, w_out, w_gate, w_up, w_down
    )
    full_in = full_rows(local_in)
    query_proj = jnp.dot(full_in, query_full, preferred_element_type=jnp.float32)
    key_proj = jnp.dot(full_in, key_full, preferred_element_type=jnp.float32)
    value_proj = jnp.dot(full_in, value_full, preferred_element_type=jnp.float32)
    query_sq, key_sq = row_pair(
        jnp.sum(query_proj * query_proj, axis=1), jnp.sum(key_proj * key_proj, axis=1)
    )
    query_scale = lax.rsqrt(query_sq / D + EPSILON)
    key_scale = lax.rsqrt(key_sq / D + EPSILON)
    query_rot = rotate(
        (query_proj * query_scale[:, None] * query_gain).reshape(tok_rows, local_heads, HD),
        offset_own,
    ).astype(jnp.bfloat16)
    key_rot = rotate(
        (key_proj * key_scale[:, None] * key_gain).reshape(tok_rows, local_heads, HD), offset_own
    ).astype(jnp.bfloat16)
    value_low = value_proj.astype(jnp.bfloat16).reshape(tok_rows, local_heads, HD)
    keys_all, values_all = (
        lax.all_gather(key_rot, "ctx", axis=0, tiled=True),
        lax.all_gather(value_low, "ctx", axis=0, tiled=True),
    )
    key_span = math.gcd(total_tokens, 1024)
    key_turns = total_tokens // key_span
    pieces = (
        keys_all.reshape(key_turns, key_span, local_heads, HD),
        values_all.reshape(key_turns, key_span, local_heads, HD),
        number_all.reshape(key_turns, key_span),
        logical.reshape(key_turns, key_span),
    )

    def scores_of(key_piece, number_piece, logical_piece):
        raw_scores = (
            jnp.einsum("qhd,khd->hqk", query_rot, key_piece, preferred_element_type=jnp.float32)
            * scaling
        )
        allowed = (number_own[:, None] == number_piece[None, :]) & (
            logical_piece[None, :] <= logical_own[:, None]
        )
        return (raw_scores, allowed)

    def stat_turn(running, piece_set):
        running_max, running_sum = running
        raw_scores, allowed = scores_of(piece_set[0], piece_set[2], piece_set[3])
        masked_scores = jnp.where(allowed[None], raw_scores, MASKED)
        new_max = jnp.maximum(running_max, jnp.max(masked_scores, axis=2))
        fresh = jnp.sum(
            jnp.where(allowed[None], jnp.exp(masked_scores - new_max[..., None]), 0.0), axis=2
        )
        return ((new_max, running_sum * jnp.exp(running_max - new_max) + fresh), None)

    start_max = jnp.full((local_heads, tok_rows), MASKED, jnp.float32)
    start_sum = jnp.zeros((local_heads, tok_rows), jnp.float32)
    final_max, final_sum = lax.scan(stat_turn, (start_max, start_sum), pieces)[0]
    log_total = final_max + jnp.log(final_sum)

    def out_turn(accum, piece_set):
        raw_scores, allowed = scores_of(piece_set[0], piece_set[2], piece_set[3])
        weights_low = jnp.where(
            allowed[None], jnp.exp(raw_scores - log_total[..., None]), 0.0
        ).astype(jnp.bfloat16)
        return (
            accum
            + jnp.einsum(
                "hqk,khd->qhd", weights_low, piece_set[1], preferred_element_type=jnp.float32
            ),
            None,
        )

    attended = lax.scan(out_turn, jnp.zeros((tok_rows, local_heads, HD), jnp.float32), pieces)[0]
    attended_low = attended.reshape(tok_rows, width_part).astype(jnp.bfloat16)
    attn_part = head_sums(jnp.dot(attended_low, out_full, preferred_element_type=jnp.float32))
    attn_scale = lax.rsqrt(row_single(jnp.sum(attn_part * attn_part, axis=1)) / D + EPSILON)
    residual = local_in.astype(jnp.float32) + attn_part * attn_scale[:, None] * attn_gain
    residual_full = full_rows(residual.astype(jnp.bfloat16))
    gate_proj = jnp.dot(residual_full, gate_full, preferred_element_type=jnp.float32)
    up_proj = jnp.dot(residual_full, up_full, preferred_element_type=jnp.float32)
    gate_sigmoid = jax.nn.sigmoid(gate_proj)
    mixed_hidden = (gate_proj * gate_sigmoid * up_proj).astype(jnp.bfloat16)
    ffn_part = head_sums(jnp.dot(mixed_hidden, down_full, preferred_element_type=jnp.float32))
    ffn_scale = lax.rsqrt(row_single(jnp.sum(ffn_part * ffn_part, axis=1)) / D + EPSILON)
    result = residual + ffn_part * ffn_scale[:, None] * ffn_gain
    query_full, key_full, value_full, gate_full, up_full, out_full, down_full = gather_weights(
        w_query, w_key, w_value, w_out, w_gate, w_up, w_down
    )
    grad_result = local_cot.astype(jnp.float32)
    grad_ffn, ffn_gain_term = norm_backward(grad_result, ffn_part, ffn_scale, ffn_gain)
    grad_ffn_low = full_rows(grad_ffn.astype(jnp.bfloat16))
    down_grad = jnp.einsum(
        "tf,td->fd", mixed_hidden, grad_ffn_low, preferred_element_type=jnp.float32
    )
    grad_mixed = jnp.einsum(
        "td,fd->tf", grad_ffn_low, down_full, preferred_element_type=jnp.float32
    )
    grad_gate_low = (
        grad_mixed * up_proj * gate_sigmoid * (1.0 + gate_proj * (1.0 - gate_sigmoid))
    ).astype(jnp.bfloat16)
    grad_up_low = (grad_mixed * gate_proj * gate_sigmoid).astype(jnp.bfloat16)
    gate_grad = jnp.einsum(
        "td,tf->df", residual_full, grad_gate_low, preferred_element_type=jnp.float32
    )
    up_grad = jnp.einsum(
        "td,tf->df", residual_full, grad_up_low, preferred_element_type=jnp.float32
    )
    resid_term = jnp.einsum(
        "tf,df->td", grad_gate_low, gate_full, preferred_element_type=jnp.float32
    ) + jnp.einsum("tf,df->td", grad_up_low, up_full, preferred_element_type=jnp.float32)
    grad_residual = grad_result + head_sums(resid_term)
    grad_attn, attn_gain_term = norm_backward(grad_residual, attn_part, attn_scale, attn_gain)
    grad_attn_low = full_rows(grad_attn.astype(jnp.bfloat16))
    out_grad = jnp.einsum(
        "te,td->ed", attended_low, grad_attn_low, preferred_element_type=jnp.float32
    )
    grad_heads = (
        jnp.einsum("td,ed->te", grad_attn_low, out_full, preferred_element_type=jnp.float32)
        .astype(jnp.bfloat16)
        .reshape(tok_rows, local_heads, HD)
    )
    row_delta = jnp.transpose(jnp.sum(grad_heads.astype(jnp.float32) * attended, axis=2))

    def score_grads(key_piece, value_piece, number_piece, logical_piece):
        raw_scores, allowed = scores_of(key_piece, number_piece, logical_piece)
        probabilities = jnp.where(allowed[None], jnp.exp(raw_scores - log_total[..., None]), 0.0)
        grad_probs = jnp.einsum(
            "qhd,khd->hqk", grad_heads, value_piece, preferred_element_type=jnp.float32
        )
        grad_scores = (probabilities * (grad_probs - row_delta[..., None])).astype(jnp.bfloat16)
        return (probabilities, grad_scores)

    zero_heads = jnp.zeros((tok_rows, local_heads, HD), jnp.float32)

    def back_turn(grad_acc, piece_set):
        key_piece, value_piece, number_piece, logical_piece = piece_set
        probabilities, grad_scores = score_grads(
            key_piece, value_piece, number_piece, logical_piece
        )
        grad_acc = (
            grad_acc
            + jnp.einsum("hqk,khd->qhd", grad_scores, key_piece, preferred_element_type=jnp.float32)
            * scaling
        )
        key_term = (
            jnp.einsum("hqk,qhd->khd", grad_scores, query_rot, preferred_element_type=jnp.float32)
            * scaling
        )
        value_term = jnp.einsum(
            "hqk,qhd->khd",
            probabilities.astype(jnp.bfloat16),
            grad_heads,
            preferred_element_type=jnp.float32,
        )
        return (grad_acc, (key_term, value_term))

    grad_query_rot, key_value_terms = lax.scan(back_turn, zero_heads, pieces)
    key_terms = key_value_terms[0].reshape(total_tokens, local_heads, HD)
    value_terms = key_value_terms[1].reshape(total_tokens, local_heads, HD)
    grad_key_rot, grad_value_own = (
        lax.psum_scatter(
            key_terms.astype(jnp.bfloat16), "ctx", scatter_dimension=0, tiled=True
        ).astype(jnp.float32),
        lax.psum_scatter(
            value_terms.astype(jnp.bfloat16), "ctx", scatter_dimension=0, tiled=True
        ).astype(jnp.float32),
    )
    grad_query_normed = rotate(grad_query_rot, -offset_own).reshape(tok_rows, width_part)
    grad_key_normed = rotate(grad_key_rot, -offset_own).reshape(tok_rows, width_part)
    query_gain_term = jnp.sum(grad_query_normed * query_proj * query_scale[:, None], axis=0)
    key_gain_term = jnp.sum(grad_key_normed * key_proj * key_scale[:, None], axis=0)
    weighted_query = grad_query_normed * query_gain
    weighted_key = grad_key_normed * key_gain
    query_dot, key_dot = row_pair(
        jnp.sum(weighted_query * query_proj, axis=1), jnp.sum(weighted_key * key_proj, axis=1)
    )
    grad_query_low = (
        query_scale[:, None] * weighted_query
        - query_proj * (query_scale * query_scale * query_scale * query_dot / D)[:, None]
    ).astype(jnp.bfloat16)
    grad_key_low = (
        key_scale[:, None] * weighted_key
        - key_proj * (key_scale * key_scale * key_scale * key_dot / D)[:, None]
    ).astype(jnp.bfloat16)
    grad_value_low = grad_value_own.reshape(tok_rows, width_part).astype(jnp.bfloat16)
    query_grad = jnp.einsum(
        "td,te->de", full_in, grad_query_low, preferred_element_type=jnp.float32
    )
    key_grad = jnp.einsum("td,te->de", full_in, grad_key_low, preferred_element_type=jnp.float32)
    value_grad = jnp.einsum(
        "td,te->de", full_in, grad_value_low, preferred_element_type=jnp.float32
    )
    input_term = jnp.einsum(
        "te,de->td", grad_query_low, query_full, preferred_element_type=jnp.float32
    )
    input_term = input_term + jnp.einsum(
        "te,de->td", grad_key_low, key_full, preferred_element_type=jnp.float32
    )
    input_term = input_term + jnp.einsum(
        "te,de->td", grad_value_low, value_full, preferred_element_type=jnp.float32
    )
    grad_input = grad_residual + head_sums(input_term)
    row_grads = (
        lax.psum_scatter(
            query_grad.astype(jnp.bfloat16), "ctx", scatter_dimension=0, tiled=True
        ).astype(jnp.float32),
        lax.psum_scatter(
            key_grad.astype(jnp.bfloat16), "ctx", scatter_dimension=0, tiled=True
        ).astype(jnp.float32),
        lax.psum_scatter(
            value_grad.astype(jnp.bfloat16), "ctx", scatter_dimension=0, tiled=True
        ).astype(jnp.float32),
        lax.psum_scatter(
            gate_grad.astype(jnp.bfloat16), "ctx", scatter_dimension=0, tiled=True
        ).astype(jnp.float32),
        lax.psum_scatter(
            up_grad.astype(jnp.bfloat16), "ctx", scatter_dimension=0, tiled=True
        ).astype(jnp.float32),
    )
    col_grads = (
        lax.psum_scatter(
            out_grad.astype(jnp.bfloat16), "ctx", scatter_dimension=1, tiled=True
        ).astype(jnp.float32),
        lax.psum_scatter(
            down_grad.astype(jnp.bfloat16), "ctx", scatter_dimension=1, tiled=True
        ).astype(jnp.float32),
    )
    gain_totals = lax.psum((query_gain_term, key_gain_term, attn_gain_term, ffn_gain_term), "ctx")
    back_result, back_grad = (
        lax.all_to_all(result.astype(jnp.bfloat16), "ctx", split_axis=0, concat_axis=0, tiled=True),
        lax.all_to_all(
            grad_input.astype(jnp.bfloat16), "ctx", split_axis=0, concat_axis=0, tiled=True
        ),
    )
    return (
        undeal(back_result),
        undeal(back_grad),
        row_grads[0],
        row_grads[1],
        row_grads[2],
        col_grads[0],
        row_grads[3],
        row_grads[4],
        col_grads[1],
        gain_totals[0],
        gain_totals[1],
        gain_totals[2],
        gain_totals[3],
    )


def solution(mesh):
    return jax.shard_map(
        on_device,
        mesh=mesh,
        in_specs=(
            P("ctx", "head"),
            P("ctx", "head"),
            P("ctx", "head"),
            P("ctx", "head"),
            P("ctx", "head"),
            P("head", "ctx"),
            P("ctx", "head"),
            P("ctx", "head"),
            P("head", "ctx"),
            P("head"),
            P("head"),
            P("head"),
            P("head"),
            P(),
            P(),
        ),
        out_specs=(
            P("ctx", "head"),
            P("ctx", "head"),
            P("ctx", "head"),
            P("ctx", "head"),
            P("ctx", "head"),
            P("head", "ctx"),
            P("ctx", "head"),
            P("ctx", "head"),
            P("head", "ctx"),
            P("head"),
            P("head"),
            P("head"),
            P("head"),
        ),
        check_vma=False,
    )
```

profile of v0, /device:TPU:1, one launch (start us, length us, event | category | flops | bytes accessed | tf_op | source)
XLA Modules:
  0.0 1874.9 jit_solution(10419693577056880299)
XLA Ops:
  8.8 13.6 all_to_all.33
  29.8 10.8 all-gather.14.cloned.1.call-done
  40.6 50.5 %all-gather.20.cloned.1.call-done = bf16[2048,512]{1,0:T(8,128)(2,1)} async-done(((bf16[256,512]{1,0:T(8,128)(2,1)}), bf16[2048,512]{1,0:T(8,128)(2,1)}) %all-gather.20.cloned.1.call-update) | async-done | bytes 2097168 | tf_op jit(solution)/shard_map/all_gather | solution.py:38
  91.1 2.7 multiply_reduce_fusion.4
  93.9 47.8 %all-gather.24.cloned.1.call-done = bf16[2048,512]{1,0:T(8,128)(2,1)} async-done(((bf16[256,512]{1,0:T(8,128)(2,1)}), bf16[2048,512]{1,0:T(8,128)(2,1)}) %all-gather.24.cloned.1.call-update) | async-done | bytes 2097168 | tf_op jit(solution)/shard_map/all_gather | solution.py:37
  144.0 6.8 all-reduce.2
  153.8 38.2 %all-gather.16.cloned.1.call-done = bf16[2048,512]{1,0:T(8,128)(2,1)} async-done(((bf16[256,512]{1,0:T(8,128)(2,1)}), bf16[2048,512]{1,0:T(8,128)(2,1)}) %all-gather.16.cloned.1.call-update) | async-done | bytes 2097168 | tf_op jit(solution)/shard_map/all_gather | solution.py:39
  196.5 45.9 %all-gather.22.cloned.1.call-done = bf16[2048,4,128]{2,0,1:T(8,128)(2,1)} async-done(((bf16[256,4,128]{2,0,1:T(8,128)(2,1)}), bf16[2048,4,128]{2,0,1:T(8,128)(2,1)}) %all-gather.22.cloned.1.call-update) | async-done | bytes 2097168 | tf_op jit(solution)/shard_map/all_gather | solution.py:163
  244.2 12.8 while.39
  244.6 2.8 fusion.160
  247.3 3.2 select_reduce_fusion.5
  251.0 2.8 fusion.160
  253.8 3.2 select_reduce_fusion.5
  257.0 35.8 %all-gather.18.cloned.1.call-done = bf16[2048,4,128]{2,0,1:T(8,128)(2,1)} async-done(((bf16[256,4,128]{2,0,1:T(8,128)(2,1)}), bf16[2048,4,128]{2,0,1:T(8,128)(2,1)}) %all-gather.18.cloned.1.call-update) | async-done | bytes 2097168 | tf_op jit(solution)/shard_map/all_gather | solution.py:164
  292.8 6.0 while.40
  300.6 44.9 %all-gather.26.cloned.1.call-done = bf16[512,2048]{1,0:T(8,128)(2,1)} async-done(((bf16[512,256]{1,0:T(8,128)(2,1)}), bf16[512,2048]{1,0:T(8,128)(2,1)}) %all-gather.26.cloned.1.call-update) | async-done | bytes 2097168 | tf_op jit(solution)/shard_map/all_gather | solution.py:44
  345.5 3.3 convolution_convert_fusion.7
  349.0 23.8 %reduce-scatter.14.cloned.1.call-done = bf16[256,512]{1,0:T(8,128)(2,1)} async-done(((bf16[256,2048]{1,0:T(8,128)(2,1)}), bf16[256,512]{1,0:T(8,128)(2,1)}) %reduce-scatter.14.cloned.1.call-update) | async-done | bytes 262160 | tf_op jit(solution)/shard_map/reduce_scatter | solution.py:22
  373.8 5.7 psum.86
  381.5 2.7 convert_element_type.203
  384.3 2.7 convert_element_type.204
  387.0 2.7 convert_element_type.206
  390.0 9.8 all-gather.28.cloned.1.call-done
  399.8 126.9 %all-gather.30.cloned.1.call-done = bf16[2048,2048]{1,0:T(8,128)(2,1)} async-done(((bf16[256,2048]{1,0:T(8,128)(2,1)}), bf16[2048,2048]{1,0:T(8,128)(2,1)}) %all-gather.30.cloned.1.call-update) | async-done | bytes 8388624 | tf_op jit(solution)/shard_map/all_gather | solution.py:40
  526.8 7.4 fusion.85
  534.1 118.7 %all-gather.32.cloned.1.call-done = bf16[2048,2048]{1,0:T(8,128)(2,1)} async-done(((bf16[256,2048]{1,0:T(8,128)(2,1)}), bf16[2048,2048]{1,0:T(8,128)(2,1)}) %all-gather.32.cloned.1.call-update) | async-done | bytes 8388624 | tf_op jit(solution)/shard_map/all_gather | solution.py:41
  652.8 8.2 multiply_convert_fusion.2
  661.0 118.1 %all-gather.34.cloned.1.call-done = bf16[2048,2048]{1,0:T(8,128)(2,1)} async-done(((bf16[2048,256]{1,0:T(8,128)(2,1)}), bf16[2048,2048]{1,0:T(8,128)(2,1)}) %all-gather.34.cloned.1.call-update) | async-done | bytes 8388624 | tf_op jit(solution)/shard_map/all_gather | solution.py:45
  779.1 7.1 convolution_convert_fusion.8
  787.5 3.4 all-to-all-start.2
  791.0 18.8 %reduce-scatter.16.cloned.1.call-done = bf16[256,512]{1,0:T(8,128)(2,1)} async-done(((bf16[256,2048]{1,0:T(8,128)(2,1)}), bf16[256,512]{1,0:T(8,128)(2,1)}) %reduce-scatter.16.cloned.1.call-update) | async-done | bytes 262160 | tf_op jit(solution)/shard_map/reduce_scatter | solution.py:22
  810.9 5.7 psum.87
  818.4 5.7 psum.88
  826.4 18.1 all-gather.36.cloned.1.call-done
  844.6 7.8 multiply_convert_fusion
  852.4 6.5 fusion.86
  859.0 6.8 fusion.44
  865.8 24.6 %reduce-scatter.18.cloned.1.call-done = bf16[256,512]{1,0:T(8,128)(2,1)} async-done(((bf16[256,2048]{1,0:T(8,128)(2,1)}), bf16[256,512]{1,0:T(8,128)(2,1)}) %reduce-scatter.18.cloned.1.call-update) | async-done | bytes 262160 | tf_op jit(solution)/shard_map/reduce_scatter | solution.py:22
  892.3 6.4 psum.89
  901.8 18.2 all-gather.38.cloned.1.call-done
  919.9 3.4 convolution_convert_fusion.9
  927.8 22.8 %while.41 = (s32[]{:T(128)}, f32[256,4,128]{0,2,1:T(8,128)S(1)}, bf16[2,1024,4,128]{3,1,0,2:T(8,128)(2,1)}, bf16[2,1024,4,128]{3,1,0,2:T(8,128)(2,1)}, bf16[2,10...) while((s32[]{:T(128)}, f32[256,4,128]{0,2,1:T(8,128)S(1)}, ...), condition=%wide.region_28.29_spmd.clone, body=%wide.region_27.28_spmd.clone.sunk | while | flops 1354366976 | bytes 88940432 | solution.py:297
  936.2 3.0 bitcast_dynamic-update-slice_fusion.5
  947.5 3.0 bitcast_dynamic-update-slice_fusion.5
  952.2 64.6 %reduce-scatter.20.cloned.1.call-done = bf16[256,4,128]{2,0,1:T(8,128)(2,1)} async-done(((bf16[2048,4,128]{2,0,1:T(8,128)(2,1)}), bf16[256,4,128]{2,0,1:T(8,128)(2,1)}) %reduce-scatter.20.cloned.1.call-update) | async-done | bytes 262160 | tf_op jit(solution)/shard_map/reduce_scatter | solution.py:301
  1020.3 7.5 all-reduce.1
  1030.4 58.2 %reduce-scatter.22.cloned.1.call-done = bf16[256,4,128]{2,0,1:T(8,128)(2,1)} async-done(((bf16[2048,4,128]{2,0,1:T(8,128)(2,1)}), bf16[256,4,128]{2,0,1:T(8,128)(2,1)}) %reduce-scatter.22.cloned.1.call-update) | async-done | bytes 262160 | tf_op jit(solution)/shard_map/reduce_scatter | solution.py:304
  1104.1 5.7 convolution_convert_fusion
  1111.3 5.7 convolution_convert_fusion.2
  1118.2 5.7 convolution_convert_fusion.1
  1123.9 4.1 all-to-all-start.1
  1129.8 5.5 all-to-all-done.1
  1135.3 7.5 all-to-all-start.3
  1144.8 50.5 %reduce-scatter.32.cloned.1.call-done = bf16[512,256]{1,0:T(8,128)(2,1)} async-done(((bf16[512,2048]{1,0:T(8,128)(2,1)}), bf16[512,256]{1,0:T(8,128)(2,1)}) %reduce-scatter.32.cloned.1.call-update) | async-done | bytes 262160 | tf_op jit(solution)/shard_map/reduce_scatter | solution.py:361
  1197.1 17.5 all-reduce
  1215.8 50.6 %reduce-scatter.28.cloned.1.call-done = bf16[256,512]{1,0:T(8,128)(2,1)} async-done(((bf16[2048,512]{1,0:T(8,128)(2,1)}), bf16[256,512]{1,0:T(8,128)(2,1)}) %reduce-scatter.28.cloned.1.call-update) | async-done | bytes 262160 | tf_op jit(solution)/shard_map/reduce_scatter | solution.py:347
  1268.3 68.8 %reduce-scatter.26.cloned.1.call-done = bf16[256,512]{1,0:T(8,128)(2,1)} async-done(((bf16[2048,512]{1,0:T(8,128)(2,1)}), bf16[256,512]{1,0:T(8,128)(2,1)}) %reduce-scatter.26.cloned.1.call-update) | async-done | bytes 262160 | tf_op jit(solution)/shard_map/reduce_scatter | solution.py:344
  1338.8 69.0 %reduce-scatter.30.cloned.1.call-done = bf16[256,512]{1,0:T(8,128)(2,1)} async-done(((bf16[2048,512]{1,0:T(8,128)(2,1)}), bf16[256,512]{1,0:T(8,128)(2,1)}) %reduce-scatter.30.cloned.1.call-update) | async-done | bytes 262160 | tf_op jit(solution)/shard_map/reduce_scatter | solution.py:350
  1409.6 152.0 %reduce-scatter.38.cloned.1.call-done = bf16[2048,256]{1,0:T(8,128)(2,1)} async-done(((bf16[2048,2048]{1,0:T(8,128)(2,1)}), bf16[2048,256]{1,0:T(8,128)(2,1)}) %reduce-scatter.38.cloned.1.call-update) | async-done | bytes 1048592 | tf_op jit(solution)/shard_map/reduce_scatter | solution.py:364
  1561.6 2.7 convert_element_type.245
  1564.3 149.4 %reduce-scatter.34.cloned.1.call-done = bf16[256,2048]{1,0:T(8,128)(2,1)} async-done(((bf16[2048,2048]{1,0:T(8,128)(2,1)}), bf16[256,2048]{1,0:T(8,128)(2,1)}) %reduce-scatter.34.cloned.1.call-update) | async-done | bytes 1048592 | tf_op jit(solution)/shard_map/reduce_scatter | solution.py:353
  1713.7 2.8 convert_element_type.241
  1716.6 148.7 %reduce-scatter.36.cloned.1.call-done = bf16[256,2048]{1,0:T(8,128)(2,1)} async-done(((bf16[2048,2048]{1,0:T(8,128)(2,1)}), bf16[256,2048]{1,0:T(8,128)(2,1)}) %reduce-scatter.36.cloned.1.call-update) | async-done | bytes 1048592 | tf_op jit(solution)/shard_map/reduce_scatter | solution.py:356
  1865.3 2.8 convert_element_type.243
  (332 shorter events, 102.4 us)
Async XLA Ops:
  7.2 17.2 copy-start.32
  7.2 18.0 copy-start.33
  7.2 33.4 %all-gather.14.cloned.1.call-start = ((), (), s32[]{:S(2)}) async-start(), calls=%async_computation.17 | async-start | bytes 1310720 | tf_op jit(solution)/shard_map/all_gather | solution.py:18
  8.1 17.9 copy-start.55
  8.2 17.7 copy-start.59
  8.8 18.2 copy-start.68
  22.5 68.6 %all-gather.20.cloned.1.call-start = ((), (), s32[]{:S(2)}) async-start(), calls=%async_computation.20 | async-start | bytes 2359296 | tf_op jit(solution)/shard_map/all_gather | solution.py:38
  24.4 117.3 %all-gather.24.cloned.1.call-start = ((), (), s32[]{:S(2)}) async-start(), calls=%async_computation.22 | async-start | bytes 2359296 | tf_op jit(solution)/shard_map/all_gather | solution.py:37
  25.2 166.8 %all-gather.16.cloned.1.call-start = ((), (), s32[]{:S(2)}) async-start(), calls=%async_computation.18 | async-start | bytes 2359296 | tf_op jit(solution)/shard_map/all_gather | solution.py:39
  26.0 216.4 %all-gather.22.cloned.1.call-start = ((), (), s32[]{:S(2)}) async-start(), calls=%async_computation.21 | async-start | bytes 2359296 | tf_op jit(solution)/shard_map/all_gather | solution.py:163
  40.6 101.0 %copy-start.6 = (bf16[256,2048]{1,0:T(8,128)(2,1)S(1)}, bf16[256,2048]{1,0:T(8,128)(2,1)}, u32[]{:S(2)}) copy-start(bf16[256,2048]{1,0:T(8,128)(2,1)} %all-gather.14.cloned.1.call-done) | copy-start | bytes 3145732
  93.8 57.4 %copy-start.10 = (f32[256,512]{1,0:T(8,128)}, f32[256,512]{1,0:T(8,128)S(1)}, u32[]{:S(2)}) copy-start(f32[256,512]{1,0:T(8,128)S(1)} %get-tuple-element.544) | copy-start | bytes 1572868
  93.9 57.0 %copy-start.46 = (f32[512]{0:T(512)S(1)}, f32[512]{0:T(512)}, u32[]{:S(2)}) copy-start(f32[512]{0:T(512)} %param.30) | copy-start | bytes 6148
  93.9 57.4 %copy-start.44 = (f32[512]{0:T(512)S(1)}, f32[512]{0:T(512)}, u32[]{:S(2)}) copy-start(f32[512]{0:T(512)} %param.31) | copy-start | bytes 6148
  144.0 7.5 copy-start.12
  153.7 41.4 %copy-start.34 = (f32[512,256]{1,0:T(8,128)S(1)}, f32[512,256]{1,0:T(8,128)}, u32[]{:S(2)}) copy-start(f32[512,256]{1,0:T(8,128)} %param.26) | copy-start | bytes 1572868
  153.7 42.3 %copy-start.43 = (s32[8,8]{1,0:T(8,128)S(1)}, s32[8,8]{1,0:T(8,128)}, u32[]{:S(2)}) copy-start(s32[8,8]{1,0:T(8,128)} %copy-done.42) | copy-start | bytes 772
  153.7 139.1 %all-gather.18.cloned.1.call-start = ((), (), s32[]{:S(2)}) async-start(), calls=%async_computation.19 | async-start | bytes 2359296 | tf_op jit(solution)/shard_map/all_gather | solution.py:164
  195.1 150.4 %all-gather.26.cloned.1.call-start = ((), (), s32[]{:S(2)}) async-start(), calls=%async_computation.23 | async-start | bytes 2359296 | tf_op jit(solution)/shard_map/all_gather | solution.py:44
  195.9 176.8 %reduce-scatter.14.cloned.1.call-start = ((), (), s32[]{:S(2)}) async-start(), calls=%async_computation.24 | async-start | bytes 1310720 | tf_op jit(solution)/shard_map/reduce_scatter | solution.py:22
  300.6 48.3 %copy-start.21 = (f32[256,4,128]{0,2,1:T(8,128)}, f32[256,4,128]{0,2,1:T(8,128)S(1)}, u32[]{:S(2)}) copy-start(f32[256,4,128]{0,2,1:T(8,128)S(1)} %get-tuple-element.189) | copy-start | bytes 1572868
  300.6 48.3 %copy-start.19 = (bf16[256,4,128]{0,2,1:T(8,128)(2,1)}, bf16[256,4,128]{0,2,1:T(8,128)(2,1)S(1)}, u32[]{:S(2)}) copy-start(bf16[256,4,128]{0,2,1:T(8,128)(2,1)S(1)} %convert_element_type.197) | copy-start | bytes 786436
  345.5 34.0 %copy-start.16 = (bf16[8,32,512]{2,1,0:T(8,128)(2,1)S(1)}, bf16[8,32,512]{2,1,0:T(8,128)(2,1)}, u32[]{:S(2)}) copy-start(bf16[8,32,512]{2,1,0:T(8,128)(2,1)} %all_to_all.33) | copy-start | bytes 786436
  348.9 50.9 %all-gather.28.cloned.1.call-start = ((), (), s32[]{:S(2)}) async-start(), calls=%async_computation.25 | async-start | bytes 1310720 | tf_op jit(solution)/shard_map/all_gather | solution.py:18
  379.5 4.6 copy-start.56
  379.5 4.6 copy-start.53
  381.4 145.3 %all-gather.30.cloned.1.call-start = ((), (), s32[]{:S(2)}) async-start(), calls=%async_computation.26 | async-start | bytes 9437184 | tf_op jit(solution)/shard_map/all_gather | solution.py:40
  384.2 268.6 %all-gather.32.cloned.1.call-start = ((), (), s32[]{:S(2)}) async-start(), calls=%async_computation.27 | async-start | bytes 9437184 | tf_op jit(solution)/shard_map/all_gather | solution.py:41
  387.0 392.1 %all-gather.34.cloned.1.call-start = ((), (), s32[]{:S(2)}) async-start(), calls=%async_computation.28 | async-start | bytes 9437184 | tf_op jit(solution)/shard_map/all_gather | solution.py:45
  389.7 420.1 %reduce-scatter.16.cloned.1.call-start = ((), (), s32[]{:S(2)}) async-start(), calls=%async_computation.29 | async-start | bytes 1310720 | tf_op jit(solution)/shard_map/reduce_scatter | solution.py:22
  399.8 253.0 %copy-start.8 = (bf16[256,2048]{1,0:T(8,128)(2,1)S(1)}, bf16[256,2048]{1,0:T(8,128)(2,1)}, u32[]{:S(2)}) copy-start(bf16[256,2048]{1,0:T(8,128)(2,1)} %all-gather.28.cloned.1.call-done) | copy-start | bytes 3145732
  779.1 7.1 copy-start.40
  786.1 30.5 %copy-start.48 = (f32[512]{0:T(512)S(1)}, f32[512]{0:T(512)}, u32[]{:S(2)}) copy-start(f32[512]{0:T(512)} %param.33) | copy-start | bytes 6148
  787.5 29.1 %all-to-all-start.2 = ((bf16[8,32,512]{2,1,0:T(8,128)(2,1)}), bf16[8,32,512]{2,1,0:T(8,128)(2,1)S(1)}, u32[]{:S(2)}, u32[]{:S(2)}) async-start(bf16[8,32,512]{2,1,0:T(8,128)(2,1)} %gather_fusion.2), calls=%async_computation.4 | async-start | bytes 524288 | tf_op jit(solution)/shard_map/all_to_all | solution.py:136
  791.0 53.6 %all-gather.36.cloned.1.call-start = ((), (), s32[]{:S(2)}) async-start(), calls=%async_computation.30 | async-start | bytes 1310720 | tf_op jit(solution)/shard_map/all_gather | solution.py:18
  816.6 35.8 %copy-start.54 = (f32[256]{0:T(256)}, f32[256]{0:T(256)S(1)}, u32[]{:S(2)}) copy-start(f32[256]{0:T(256)S(1)} %add_rsqrt_fusion) | copy-start | bytes 3076
  826.0 64.5 %reduce-scatter.18.cloned.1.call-start = ((), (), s32[]{:S(2)}) async-start(), calls=%async_computation.31 | async-start | bytes 1310720 | tf_op jit(solution)/shard_map/reduce_scatter | solution.py:22
  852.4 6.5 copy-start.28
  852.4 6.5 copy-start.25
  858.9 31.5 %copy-start.14 = (bf16[256,512]{1,0:T(8,128)(2,1)S(1)}, bf16[256,512]{1,0:T(8,128)(2,1)}, u32[]{:S(2)}) copy-start(bf16[256,512]{1,0:T(8,128)(2,1)} %reduce-scatter.14.cloned.1.call-done) | copy-start | bytes 786436
  859.0 40.4 %copy-start.15 = (bf16[256,512]{1,0:T(8,128)(2,1)S(1)}, bf16[256,512]{1,0:T(8,128)(2,1)}, u32[]{:S(2)}) copy-start(bf16[256,512]{1,0:T(8,128)(2,1)} %reduce-scatter.16.cloned.1.call-done) | copy-start | bytes 786436
  859.0 40.4 %copy-start.17 = (bf16[8,32,512]{2,1,0:T(8,128)(2,1)S(1)}, bf16[8,32,512]{2,1,0:T(8,128)(2,1)}, u32[]{:S(2)}) copy-start(bf16[8,32,512]{2,1,0:T(8,128)(2,1)} %all_to_all.33) | copy-start | bytes 786436
  865.8 54.1 %all-gather.38.cloned.1.call-start = ((), (), s32[]{:S(2)}) async-start(), calls=%async_computation.32 | async-start | bytes 1310720 | tf_op jit(solution)/shard_map/all_gather | solution.py:18
  901.5 115.3 %reduce-scatter.20.cloned.1.call-start = ((), (), s32[]{:S(2)}) async-start(), calls=%async_computation.33 | async-start | bytes 2359296 | tf_op jit(solution)/shard_map/reduce_scatter | solution.py:301
  936.2 3.0 copy-start.3
  947.5 3.0 copy-start.3
  950.6 67.3 %copy-start.31 = (f32[256,64]{1,0:T(8,128)S(1)}, f32[256,64]{1,0:T(8,128)}, u32[]{:S(2)}) copy-start(f32[256,64]{1,0:T(8,128)} %get-tuple-element.538) | copy-start | bytes 196612
  950.6 138.0 %reduce-scatter.22.cloned.1.call-start = ((), (), s32[]{:S(2)}) async-start(), calls=%async_computation.34 | async-start | bytes 2359296 | tf_op jit(solution)/shard_map/reduce_scatter | solution.py:304
  951.2 176.9 %reduce-scatter.24.cloned.1.call-start = ((), (), s32[]{:S(2)}) async-start(), calls=%async_computation.35 | async-start | bytes 1310720 | tf_op jit(solution)/shard_map/reduce_scatter | solution.py:22
  1019.6 8.3 copy-start.64
  1019.6 8.3 copy-start.66
  1094.0 101.3 %reduce-scatter.32.cloned.1.call-start = ((), (), s32[]{:S(2)}) async-start(), calls=%async_computation.39 | async-start | bytes 2359296 | tf_op jit(solution)/shard_map/reduce_scatter | solution.py:361
  1096.2 170.3 %reduce-scatter.28.cloned.1.call-start = ((), (), s32[]{:S(2)}) async-start(), calls=%async_computation.37 | async-start | bytes 2359296 | tf_op jit(solution)/shard_map/reduce_scatter | solution.py:347
  1098.3 238.7 %reduce-scatter.26.cloned.1.call-start = ((), (), s32[]{:S(2)}) async-start(), calls=%async_computation.36 | async-start | bytes 2359296 | tf_op jit(solution)/shard_map/reduce_scatter | solution.py:344
  1100.5 307.3 %reduce-scatter.30.cloned.1.call-start = ((), (), s32[]{:S(2)}) async-start(), calls=%async_computation.38 | async-start | bytes 2359296 | tf_op jit(solution)/shard_map/reduce_scatter | solution.py:350
  1102.8 458.8 %reduce-scatter.38.cloned.1.call-start = ((), (), s32[]{:S(2)}) async-start(), calls=%async_computation.42 | async-start | bytes 9437184 | tf_op jit(solution)/shard_map/reduce_scatter | solution.py:364
  1109.8 604.0 %reduce-scatter.34.cloned.1.call-start = ((), (), s32[]{:S(2)}) async-start(), calls=%async_computation.40 | async-start | bytes 9437184 | tf_op jit(solution)/shard_map/reduce_scatter | solution.py:353
  1117.0 748.3 %reduce-scatter.36.cloned.1.call-start = ((), (), s32[]{:S(2)}) async-start(), calls=%async_computation.41 | async-start | bytes 9437184 | tf_op jit(solution)/shard_map/reduce_scatter | solution.py:356
  1123.9 4.2 copy-start.18
  1123.9 73.2 %copy-start.57 = (f32[512]{0:T(512)S(1)}, f32[512]{0:T(512)}, u32[]{:S(2)}) copy-start(f32[512]{0:T(512)} %get-tuple-element.430) | copy-start | bytes 6148
  1123.9 73.2 %copy-start.58 = (f32[512]{0:T(512)S(1)}, f32[512]{0:T(512)}, u32[]{:S(2)}) copy-start(f32[512]{0:T(512)} %get-tuple-element.428) | copy-start | bytes 6148
  1123.9 11.4 all-to-all-start.1
  1135.3 79.3 %all-to-all-start.3 = ((bf16[8,32,512]{2,1,0:T(8,128)(2,1)}), bf16[8,32,512]{2,1,0:T(8,128)(2,1)S(1)}, u32[]{:S(2)}, u32[]{:S(2)}) async-start(bf16[8,32,512]{2,1,0:T(8,128)(2,1)} %bitcast.22), calls=%async_computation.9 | async-start | bytes 524288 | tf_op jit(solution)/shard_map/all_to_all | solution.py:371
  1713.7 154.3 %copy-start.1 = (bf16[256,512]{1,0:T(8,128)(2,1)S(1)}, bf16[256,512]{1,0:T(8,128)(2,1)}, u32[]{:S(2)}) copy-start(bf16[256,512]{1,0:T(8,128)(2,1)} %param.21) | copy-start | bytes 786436
  (42 other events, 61.7 us)
Sparse Core Ops, SparseCore 0:
  22.6 17.9 all-gather.13
  43.3 47.7 all-gather.19
  93.8 47.7 all-gather.23
  144.2 47.7 all-gather.15
  194.6 47.7 all-gather.21
  245.0 47.7 all-gather.17
  295.4 50.0 all-gather.25
  349.0 23.6 reduce-scatter.13
  381.5 18.2 all-gather.27
  402.6 124.1 all-gather.29
  529.7 123.1 all-gather.31
  655.5 123.5 all-gather.33
  786.3 23.4 reduce-scatter.15
  826.1 18.4 all-gather.35
  865.9 24.4 reduce-scatter.17
  901.6 18.2 all-gather.37
  950.7 66.0 reduce-scatter.19
  1021.2 67.3 reduce-scatter.21
  1094.1 25.7 reduce-scatter.23
  1123.3 71.9 reduce-scatter.31
  1199.4 66.9 reduce-scatter.27
  1270.6 66.4 reduce-scatter.25
  1341.1 66.6 reduce-scatter.29
  1411.3 150.3 reduce-scatter.37
  1565.7 148.0 reduce-scatter.33
  1717.2 148.0 reduce-scatter.35
where the time goes:
time: 1890 us; the launch traced here: 1870 us
  waiting for transfers between devices  1570 us (83%)
  matrix products  116 us (6%)
  blocking collectives  69.1 us (4%)
  other arithmetic  63.6 us (3%)
  local copies, waits for them, and re-layouts  24 us (1%)
    reduce_scatter x1, waiting for transfers between devices, on_device(): lax.psum_scatter(down_grad.astype(jnp.bfloat16), 'ctx', scatter_dimension...  152 us
    reduce_scatter x1, waiting for transfers between devices, on_device(): lax.psum_scatter(gate_grad.astype(jnp.bfloat16), 'ctx', scatter_dimension...  149 us
    reduce_scatter x1, waiting for transfers between devices, on_device(): lax.psum_scatter(up_grad.astype(jnp.bfloat16), 'ctx', scatter_dimension=0...  149 us
    all_gather x1, waiting for transfers between devices, gather_weights(): lax.all_gather(w_gate.astype(jnp.bfloat16), 'ctx', axis=0, tiled=True)  127 us
    all_gather x1, waiting for transfers between devices, gather_weights(): lax.all_gather(w_up.astype(jnp.bfloat16), 'ctx', axis=0, tiled=True)  119 us
    all_gather x1, waiting for transfers between devices, gather_weights(): lax.all_gather(w_down.astype(jnp.bfloat16), 'ctx', axis=1, tiled=True)  118 us
    reduce_scatter x1, waiting for transfers between devices, on_device(): lax.psum_scatter(value_grad.astype(jnp.bfloat16), 'ctx', scatter_dimensio...  69 us
    reduce_scatter x1, waiting for transfers between devices, on_device(): lax.psum_scatter(query_grad.astype(jnp.bfloat16), 'ctx', scatter_dimensio...  68.8 us
  transfers between devices with their start and end apart: 29, of which 26 were waited for; matrix products, arithmetic and copies ran while one was open for 6% of the time, Pallas kernels for 0%

commit v1 on v0

--- a/solution.py
+++ b/solution.py
@@ -3,6 +3,9 @@
 import jax
 import jax.numpy as jnp
 from jax import lax
+from jax.experimental import pallas as pl
+from jax.experimental.pallas import tpu as pltpu
+from jax.sharding import Mesh
 from jax.sharding import PartitionSpec as P
 
 D = 2048
@@ -12,6 +15,1254 @@
 EPSILON = 1e-06
 ROPE_THETA = 500000.0
 MASKED = -1e30
+
+
+BF = jnp.bfloat16
+F32 = jnp.float32
+MESH = pl.DeviceIdType.MESH
+AXES = ("z", "y", "x", "core")
+CTX = ("z", "y")
+STRIP = 16
+ANY = pl.BlockSpec(memory_space=pl.ANY)
+VMEM = pl.BlockSpec(memory_space=pltpu.VMEM)
+DMA = pltpu.SemaphoreType.DMA
+BIG_VMEM = 56 * 1024 * 1024
+
+
+def place():
+    return tuple(lax.axis_index(name) for name in AXES)
+
+
+def greet(targets):
+    barrier = pltpu.get_barrier_semaphore()
+    for target in targets:
+        pl.semaphore_signal(barrier, inc=1, device_id=target, device_id_type=MESH)
+    pl.semaphore_wait(barrier, len(targets))
+
+
+def near_first(step, z):
+    high = z // 2
+    low = z + high * (3 - 2 * z)
+    value = (low, 1 - low, 2, 3)[step]
+    return value + high * (3 - 2 * value)
+
+
+def plane_axes(me):
+    z, y, x, k = me
+    a = x * (1 - k) + y * k
+    b = y * (1 - k) + x * k
+
+    def slot(zp, ap, bp):
+        yp = bp * (1 - k) + ap * k
+        xp = ap * (1 - k) + bp * k
+        return zp * 4 + yp * 2 + xp
+
+    dev_a = (z, y * (1 - k) + (1 - y) * k, (1 - x) * (1 - k) + x * k, k)
+    dev_b = (z, (1 - y) * (1 - k) + y * k, x * (1 - k) + (1 - x) * k, k)
+    return a, b, slot, dev_a, dev_b
+
+
+def plane_neighbours(me):
+    z, y, x, k = me
+    up = z + 1 - 2 * (z // 3)
+    down = z - 1 + 2 * ((3 - z) // 3)
+    return [(z, 1 - y, x, k), (z, y, 1 - x, k)], up, down
+
+
+def greet_plane(me, others=()):
+    z, y, x, k = me
+    barrier = pltpu.get_barrier_semaphore()
+    targets = [(z, 1 - y, x, k), (z, y, 1 - x, k), *others]
+    for target in targets:
+        pl.semaphore_signal(barrier, inc=1, device_id=target, device_id_type=MESH)
+
+    @pl.when(z < 3)
+    def _():
+        pl.semaphore_signal(barrier, inc=1, device_id=(z + 1, y, x, k), device_id_type=MESH)
+
+    @pl.when(z > 0)
+    def _():
+        pl.semaphore_signal(barrier, inc=1, device_id=(z - 1, y, x, k), device_id_type=MESH)
+
+    inner = (z + 2) // 3 - z // 3
+    pl.semaphore_wait(barrier, len(targets) + 1 + inner)
+
+
+GATHER_SEMS = [DMA((16,)), DMA((4,)), DMA((4,)), DMA((4,)), DMA((8,))]
+
+
+def gather_plane(me, own_ref, view, sems):
+    z, y, x, k = me
+    recv, up_send, down_send, a_send, b_send = sems
+    a, b, slot, dev_a, dev_b = plane_axes(me)
+    own = slot(z, a, b)
+
+    def copy(src, index, send_sem, device):
+        return pltpu.make_async_remote_copy(
+            src_ref=src,
+            dst_ref=view(index),
+            send_sem=send_sem,
+            recv_sem=recv.at[index],
+            device_id=device,
+            device_id_type=MESH,
+        )
+
+    def landed(index):
+        copy(view(index), index, a_send.at[0], dev_a).wait_recv()
+
+    for step in range(5):
+        if step < 4:
+            zp = near_first(step, z)
+            index = slot(zp, a, b)
+            if step == 0:
+                src = own_ref
+            else:
+                landed(index)
+                src = view(index)
+
+            @pl.when((zp <= z) & (z < 3))
+            def _():
+                copy(src, index, up_send.at[zp], (z + 1, y, x, k)).start()
+
+            @pl.when((zp >= z) & (z > 0))
+            def _():
+                copy(src, index, down_send.at[zp], (z - 1, y, x, k)).start()
+
+            copy(src, index, a_send.at[step], dev_a).start()
+            copy(src, index, b_send.at[step], dev_b).start()
+        if step > 0:
+            index = slot(near_first(step - 1, z), 1 - a, b)
+            landed(index)
+            copy(view(index), index, b_send.at[3 + step], dev_b).start()
+    for step in range(4):
+        zp = near_first(step, z)
+        landed(slot(zp, a, 1 - b))
+        landed(slot(zp, 1 - a, 1 - b))
+    for step in range(4):
+        zp = near_first(step, z)
+        for ap, number in ((a, step), (1 - a, 4 + step)):
+            index = slot(zp, ap, b)
+            copy(view(index), index, b_send.at[number], dev_b).wait_send()
+        index = slot(zp, a, b)
+        copy(view(index), index, a_send.at[step], dev_a).wait_send()
+
+        @pl.when((zp <= z) & (z < 3))
+        def _():
+            copy(view(index), index, up_send.at[zp], (z + 1, y, x, k)).wait_send()
+
+        @pl.when((zp >= z) & (z > 0))
+        def _():
+            copy(view(index), index, down_send.at[zp], (z - 1, y, x, k)).wait_send()
+
+
+def reduce_scratch(rows, width):
+    return [
+        pltpu.VMEM((4, 2, rows, width), BF),
+        pltpu.VMEM((4, 2, rows, width), BF),
+        pltpu.VMEM((4, rows, width), BF),
+        pltpu.VMEM((4, rows, width), BF),
+        pltpu.VMEM((4, rows, width), BF),
+        pltpu.VMEM((4, rows, width), BF),
+        pltpu.VMEM((4, rows, width), BF),
+        DMA((8,)),
+        DMA((8,)),
+        DMA((8,)),
+        DMA((4,)),
+        DMA((4,)),
+        DMA((4,)),
+        DMA((4,)),
+        DMA((4,)),
+    ]
+
+
+def reduce_plane(me, view, rows, scratch, finish):
+    z, y, x, k = me
+    (mine, from_b, to_a, from_a, to_z, from_low, from_high) = scratch[:7]
+    (load_sem, b_send, b_recv, a_send, a_recv, z_send, low_recv, high_recv) = scratch[7:]
+    a, b, slot, dev_a, dev_b = plane_axes(me)
+    order = [near_first(step, z) for step in (3, 2, 1, 0)]
+
+    def copy_b(zp, ap):
+        return pltpu.make_async_remote_copy(
+            src_ref=view(slot(zp, ap, 1 - b)),
+            dst_ref=from_b.at[zp, ap],
+            send_sem=b_send.at[zp * 2 + ap],
+            recv_sem=b_recv.at[zp * 2 + ap],
+            device_id=dev_b,
+            device_id_type=MESH,
+        )
+
+    def copy_a(zp):
+        return pltpu.make_async_remote_copy(
+            src_ref=to_a.at[zp],
+            dst_ref=from_a.at[zp],
+            send_sem=a_send.at[zp],
+            recv_sem=a_recv.at[zp],
+            device_id=dev_a,
+            device_id_type=MESH,
+        )
+
+    def copy_up(zp):
+        return pltpu.make_async_remote_copy(
+            src_ref=to_z.at[zp],
+            dst_ref=from_low.at[zp],
+            send_sem=z_send.at[zp],
+            recv_sem=low_recv.at[zp],
+            device_id=(z + 1, y, x, k),
+            device_id_type=MESH,
+        )
+
+    def copy_down(zp):
+        return pltpu.make_async_remote_copy(
+            src_ref=to_z.at[zp],
+            dst_ref=from_high.at[zp],
+            send_sem=z_send.at[zp],
+            recv_sem=high_recv.at[zp],
+            device_id=(z - 1, y, x, k),
+            device_id_type=MESH,
+        )
+
+    def load(zp, ap):
+        return pltpu.make_async_copy(
+            view(slot(zp, ap, b)), mine.at[zp, ap], load_sem.at[zp * 2 + ap]
+        )
+
+    for zp in order:
+        for ap in (1 - a, a):
+            copy_b(zp, ap).start()
+    for zp in order:
+        for ap in (1 - a, a):
+            load(zp, ap).start()
+
+    def strips(work):
+        def body(i, carry):
+            work(pl.ds(pl.multiple_of(i * STRIP, STRIP), STRIP))
+            return carry
+
+        lax.fori_loop(0, rows // STRIP, body, 0)
+
+    for step in range(5):
+        if step < 4:
+            zp = order[step]
+            load(zp, 1 - a).wait()
+            copy_b(zp, 1 - a).wait_recv()
+
+            def first(strip, zp=zp):
+                to_a[zp, strip] = (
+                    mine[zp, 1 - a, strip].astype(F32) + from_b[zp, 1 - a, strip].astype(F32)
+                ).astype(BF)
+
+            strips(first)
+            copy_a(zp).start()
+        if step > 0:
+            zp = order[step - 1]
+            load(zp, a).wait()
+            copy_b(zp, a).wait_recv()
+            copy_a(zp).wait_recv()
+
+            def own_sum(strip, zp=zp):
+                return (
+                    mine[zp, a, strip].astype(F32)
+                    + from_b[zp, a, strip].astype(F32)
+                    + from_a[zp, strip].astype(F32)
+                )
+
+            if step < 4:
+                upward = zp > z
+
+                @pl.when(upward & (z > 0))
+                def _(zp=zp, own_sum=own_sum):
+                    pltpu.make_async_remote_copy(
+                        src_ref=to_z.at[zp],
+                        dst_ref=from_low.at[zp],
+                        send_sem=z_send.at[zp],
+                        recv_sem=low_recv.at[zp],
+                        device_id=(z, y, x, k),
+                        device_id_type=MESH,
+                    ).wait_recv()
+
+                    def work(strip):
+                        to_z[zp, strip] = (own_sum(strip) + from_low[zp, strip].astype(F32)).astype(BF)
+
+                    strips(work)
+
+                @pl.when(jnp.logical_not(upward) & (z < 3))
+                def _(zp=zp, own_sum=own_sum):
+                    pltpu.make_async_remote_copy(
+                        src_ref=to_z.at[zp],
+                        dst_ref=from_high.at[zp],
+                        send_sem=z_send.at[zp],
+                        recv_sem=high_recv.at[zp],
+                        device_id=(z, y, x, k),
+                        device_id_type=MESH,
+                    ).wait_recv()
+
+                    def work(strip):
+                        to_z[zp, strip] = (own_sum(strip) + from_high[zp, strip].astype(F32)).astype(BF)
+
+                    strips(work)
+
+                @pl.when((z == 0) | (z == 3))
+                def _(zp=zp, own_sum=own_sum):
+                    def work(strip):
+                        to_z[zp, strip] = own_sum(strip).astype(BF)
+
+                    strips(work)
+
+                @pl.when(upward)
+                def _(zp=zp):
+                    copy_up(zp).start()
+
+                @pl.when(jnp.logical_not(upward))
+                def _(zp=zp):
+                    copy_down(zp).start()
+
+            else:
+
+                @pl.when(z == 0)
+                def _():
+                    copy_down(z).wait_recv()
+                    strips(lambda s: finish(s, own_sum(s) + from_high[z, s].astype(F32)))
+
+                @pl.when(z == 3)
+                def _():
+                    copy_up(z).wait_recv()
+                    strips(lambda s: finish(s, own_sum(s) + from_low[z, s].astype(F32)))
+
+                @pl.when((z > 0) & (z < 3))
+                def _():
+                    copy_up(z).wait_recv()
+                    copy_down(z).wait_recv()
+                    strips(
+                        lambda s: finish(
+                            s,
+                            own_sum(s) + from_low[z, s].astype(F32) + from_high[z, s].astype(F32),
+                        )
+                    )
+
+    def settle():
+        for zp in order:
+            copy_b(zp, 0).wait_send()
+            copy_b(zp, 1).wait_send()
+            copy_a(zp).wait_send()
+        for zp in order[:3]:
+            copy_up(zp).wait_send()
+
+    return settle
+
+
+def own_tile(me):
+    z, y, x, k = me
+    return z * 2 + y
+
+
+def gather_view(out_ref, rows):
+    def view(slot):
+        return out_ref.at[pl.ds(pl.multiple_of(slot * rows, rows), rows), :]
+
+    return view
+
+
+def hand_out_copies(me, own_ref, out_ref, send, recv):
+    z, y, x, k = me
+    rows, width = own_ref.shape
+    part = width // 4
+    target_rows = pl.ds(pl.multiple_of(k * 2 * rows + x * rows, rows), rows)
+
+    def copy(xt, kt, number):
+        return pltpu.make_async_remote_copy(
+            src_ref=own_ref.at[:, pl.ds(pl.multiple_of((2 * xt + kt) * part, part), part)],
+            dst_ref=out_ref.at[target_rows, :],
+            send_sem=send.at[number],
+            recv_sem=recv.at[number],
+            device_id=(z, y, xt, kt),
+            device_id_type=MESH,
+        )
+
+    local = pltpu.make_async_copy(
+        own_ref.at[:, pl.ds(pl.multiple_of((2 * x + k) * part, part), part)],
+        out_ref.at[target_rows, :],
+        recv.at[3],
+    )
+    return [copy(x, 1 - k, 0), copy(1 - x, k, 1), copy(1 - x, 1 - k, 2)], local
+
+
+def pair_devices(me):
+    z, y, x, k = me
+    return [(z, y, x, 1 - k), (z, y, 1 - x, 1 - k)]
+
+
+def row_scale(values):
+    return lax.rsqrt(jnp.sum(values * values, axis=1, keepdims=True) / values.shape[1] + EPSILON)
+
+
+def norm_back_strip(grad, values, gain):
+    scale = row_scale(values)
+    term = grad * values * scale
+    weighted = grad * gain
+    dot = jnp.sum(weighted * values, axis=1, keepdims=True)
+    back = scale * weighted - values * (scale * scale * scale * dot / values.shape[1])
+    return back, term[:8] + term[8:]
+
+
+def comm_call(body, name, number, out_shape, in_specs, out_specs, scratch, cost=None):
+    return pl.pallas_call(
+        body,
+        name=name,
+        out_shape=out_shape,
+        in_specs=in_specs,
+        out_specs=out_specs,
+        scratch_shapes=scratch,
+        cost_estimate=cost,
+        compiler_params=pltpu.CompilerParams(
+            collective_id=number, has_side_effects=True, vmem_limit_bytes=BIG_VMEM
+        ),
+    )
+
+
+def same_x_greet(me):
+    z, y, x, k = me
+    barrier = pltpu.get_barrier_semaphore()
+    number = z * 4 + y * 2 + k
+
+    def body(i, carry):
+        other = lax.rem(number + i, 16)
+        pl.semaphore_signal(
+            barrier,
+            inc=1,
+            device_id=(other // 4, (other // 2) % 2, x, other % 2),
+            device_id_type=MESH,
+        )
+        return carry
+
+    lax.fori_loop(1, 16, body, 0)
+    for kt in (k, 1 - k):
+        pl.semaphore_signal(barrier, inc=1, device_id=(z, y, 1 - x, kt), device_id_type=MESH)
+    pl.semaphore_wait(barrier, 17)
+
+
+def open_layer(inputs, cotangent, blob, gains):
+    rows, part = inputs.shape
+    half = rows // 2
+    quarter = half // 2
+
+    def body(in_ref, cot_ref, blob_ref, gain_ref, full_ref, own_cot_ref, wall_ref, gains_ref, *scratch):
+        shard, cot_half, pair_send, pair_recv, local_sem = scratch[:5]
+        deal_send, deal_recv, share_send, share_recv, gain_send, gain_recv, cot_sems = scratch[5:12]
+        gather_sems = scratch[12:]
+        me = z, y, x, k = place()
+        ctx = own_tile(me)
+        sibling = (z, y, x, 1 - k)
+        same_x_greet(me)
+
+        def pair_copy(src, dst, number):
+            columns = pl.ds(pl.multiple_of(k * part, part), part)
+            remote = pltpu.make_async_remote_copy(
+                src_ref=src.at[pl.ds(pl.multiple_of((1 - k) * half, half), half), :],
+                dst_ref=dst.at[:, columns],
+                send_sem=pair_send.at[number],
+                recv_sem=pair_recv.at[number],
+                device_id=sibling,
+                device_id_type=MESH,
+            )
+            local = pltpu.make_async_copy(
+                src.at[pl.ds(pl.multiple_of(k * half, half), half), :],
+                dst.at[:, columns],
+                local_sem.at[number],
+            )
+            remote.start()
+            local.start()
+            return remote, local
+
+        first = pair_copy(in_ref, shard, 0)
+        second = pair_copy(cot_ref, cot_half, 1)
+
+        def deal(e):
+            return pltpu.make_async_remote_copy(
+                src_ref=blob_ref.at[e],
+                dst_ref=wall_ref.at[:, ctx, e % 2],
+                send_sem=deal_send.at[e],
+                recv_sem=deal_recv.at[ctx],
+                device_id=(2 * k + e // 4, (e // 2) % 2, x, e % 2),
+                device_id_type=MESH,
+            )
+
+        def deal_own(e):
+            return pltpu.make_async_copy(
+                blob_ref.at[e], wall_ref.at[:, ctx, k], deal_recv.at[ctx]
+            )
+
+        stays = k == z // 2
+        own_e = (z % 2) * 4 + y * 2 + k
+        for e in range(8):
+
+            @pl.when(jnp.logical_not(stays & (own_e == e)))
+            def _(e=e):
+                deal(e).start()
+
+            @pl.when(stays & (own_e == e))
+            def _(e=e):
+                deal_own(e).start()
+
+        def gain_copy(xt, kt, number):
+            return pltpu.make_async_remote_copy(
+                src_ref=gain_ref,
+                dst_ref=gains_ref.at[:, pl.ds(pl.multiple_of((2 * x + k) * part, part), part)],
+                send_sem=gain_send.at[number],
+                recv_sem=gain_recv.at[number],
+                device_id=(z, y, xt, kt),
+                device_id_type=MESH,
+            )
+
+        gain_copies = [gain_copy(x, 1 - k, 0), gain_copy(1 - x, k, 1), gain_copy(1 - x, 1 - k, 2)]
+        for copy in gain_copies:
+            copy.start()
+        gain_local = pltpu.make_async_copy(
+            gain_ref,
+            gains_ref.at[:, pl.ds(pl.multiple_of((2 * x + k) * part, part), part)],
+            local_sem.at[2],
+        )
+        gain_local.start()
+
+        first[0].wait_recv()
+        first[1].wait()
+
+        def view(slot):
+            return full_ref.at[
+                pl.ds(pl.multiple_of((slot // 2) * half, half), half),
+                pl.ds(pl.multiple_of((slot % 2) * 2 * part, 2 * part), 2 * part),
+            ]
+
+        own_slot = ctx * 2 + x
+        own_local = pltpu.make_async_copy(shard, view(own_slot), local_sem.at[3])
+        own_local.start()
+        second[0].wait_recv()
+        second[1].wait()
+        wide = pl.ds(pl.multiple_of(x * 2 * part, 2 * part), 2 * part)
+        cot_remote = pltpu.make_async_remote_copy(
+            src_ref=cot_half.at[pl.ds(pl.multiple_of((1 - x) * quarter, quarter), quarter), :],
+            dst_ref=own_cot_ref.at[:, wide],
+            send_sem=cot_sems.at[0],
+            recv_sem=cot_sems.at[1],
+            device_id=(z, y, 1 - x, k),
+            device_id_type=MESH,
+        )
+        cot_remote.start()
+        cot_local = pltpu.make_async_copy(
+            cot_half.at[pl.ds(pl.multiple_of(x * quarter, quarter), quarter), :],
+            own_cot_ref.at[:, wide],
+            cot_sems.at[2],
+        )
+        cot_local.start()
+        gather_plane(me, shard, view, gather_sems)
+        for c in range(8):
+
+            def wait_deal(c=c):
+                pltpu.make_async_copy(
+                    blob_ref.at[0], wall_ref.at[:, c, k], deal_recv.at[c]
+                ).wait()
+
+            wait_deal()
+        share = pltpu.make_async_remote_copy(
+            src_ref=wall_ref.at[:, :, k],
+            dst_ref=wall_ref.at[:, :, k],
+            send_sem=share_send,
+            recv_sem=share_recv,
+            device_id=sibling,
+            device_id_type=MESH,
+        )
+        share.start()
+        for e in range(8):
+
+            @pl.when(jnp.logical_not(stays & (own_e == e)))
+            def _(e=e):
+                deal(e).wait_send()
+
+        own_local.wait()
+        first[0].wait_send()
+        second[0].wait_send()
+        for copy in gain_copies:
+            copy.wait()
+        gain_local.wait()
+        cot_remote.wait()
+        cot_local.wait()
+        share.wait_send()
+        pltpu.make_async_remote_copy(
+            src_ref=wall_ref.at[:, :, 1 - k],
+            dst_ref=wall_ref.at[:, :, 1 - k],
+            send_sem=share_send,
+            recv_sem=share_recv,
+            device_id=sibling,
+            device_id_type=MESH,
+        ).wait_recv()
+
+    shape = jax.ShapeDtypeStruct
+    return comm_call(
+        body,
+        "open_layer",
+        0,
+        (
+            shape((8 * half, 4 * part), BF),
+            shape((quarter, 4 * part), BF),
+            shape((4, 8, 2, HD, HD), BF),
+            shape((4, 4 * part), F32),
+        ),
+        [ANY, ANY, ANY, ANY],
+        (ANY, ANY, ANY, ANY),
+        [
+            pltpu.VMEM((half, 2 * part), BF),
+            pltpu.VMEM((half, 2 * part), BF),
+            DMA((2,)),
+            DMA((2,)),
+            DMA((4,)),
+            DMA((8,)),
+            DMA((8,)),
+            DMA,
+            DMA,
+            DMA((3,)),
+            DMA((3,)),
+            DMA((3,)),
+            *GATHER_SEMS,
+        ],
+    )(inputs, cotangent, blob, gains)
+
+
+def plane_totals(terms, number, share=None):
+    count = terms.shape[0]
+
+    def body(*refs):
+        if share is None:
+            term_ref, total_ref, buffer, send, recv, local = refs
+        else:
+            term_ref, a_ref, b_ref, total_ref, other_ref, a_out, b_out, buffer, send, recv, local, pair_send, pair_recv = refs
+        me = z, y, x, k = place()
+        own = z * 4 + y * 2 + x
+        barrier = pltpu.get_barrier_semaphore()
+
+        def device(i):
+            other = lax.rem(own + i, 16)
+            return (other // 4, (other // 2) % 2, other % 2, k)
+
+        def call(i, carry):
+            pl.semaphore_signal(barrier, inc=1, device_id=device(i), device_id_type=MESH)
+            return carry
+
+        lax.fori_loop(1, 16, call, 0)
+        sibling = (z, y, x, 1 - k)
+        if share is not None:
+            pl.semaphore_signal(barrier, inc=1, device_id=sibling, device_id_type=MESH)
+        pl.semaphore_wait(barrier, 15 if share is None else 16)
+
+        def copy(i):
+            return pltpu.make_async_remote_copy(
+                src_ref=term_ref,
+                dst_ref=buffer.at[own],
+                send_sem=send.at[i],
+                recv_sem=recv.at[own],
+                device_id=device(i),
+                device_id_type=MESH,
+            )
+
+        def begin(i, carry):
+            copy(i).start()
+            return carry
+
+        lax.fori_loop(1, 16, begin, 0)
+
+        def pair(src, dst, n):
+            return pltpu.make_async_remote_copy(
+                src_ref=src,
+                dst_ref=dst,
+                send_sem=pair_send.at[n],
+                recv_sem=pair_recv.at[n],
+                device_id=sibling,
+                device_id_type=MESH,
+            )
+
+        if share is not None:
+            pairs = [pair(a_ref, a_out, 0), pair(b_ref, b_out, 1)]
+            for c in pairs:
+                c.start()
+
+        total_ref[...] = term_ref[...]
+
+        def add(i, carry):
+            other = lax.rem(own + i, 16)
+            pltpu.make_async_remote_copy(
+                src_ref=term_ref,
+                dst_ref=buffer.at[other],
+                send_sem=send.at[0],
+                recv_sem=recv.at[other],
+                device_id=device(i),
+                device_id_type=MESH,
+            ).wait_recv()
+            total_ref[...] += buffer[other]
+            return carry
+
+        lax.fori_loop(1, 16, add, 0)
+        if share is not None:
+            last = pair(total_ref.at[pl.ds(count // 2, count // 2), :], other_ref, 2)
+            last.start()
+            for c in (*pairs, last):
+                c.wait()
+
+        def finish(i, carry):
+            copy(i).wait_send()
+            return carry
+
+        lax.fori_loop(1, 16, finish, 0)
+
+    shape = jax.ShapeDtypeStruct
+    scratch = [pltpu.VMEM((16, count, 128), F32), DMA((16,)), DMA((16,)), DMA]
+    if share is None:
+        return comm_call(
+            body, "plane_totals", number, shape(terms.shape, F32), [VMEM], VMEM, scratch
+        )(terms)
+    return comm_call(
+        body,
+        "plane_totals_keys",
+        number,
+        (
+            shape(terms.shape, F32),
+            shape((count // 2, 128), F32),
+            shape(share[0].shape, share[0].dtype),
+            shape(share[1].shape, share[1].dtype),
+        ),
+        [VMEM, ANY, ANY],
+        (VMEM, VMEM, ANY, ANY),
+        [*scratch, DMA((3,)), DMA((3,))],
+    )(terms, *share)
+
+
+def after_attention(terms, source, gain):
+    tokens, width = terms.shape
+    rows = tokens // 16
+
+    def body(term_ref, source_ref, gain_ref, full_ref, own_ref, branch_ref, shard, local, *scratch):
+        me = place()
+        greet_plane(me)
+
+        def finish(strip, total):
+            branch_ref[strip] = total
+            h = source_ref[strip].astype(F32) + total * row_scale(total) * gain_ref[...]
+            own_ref[strip] = h
+            shard[strip] = h.astype(BF)
+
+        settle = reduce_plane(me, gather_view(term_ref, rows), rows, scratch[:15], finish)
+        view = gather_view(full_ref, rows)
+        keep = pltpu.make_async_copy(shard, view(me[0] * 4 + me[1] * 2 + me[2]), local)
+        keep.start()
+        gather_plane(me, shard, view, scratch[15:])
+        keep.wait()
+        settle()
+
+    shape = jax.ShapeDtypeStruct
+    return comm_call(
+        body,
+        "after_attention",
+        2,
+        (shape((tokens, width), BF), shape((rows, width), F32), shape((rows, width), F32)),
+        [ANY, VMEM, VMEM],
+        (ANY, VMEM, VMEM),
+        [pltpu.VMEM((rows, width), BF), DMA, *reduce_scratch(rows, width), *GATHER_SEMS],
+    )(terms, source, gain)
+
+
+def after_ffn(terms, residual, cotangent, gain):
+    tokens, width = terms.shape
+    rows = tokens // 16
+
+    def body(term_ref, res_ref, cot_ref, gain_ref, full_ref, out_ref, gg_ref, shard, result, local, out_send, out_recv, *scratch):
+        me = place()
+        greet_plane(me, pair_devices(me))
+        gg_ref[...] = jnp.zeros_like(gg_ref)
+
+        def finish(strip, total):
+            gain_row = gain_ref[...]
+            out = res_ref[strip] + total * row_scale(total) * gain_row
+            result[strip] = out.astype(BF)
+            back, term = norm_back_strip(cot_ref[strip].astype(F32), total, gain_row)
+            gg_ref[...] += term
+            shard[strip] = back.astype(BF)
+
+        settle = reduce_plane(me, gather_view(term_ref, rows), rows, scratch[:15], finish)
+        view = gather_view(full_ref, rows)
+        keep = pltpu.make_async_copy(shard, view(me[0] * 4 + me[1] * 2 + me[2]), local)
+        keep.start()
+        copies, own = hand_out_copies(me, result, out_ref, out_send, out_recv)
+        for copy in copies:
+            copy.start()
+        own.start()
+        gather_plane(me, shard, view, scratch[15:])
+        keep.wait()
+        settle()
+        own.wait()
+        for copy in copies:
+            copy.wait()
+
+    shape = jax.ShapeDtypeStruct
+    return comm_call(
+        body,
+        "after_ffn",
+        3,
+        (shape((tokens, width), BF), shape((rows * 4, width // 4), BF), shape((8, width), F32)),
+        [ANY, VMEM, VMEM, VMEM],
+        (ANY, ANY, VMEM),
+        [
+            pltpu.VMEM((rows, width), BF),
+            pltpu.VMEM((rows, width), BF),
+            DMA,
+            DMA((3,)),
+            DMA((4,)),
+            *reduce_scratch(rows, width),
+            *GATHER_SEMS,
+        ],
+    )(terms, residual, cotangent, gain)
+
+
+def after_ffn_back(terms, cotangent, branch, gain):
+    tokens, width = terms.shape
+    rows = tokens // 16
+
+    def body(term_ref, cot_ref, branch_ref, gain_ref, full_ref, own_ref, gg_ref, shard, local, *scratch):
+        me = place()
+        greet_plane(me)
+        gg_ref[...] = jnp.zeros_like(gg_ref)
+
+        def finish(strip, total):
+            grad = cot_ref[strip].astype(F32) + total
+            own_ref[strip] = grad
+            back, term = norm_back_strip(grad, branch_ref[strip], gain_ref[...])
+            gg_ref[...] += term
+            shard[strip] = back.astype(BF)
+
+        settle = reduce_plane(me, gather_view(term_ref, rows), rows, scratch[:15], finish)
+        view = gather_view(full_ref, rows)
+        keep = pltpu.make_async_copy(shard, view(me[0] * 4 + me[1] * 2 + me[2]), local)
+        keep.start()
+        gather_plane(me, shard, view, scratch[15:])
+        keep.wait()
+        settle()
+
+    shape = jax.ShapeDtypeStruct
+    return comm_call(
+        body,
+        "after_ffn_back",
+        4,
+        (shape((tokens, width), BF), shape((rows, width), F32), shape((8, width), F32)),
+        [ANY, VMEM, VMEM, VMEM],
+        (ANY, VMEM, VMEM),
+        [pltpu.VMEM((rows, width), BF), DMA, *reduce_scratch(rows, width), *GATHER_SEMS],
+    )(terms, cotangent, branch, gain)
+
+
+def close_layer(terms, grad, blob):
+    tokens, width = terms.shape
+    rows = tokens // 16
+
+    def body(term_ref, grad_ref, blob_ref, out_ref, back_ref, result, out_send, out_recv, deal_send, deal_recv, *scratch):
+        me = z, y, x, k = place()
+        same_x_greet(me)
+        head = z // 2
+        number = ((z % 2) * 2 + y) * 2 + k
+
+        def deal(c):
+            return pltpu.make_async_remote_copy(
+                src_ref=blob_ref.at[c],
+                dst_ref=back_ref.at[number],
+                send_sem=deal_send.at[c],
+                recv_sem=deal_recv.at[number],
+                device_id=(c // 2, c % 2, x, head),
+                device_id_type=MESH,
+            )
+
+        stays = k == z // 2
+        ctx = own_tile(me)
+        for c in range(8):
+
+            @pl.when(jnp.logical_not(stays & (ctx == c)))
+            def _(c=c):
+                deal(c).start()
+
+            @pl.when(stays & (ctx == c))
+            def _(c=c):
+                pltpu.make_async_copy(
+                    blob_ref.at[c], back_ref.at[number], deal_recv.at[number]
+                ).start()
+
+        def finish(strip, total):
+            result[strip] = (grad_ref[strip] + total).astype(BF)
+
+        settle = reduce_plane(me, gather_view(term_ref, rows), rows, scratch, finish)
+        copies, own = hand_out_copies(me, result, out_ref, out_send, out_recv)
+        for copy in copies:
+            copy.start()
+        own.start()
+        settle()
+        own.wait()
+        for copy in copies:
+            copy.wait()
+        for c in range(8):
+
+            @pl.when(jnp.logical_not(stays & (ctx == c)))
+            def _(c=c):
+                deal(c).wait_send()
+
+            pltpu.make_async_copy(blob_ref.at[c], back_ref.at[c], deal_recv.at[c]).wait()
+
+    shape = jax.ShapeDtypeStruct
+    return comm_call(
+        body,
+        "close_layer",
+        5,
+        (shape((rows * 4, width // 4), BF), shape(blob.shape, BF)),
+        [ANY, VMEM, ANY],
+        (ANY, ANY),
+        [
+            pltpu.VMEM((rows, width), BF),
+            DMA((3,)),
+            DMA((4,)),
+            DMA((8,)),
+            DMA((8,)),
+            *reduce_scratch(rows, width),
+        ],
+    )(terms, grad, blob)
+
+
+QUERY_ROWS = 256
+
+
+def masked_scores(q, keys, low, high, logical):
+    raw = lax.dot_general(q, keys, (((1,), (1,)), ((), ())), preferred_element_type=F32)
+    allowed = (logical >= low) & (logical <= high)
+    return raw * (1.0 / math.sqrt(HD)), allowed
+
+
+def attend(query, keys, values, low, high, logical):
+    tokens, total = query.shape[0], keys.shape[0]
+
+    def body(q_ref, k_ref, v_ref, low_ref, high_ref, log_ref, out_ref, lse_ref):
+        raw, allowed = masked_scores(q_ref[...], k_ref[...], low_ref[...], high_ref[...], log_ref[...])
+        raw = jnp.where(allowed, raw, MASKED)
+        top = jnp.max(raw, axis=1, keepdims=True)
+        weights = jnp.where(allowed, jnp.exp(raw - top), 0.0)
+        total_weight = jnp.sum(weights, axis=1, keepdims=True)
+        weights = (weights / total_weight).astype(BF)
+        out_ref[...] = jnp.dot(weights, v_ref[...], preferred_element_type=F32)
+        lse_ref[...] = top + jnp.log(total_weight)
+
+    row = pl.BlockSpec((QUERY_ROWS, HD), lambda i: (i, 0))
+    single = pl.BlockSpec((QUERY_ROWS, 1), lambda i: (i, 0))
+    whole = pl.BlockSpec((total, HD), lambda i: (0, 0))
+    line = pl.BlockSpec((1, total), lambda i: (0, 0))
+    return pl.pallas_call(
+        body,
+        name="attend",
+        grid=(tokens // QUERY_ROWS,),
+        out_shape=(
+            jax.ShapeDtypeStruct((tokens, HD), F32),
+            jax.ShapeDtypeStruct((tokens, 1), F32),
+        ),
+        in_specs=[row, whole, whole, single, single, line],
+        out_specs=(row, single),
+        compiler_params=pltpu.CompilerParams(vmem_limit_bytes=BIG_VMEM),
+    )(query, keys, values, low, high, logical)
+
+
+def attend_back(query, keys, values, low, high, logical, lse, grad, delta):
+    tokens, total = query.shape[0], keys.shape[0]
+
+    def body(q_ref, k_ref, v_ref, low_ref, high_ref, log_ref, lse_ref, g_ref, d_ref, dq_ref, dk_ref, dv_ref):
+        @pl.when(pl.program_id(0) == 0)
+        def _():
+            dk_ref[...] = jnp.zeros_like(dk_ref)
+            dv_ref[...] = jnp.zeros_like(dv_ref)
+
+        q, keys_all, g = q_ref[...], k_ref[...], g_ref[...]
+        raw, allowed = masked_scores(q, keys_all, low_ref[...], high_ref[...], log_ref[...])
+        weights = jnp.where(allowed, jnp.exp(raw - lse_ref[...]), 0.0)
+        dp = lax.dot_general(g, v_ref[...], (((1,), (1,)), ((), ())), preferred_element_type=F32)
+        ds = (weights * (dp - d_ref[...])).astype(BF)
+        scaling = 1.0 / math.sqrt(HD)
+        dq_ref[...] = jnp.dot(ds, keys_all, preferred_element_type=F32) * scaling
+        across = (((0,), (0,)), ((), ()))
+        dk_ref[...] += lax.dot_general(ds, q, across, preferred_element_type=F32) * scaling
+        dv_ref[...] += lax.dot_general(weights.astype(BF), g, across, preferred_element_type=F32)
+
+    row = pl.BlockSpec((QUERY_ROWS, HD), lambda i: (i, 0))
+    single = pl.BlockSpec((QUERY_ROWS, 1), lambda i: (i, 0))
+    whole = pl.BlockSpec((total, HD), lambda i: (0, 0))
+    line = pl.BlockSpec((1, total), lambda i: (0, 0))
+    return pl.pallas_call(
+        body,
+        name="attend_back",
+        grid=(tokens // QUERY_ROWS,),
+        out_shape=(
+            jax.ShapeDtypeStruct((tokens, HD), F32),
+            jax.ShapeDtypeStruct((total, HD), F32),
+            jax.ShapeDtypeStruct((total, HD), F32),
+        ),
+        in_specs=[row, whole, whole, single, single, line, single, row, single],
+        out_specs=(row, whole, whole),
+        compiler_params=pltpu.CompilerParams(vmem_limit_bytes=BIG_VMEM),
+    )(query, keys, values, low, high, logical, lse, grad, delta)
+
+
+def rotary_tables(offset):
+    half_dim = HD // 2
+    inverse = jnp.power(ROPE_THETA, -jnp.arange(half_dim, dtype=F32) * 2.0 / HD)
+    angles = offset.astype(F32)[:, None] * inverse[None, :]
+    return jnp.cos(angles), jnp.sin(angles)
+
+
+def turn(values, tables, sign):
+    cosine, sine_part = tables
+    first, second = values[:, : HD // 2], sign * values[:, HD // 2 :]
+    return jnp.concatenate(
+        [first * cosine - second * sine_part, (second * cosine + first * sine_part) * sign], axis=1
+    )
+
+
+def swap_cores(values):
+    return lax.ppermute(values, "core", [(0, 1), (1, 0)])
+
+
+def dotf(left, right, dims):
+    return lax.dot_general(left, right, (dims, ((), ())), preferred_element_type=F32)
+
+
+def plane_layer(
+    inputs,
+    cotangent,
+    w_query,
+    w_key,
+    w_value,
+    w_out,
+    w_gate,
+    w_up,
+    w_down,
+    query_gain,
+    key_gain,
+    attn_gain,
+    ffn_gain,
+    lengths,
+    block_order,
+):
+    z, y, x, k = place()
+    ctx = z * 2 + y
+    tok_rows, width_part = inputs.shape
+    plane_rows = tok_rows // 2
+    tokens = 8 * plane_rows
+    hidden = w_gate.shape[1] // 8
+
+    order = block_order.reshape(8, 2, -1)
+    block_rows = plane_rows // order.shape[2]
+
+    def logical_of(core):
+        blocks = lax.dynamic_index_in_dim(order, core, 1, keepdims=False).reshape(-1)
+        return (
+            blocks[:, None] * block_rows + jnp.arange(block_rows, dtype=jnp.int32)[None, :]
+        ).reshape(-1)
+
+    logical_own, logical_other = logical_of(k), logical_of(1 - k)
+    offset_own = sequence_tables(logical_own, lengths)[1]
+    offset_other = sequence_tables(logical_other, lengths)[1]
+    tables_own, tables_other = rotary_tables(offset_own), rotary_tables(offset_other)
+    low = (logical_own - offset_own)[:, None]
+    high = logical_own[:, None]
+    logical_keys = jnp.concatenate([logical_own, logical_other])[None, :]
+
+    def columns(weight):
+        return jnp.transpose(weight.astype(BF).reshape(2, HD, 4, HD), (2, 0, 1, 3))
+
+    out_part = jnp.transpose(w_out.astype(BF).reshape(4, HD, 2, HD), (0, 2, 1, 3))
+    blob = jnp.stack([columns(w_query), columns(w_key), columns(w_value), out_part], axis=2)
+    gains = jnp.stack([query_gain, key_gain, attn_gain, ffn_gain])
+    full_in, own_cot, wall, gains_full = open_layer(
+        inputs, cotangent, blob.reshape(8, 4, HD, HD), gains
+    )
+    head = x * 8 + ctx
+    attn_gain_row, ffn_gain_row = gains_full[2:3], gains_full[3:4]
+    query_gain_row = lax.dynamic_slice_in_dim(gains_full[0], head * HD, HD)[None, :]
+    key_gain_row = lax.dynamic_slice_in_dim(gains_full[1], head * HD, HD)[None, :]
+
+    def ffn_columns(weight):
+        return jnp.transpose(weight.astype(BF).reshape(-1, 8, hidden), (1, 0, 2))
+
+    ffn_blob = jnp.stack(
+        [
+            ffn_columns(w_gate),
+            ffn_columns(w_up),
+            w_down.astype(BF).reshape(8, hidden, -1),
+        ],
+        axis=1,
+    )
+    ffn_mine = lax.all_to_all(ffn_blob, CTX, split_axis=0, concat_axis=0, tiled=True)
+    ffn_other = swap_cores(ffn_mine)
+
+    def up_like(i):
+        return jnp.concatenate(
+            [ffn_mine[:, i].reshape(D, hidden), ffn_other[:, i].reshape(D, hidden)], axis=1
+        )
+
+    gate_w, up_w = up_like(0), up_like(1)
+    down_w = jnp.concatenate(
+        [
+            jnp.transpose(ffn_mine[:, 2], (1, 0, 2)).reshape(hidden, D),
+            jnp.transpose(ffn_other[:, 2], (1, 0, 2)).reshape(hidden, D),
+        ],
+        axis=0,
+    )
+
+    qkv_w = wall[:3].reshape(3, D, HD)
+    out_w = jnp.transpose(wall[3].reshape(16, HD, HD), (1, 0, 2)).reshape(HD, D)
+    rows_dims = ((1,), (0,))
+    query_proj = dotf(full_in, qkv_w[0], rows_dims)
+    key_proj = dotf(full_in, qkv_w[1], rows_dims)
+    value_low = dotf(full_in, qkv_w[2], rows_dims).astype(BF)
+    squares = jnp.concatenate(
+        [jnp.sum(query_proj * query_proj, axis=1), jnp.sum(key_proj * key_proj, axis=1)]
+    ).reshape(-1, 128)
+    totals, key_total_other, key_other, value_other = plane_totals(
+        squares, 1, (key_proj, value_low)
+    )
+    totals = totals.reshape(2, tokens)
+    query_scale = lax.rsqrt(totals[0] / D + EPSILON)[:, None]
+    key_scale = lax.rsqrt(totals[1] / D + EPSILON)[:, None]
+    key_scale_other = lax.rsqrt(key_total_other.reshape(tokens) / D + EPSILON)[:, None]
+    query_rot = turn(query_proj * query_scale * query_gain_row, tables_own, 1.0).astype(BF)
+    key_rot = turn(key_proj * key_scale * key_gain_row, tables_own, 1.0).astype(BF)
+    key_rot_other = turn(key_other * key_scale_other * key_gain_row, tables_other, 1.0).astype(BF)
+    keys_all = jnp.concatenate([key_rot, key_rot_other], axis=0)
+    values_all = jnp.concatenate([value_low, value_other], axis=0)
+    attended, lse = attend(query_rot, keys_all, values_all, low, high, logical_keys)
+    attended_low = attended.astype(BF)
+    source_own = lax.dynamic_slice_in_dim(full_in, (ctx * 2 + x) * (tokens // 16), tokens // 16)
+    residual_full, residual_own, branch_own = after_attention(
+        dotf(attended_low, out_w, rows_dims).astype(BF), source_own, attn_gain_row
+    )
+
+    gate_proj = dotf(residual_full, gate_w, rows_dims)
+    up_proj = dotf(residual_full, up_w, rows_dims)
+    gate_sigmoid = jax.nn.sigmoid(gate_proj)
+    mixed = (gate_proj * gate_sigmoid * up_proj).astype(BF)
+    grad_ffn, outputs, ffn_gain_term = after_ffn(
+        dotf(mixed, down_w, rows_dims).astype(BF), residual_own, own_cot, ffn_gain_row
+    )
+
+    sum_rows = ((0,), (0,))
+    turned = ((1,), (1,))
+    grad_mixed = dotf(grad_ffn, down_w, turned)
+    grad_gate = (
+        grad_mixed * up_proj * gate_sigmoid * (1.0 + gate_proj * (1.0 - gate_sigmoid))
+    ).astype(BF)
+    grad_up = (grad_mixed * gate_proj * gate_sigmoid).astype(BF)
+    resid_term = dotf(grad_gate, gate_w, turned) + dotf(grad_up, up_w, turned)
+    grad_attn, grad_own, attn_gain_term = after_ffn_back(
+        resid_term.astype(BF), own_cot, branch_own, attn_gain_row
+    )
+    gate_grad = dotf(residual_full, grad_gate, sum_rows)
+    up_grad = dotf(residual_full, grad_up, sum_rows)
+    down_grad = dotf(mixed, grad_ffn, sum_rows)
+    mine_grads = (gate_grad[:, :hidden], up_grad[:, :hidden], down_grad[:hidden])
+    other_grads = (gate_grad[:, hidden:], up_grad[:, hidden:], down_grad[hidden:])
+
+    def ffn_stack(grads):
+        return jnp.stack(
+            [
+                grads[0].reshape(8, -1, hidden),
+                grads[1].reshape(8, -1, hidden),
+                jnp.transpose(grads[2].reshape(hidden, 8, -1), (1, 0, 2)),
+            ],
+            axis=1,
+        )
+
+    from_other = swap_cores(ffn_stack(other_grads).astype(BF))
+    ffn_sum = (ffn_stack(mine_grads) + from_other.astype(F32)).astype(BF)
+    ffn_back = lax.all_to_all(ffn_sum, CTX, split_axis=0, concat_axis=0, tiled=True).astype(F32)
+    grad_w_gate = jnp.transpose(ffn_back[:, 0], (1, 0, 2)).reshape(w_gate.shape)
+    grad_w_up = jnp.transpose(ffn_back[:, 1], (1, 0, 2)).reshape(w_up.shape)
+    grad_w_down = ffn_back[:, 2].reshape(w_down.shape)
+
+    grad_heads = dotf(grad_attn, out_w, turned).astype(BF)
+    delta = jnp.sum(grad_heads.astype(F32) * attended, axis=1, keepdims=True)
+    grad_query_rot, grad_keys, grad_values = attend_back(
+        query_rot, keys_all, values_all, low, high, logical_keys, lse, grad_heads, delta
+    )
+    both = jnp.concatenate([grad_keys[tokens:], grad_values[tokens:]], axis=1).astype(BF)
+    received = swap_cores(both).astype(F32)
+    grad_key_rot = grad_keys[:tokens] + received[:, :HD]
+    grad_value_low = (grad_values[:tokens] + received[:, HD:]).astype(BF)
+    grad_query_normed = turn(grad_query_rot, tables_own, -1.0)
+    grad_key_normed = turn(grad_key_rot, tables_own, -1.0)
+    query_gain_term = jnp.sum(grad_query_normed * query_proj * query_scale, axis=0)
+    key_gain_term = jnp.sum(grad_key_normed * key_proj * key_scale, axis=0)
+    weighted_query = grad_query_normed * query_gain_row
+    weighted_key = grad_key_normed * key_gain_row
+    dots = jnp.concatenate(
+        [jnp.sum(weighted_query * query_proj, axis=1), jnp.sum(weighted_key * key_proj, axis=1)]
+    ).reshape(-1, 128)
+    dots = plane_totals(dots, 6).reshape(2, tokens, 1)
+    grad_query_low = (
+        query_scale * weighted_query - query_proj * (query_scale * query_scale * query_scale * dots[0] / D)
+    ).astype(BF)
+    grad_key_low = (
+        key_scale * weighted_key - key_proj * (key_scale * key_scale * key_scale * dots[1] / D)
+    ).astype(BF)
+    grad_qkv = jnp.concatenate([grad_query_low, grad_key_low, grad_value_low], axis=1)
+    input_term = dotf(grad_qkv, jnp.transpose(qkv_w, (1, 0, 2)).reshape(D, 3 * HD), turned)
+    qkv_grad = dotf(full_in, grad_qkv, sum_rows)
+    out_grad = dotf(attended_low, grad_attn, sum_rows)
+    wall_grad = jnp.concatenate(
+        [
+            jnp.transpose(qkv_grad.reshape(8, 2, HD, 3, HD), (1, 0, 3, 2, 4)),
+            jnp.transpose(out_grad.reshape(HD, 8, 2, HD), (2, 1, 0, 3))[:, :, None],
+        ],
+        axis=2,
+    )
+    to_other = lax.dynamic_index_in_dim(wall_grad, 1 - k, 0, keepdims=False).astype(BF)
+    to_owner = (
+        lax.dynamic_index_in_dim(wall_grad, k, 0, keepdims=False)
+        + swap_cores(to_other).astype(F32)
+    ).astype(BF)
+    input_grad, wall_back = close_layer(input_term.astype(BF), grad_own, to_owner)
+    wall_back = wall_back.astype(F32).reshape(4, 2, 4, HD, HD)
+
+    def columns_back(i):
+        return jnp.transpose(wall_back[:, :, i], (1, 2, 0, 3)).reshape(w_query.shape)
+
+    grad_w_out = jnp.transpose(wall_back[:, :, 3], (0, 2, 1, 3)).reshape(w_out.shape)
+
+    def all_features(term):
+        return lax.dynamic_update_slice_in_dim(jnp.zeros((D,), F32), term, head * HD, 0)
+
+    gain_totals = lax.psum(
+        jnp.stack(
+            [
+                all_features(query_gain_term),
+                all_features(key_gain_term),
+                jnp.sum(attn_gain_term, axis=0),
+                jnp.sum(ffn_gain_term, axis=0),
+            ]
+        ),
+        AXES,
+    )
+    gain_grads = lax.dynamic_slice_in_dim(gain_totals, (2 * x + k) * width_part, width_part, 1)
+    return (
+        outputs,
+        input_grad,
+        columns_back(0),
+        columns_back(1),
+        columns_back(2),
+        grad_w_out,
+        grad_w_gate,
+        grad_w_up,
+        grad_w_down,
+        gain_grads[0],
+        gain_grads[1],
+        gain_grads[2],
+        gain_grads[3],
+    )
 
 
 def full_rows(piece):
@@ -389,41 +1640,28 @@
     )
 
 
-def solution(mesh):
+def sharded(layer, mesh, ctx, head):
+    wide, tall, line = P(ctx, head), P(head, ctx), P(head)
     return jax.shard_map(
-        on_device,
+        layer,
         mesh=mesh,
         in_specs=(
-            P("ctx", "head"),
-            P("ctx", "head"),
-            P("ctx", "head"),
-            P("ctx", "head"),
-            P("ctx", "head"),
-            P("head", "ctx"),
-            P("ctx", "head"),
-            P("ctx", "head"),
-            P("head", "ctx"),
-            P("head"),
-            P("head"),
-            P("head"),
-            P("head"),
+            *(wide,) * 5,
+            tall,
+            wide,
+            wide,
+            tall,
+            *(line,) * 4,
             P(),
             P(),
         ),
-        out_specs=(
-            P("ctx", "head"),
-            P("ctx", "head"),
-            P("ctx", "head"),
-            P("ctx", "head"),
-            P("ctx", "head"),
-            P("head", "ctx"),
-            P("ctx", "head"),
-            P("ctx", "head"),
-            P("head", "ctx"),
-            P("head"),
-            P("head"),
-            P("head"),
-            P("head"),
-        ),
+        out_specs=(*(wide,) * 5, tall, wide, wide, tall, *(line,) * 4),
         check_vma=False,
     )
+
+
+def solution(mesh):
+    if dict(mesh.shape) == {"ctx": 8, "head": 4}:
+        split = Mesh(mesh.devices.reshape(4, 2, 2, 2), AXES)
+        return sharded(plane_layer, split, CTX, ("x", "core"))
+    return sharded(on_device, mesh, "ctx", "head")

time: 1890 us -> 738 us (0.39)
  waiting for transfers between devices: 1570 us -> 0.02 us
  Pallas kernels: 0 us -> 483 us
  local copies, waits for them, and re-layouts: 24 us -> 82.2 us
  matrix products: 116 us -> 66.7 us
  blocking collectives: 69.1 us -> 38.9 us
  other arithmetic: 63.6 us -> 41.8 us
    reduce_scatter x13 -> x0, waiting for transfers between devices: 879 us -> none  [the longest x1 152 us: on_device(): lax.psum_scatter(down_grad.astype(jnp.bfloat16), 'ctx', scatter_dimension...]
    all_gather x13 -> x0, waiting for transfers between devices: 684 us -> none  [the longest x1 127 us: gather_weights(): lax.all_gather(w_gate.astype(jnp.bfloat16), 'ctx', axis=0, tiled=True)]
    pallas_call x0 -> x9, Pallas kernels: none -> 483 us  [the longest x1 113 us: after_ffn_back(): comm_call(body, 'after_ffn_back', 4, (shape((tokens, width), BF), shape((...]
    dot_general x35 -> x17, matrix products: 116 us -> 66.7 us  [dotf(): lax.dot_general(left, right, (dims, ((), ())), preferred_element_type=F32)]
    convert_element_type x23 -> x12, other arithmetic: 38.5 us -> 15 us  [the longest x3 3.23 us: columns(): return jnp.transpose(weight.astype(BF).reshape(2, HD, 4, HD), (2, 0, 1, 3))]
    psum x7 -> x1, blocking collectives: 55.4 us -> 38.9 us  [plane_layer(): lax.psum(jnp.stack([all_features(query_gain_term), all_features(key_gain_...]
  transfers between devices with their start and end apart: 29 -> 6, of which waited for: 26 -> 0; matrix products, arithmetic and copies ran while one was open for 6% -> 17% of each run, Pallas kernels for 0% -> 55%
where the time goes in v1:
time: 738 us; the launch traced here: 727 us
  Pallas kernels  483 us (65%)
  local copies, waits for them, and re-layouts  82.2 us (11%)
  matrix products  66.7 us (9%)
  other arithmetic  41.8 us (6%)
  blocking collectives  38.9 us (5%)
  starting transfers between devices  13.1 us (2%)
    pallas_call x1, Pallas kernels, after_ffn_back(): comm_call(body, 'after_ffn_back', 4, (shape((tokens, width), BF), shape((...  113 us
    pallas_call x1, Pallas kernels, open_layer(): comm_call(body, 'open_layer', 0, (shape((8 * half, 4 * part), BF), shape(...  111 us
    pallas_call x1, Pallas kernels, after_ffn(): comm_call(body, 'after_ffn', 3, (shape((tokens, width), BF), shape((rows...  80.2 us
    pallas_call x1, Pallas kernels, after_attention(): comm_call(body, 'after_attention', 2, (shape((tokens, width), BF), shape(...  78.4 us
    dot_general x17, matrix products, dotf(): lax.dot_general(left, right, (dims, ((), ())), preferred_element_type=F32)  66.7 us
    pallas_call x1, Pallas kernels, close_layer(): comm_call(body, 'close_layer', 5, (shape((rows * 4, width // 4), BF), sha...  61.1 us
    psum x1, blocking collectives, plane_layer(): lax.psum(jnp.stack([all_features(query_gain_term), all_features(key_gain_...  38.9 us
    unnamed x96, local copies, waits for them, and re-layouts  17.1 us
  transfers between devices with their start and end apart: 6, of which 0 were waited for; matrix products, arithmetic and copies ran while one was open for 17% of the time, Pallas kernels for 55%

profile of v1, /device:TPU:1, one launch (start us, length us, event | category | flops | bytes accessed | tf_op | source)
XLA Modules:
  0.0 727.0 jit_solution(5435608404058644896)
XLA Ops:
  0.6 1.8 copy.360
  2.4 1.8 copy.361
  4.2 1.7 convert_element_type.126
  7.2 1.6 pad_maximum_fusion
  8.8 1.9 copy.363
  10.7 6.5 all-to-all-start
  19.9 1.7 copy.349
  23.5 1.7 copy.350
  27.0 1.7 copy.351
  32.2 2.2 pad_maximum_fusion.11.blob_ref
  34.4 111.4 %open_layer.1 = (bf16[1024,2048]{1,0:T(8,128)(2,1)}, bf16[64,2048]{1,0:T(8,128)(2,1)}, bf16[4,8,2,128,128]{4,3,2,1,0:T(8,128)(2,1)}, f32[4,2048]{1,0:T(4,128)}) custom-call(bf16[256,512]{1,0:T(8,128)(2,1)} %in_ref.1, bf16[256,512]{1,0:T(8,128)(2,1)} %cot_ref.1, bf16[8,4,128,128]{3,2,1,0:T(8,128)(2,1)} %pad_maximum_fusion.11.blob_ref, ...), custom_call_target="tpu_custom_call" | custom-call | tf_op jit(solution)/shard_map/open_layer/pallas_call | solution.py:600
  146.0 2.7 fusion.71
  148.7 2.3 multiply_reduce_fusion.5
  151.0 2.3 multiply_reduce_fusion.6
  153.3 1.9 convolution_convert_fusion.4.refs_2_
  155.9 2.8 copy.364
  159.4 1.3 add.191.high_ref
  161.8 2.0 copy.359
  163.8 2.0 copy.353.refs_1_
  165.9 2.0 copy.354
  167.9 10.1 %plane_totals_keys.1 = (f32[16,128]{1,0:T(8,128)}, f32[8,128]{1,0:T(8,128)}, f32[1024,128]{1,0:T(8,128)}, bf16[1024,128]{1,0:T(8,128)(2,1)}) custom-call(f32[16,128]{1,0:T(8,128)} %pad_maximum_fusion.22.refs_0_, f32[1024,128]{1,0:T(8,128)} %copy.353.refs_1_, bf16[1024,128]{1,0:T(8,128)(2,1)} %convolution_convert_fusion.4.refs_2_), custom_call_target="tpu_custom_call" | custom-call | tf_op jit(solution)/shard_map/plane_totals_keys/pallas_call | solution.py:721
  180.6 1.5 multiply_multiply_fusion.1
  182.2 4.9 fusion.41
  189.9 8.4 %attend.1 = (f32[1024,128]{1,0:T(8,128)}, f32[1024,1]{1,0:T(8,128)}) custom-call(bf16[1024,128]{1,0:T(8,128)(2,1)} %pad_maximum_fusion.19.q_ref, bf16[2048,128]{1,0:T(8,128)(2,1)} %maximum_maximum_fusion.k_ref, bf16[2048,128]{1,0:T(8,128)(2,1)} %pad_maximum_fusion.13.v_ref, s32[1024,1]{1,0:T(8,128)} %copy.357.low_ref, s32[1024,1]{1,0:T(8,128)} %add.191.high_ref, ...), custom_call_target="tpu_custom_call" | custom-call | tf_op jit(solution)/shard_map/attend/pallas_call | solution.py:958
  198.3 1.7 constant_dynamic-slice_fusion.source_ref
  200.0 4.3 convolution_convert_fusion.2.term_ref
  204.3 78.4 %after_attention.1 = (bf16[1024,2048]{1,0:T(8,128)(2,1)}, f32[64,2048]{1,0:T(8,128)}, f32[64,2048]{1,0:T(8,128)}) custom-call(bf16[1024,2048]{1,0:T(8,128)(2,1)} %convolution_convert_fusion.2.term_ref, bf16[64,2048]{1,0:T(8,128)(2,1)} %constant_dynamic-slice_fusion.source_ref, f32[1,2048]{1,0:T(1,128)} %get-tuple-element.158.gain_ref), custom_call_target="tpu_custom_call" | custom-call | tf_op jit(solution)/shard_map/after_attention/pallas_call | solution.py:760
  285.0 3.4 slice_bitcast_fusion
  289.0 5.0 fusion.10
  294.0 3.8 multiply_convert_fusion.2
  297.9 4.3 convolution_convert_fusion.1.term_ref
  302.2 80.2 %after_ffn.1 = (bf16[1024,2048]{1,0:T(8,128)(2,1)}, bf16[256,512]{1,0:T(8,128)(2,1)}, f32[8,2048]{1,0:T(8,128)}) custom-call(bf16[1024,2048]{1,0:T(8,128)(2,1)} %convolution_convert_fusion.1.term_ref, f32[64,2048]{1,0:T(8,128)} %get-tuple-element.46.res_ref, bf16[64,2048]{1,0:T(8,128)(2,1)} %get-tuple-element.47.cot_ref, f32[1,2048]{1,0:T(1,128)} %get-tuple-element.157.gain_ref), custom_call_target="tpu_custom_call" | custom-call | tf_op jit(solution)/shard_map/after_ffn/pallas_call | solution.py:804
  382.4 4.7 fusion.76
  387.1 2.9 multiply_convert_fusion.1
  390.3 2.3 copy-done.36
  392.6 2.4 fusion.74
  395.1 2.4 fusion.75
  399.6 1.6 slice-done
  401.4 5.7 fusion.8
  407.1 2.3 fusion
  409.4 4.6 all-to-all-start.1
  414.0 7.7 %add_convert_fusion.term_ref = bf16[1024,2048]{1,0:T(8,128)(2,1)} fusion(f32[1024,2048]{1,0:T(8,128)} %fusion.8, bf16[1024,512]{1,0:T(8,128)(2,1)S(1)} %copy-done.39, bf16[2048,256]{1,0:T(8,128)(2,1)S(1)} %bitcast.248, bf16[2048,256]{1,0:T(8,128)(2,1)S(1)} %bitcast.246), kind=kOutput, calls=%fused_computation | convolution fusion | flops 2155872256 | bytes 15728640 | tf_op jit(solution)/shard_map/dot_general | solution.py:1031
  421.7 113.2 %after_ffn_back.1 = (bf16[1024,2048]{1,0:T(8,128)(2,1)}, f32[64,2048]{1,0:T(8,128)}, f32[8,2048]{1,0:T(8,128)}) custom-call(bf16[1024,2048]{1,0:T(8,128)(2,1)} %add_convert_fusion.term_ref, bf16[64,2048]{1,0:T(8,128)(2,1)} %get-tuple-element.47.cot_ref, f32[64,2048]{1,0:T(8,128)} %get-tuple-element.51.branch_ref, f32[1,2048]{1,0:T(1,128)} %get-tuple-element.158.gain_ref), custom_call_target="tpu_custom_call" | custom-call | tf_op jit(solution)/shard_map/after_ffn_back/pallas_call | solution.py:848
  534.9 4.1 multiply_reduce_fusion.4
  540.1 10.8 %attend_back.1 = (f32[1024,128]{1,0:T(8,128)}, f32[2048,128]{1,0:T(8,128)}, f32[2048,128]{1,0:T(8,128)}) custom-call(bf16[1024,128]{1,0:T(8,128)(2,1)} %pad_maximum_fusion.19.q_ref, bf16[2048,128]{1,0:T(8,128)(2,1)} %maximum_maximum_fusion.k_ref, bf16[2048,128]{1,0:T(8,128)(2,1)} %pad_maximum_fusion.13.v_ref, s32[1024,1]{1,0:T(8,128)} %copy.357.low_ref, ...), custom_call_target="tpu_custom_call" | custom-call | tf_op jit(solution)/shard_map/attend_back/pallas_call | solution.py:996
  555.2 2.6 copy.377
  557.8 4.0 fusion.52
  564.3 1.9 slice_add_fusion.1
  566.2 2.5 fusion.44
  570.4 8.8 %plane_totals.1 = f32[16,128]{1,0:T(8,128)} custom-call(f32[16,128]{1,0:T(8,128)} %pad_maximum_fusion.23.refs_0_), custom_call_target="tpu_custom_call" | custom-call | tf_op jit(solution)/shard_map/plane_totals/pallas_call | solution.py:718
  581.6 2.8 fusion.51
  584.4 3.8 reshape.339
  588.2 4.1 copy.379
  592.2 2.1 fusion.11
  595.8 38.9 %psum.7 = f32[4,2048]{1,0:T(4,128)S(1)} all-reduce(f32[4,2048]{1,0:T(4,128)S(1)} %pad_maximum_fusion.20), channel_id=1, replica_groups=mesh['z'=4,'y'=2,'x'=2,'core'=2] {'z','y','x','core'}, use_global_device_ids=true, to_apply=%region_14.15 | all-reduce | flops 8192 | bytes 65536 | tf_op jit(solution)/shard_map/psum | solution.py:1239
  635.3 6.0 convolution_convert_fusion.term_ref
  641.3 2.5 fusion.6.blob_ref
  643.8 61.1 %close_layer.1 = (bf16[256,512]{1,0:T(8,128)(2,1)}, bf16[8,4,128,128]{3,2,1,0:T(8,128)(2,1)}) custom-call(bf16[1024,2048]{1,0:T(8,128)(2,1)} %convolution_convert_fusion.term_ref, f32[64,2048]{1,0:T(8,128)} %get-tuple-element.56.grad_ref, bf16[8,4,128,128]{3,2,1,0:T(8,128)(2,1)} %fusion.6.blob_ref), custom_call_target="tpu_custom_call" | custom-call | tf_op jit(solution)/shard_map/close_layer/pallas_call | solution.py:914
  704.9 1.5 convert.55
  711.3 3.2 copy.392
  714.5 2.9 fusion.69
  717.5 2.9 copy.393
  720.3 3.0 copy.397
  723.4 1.8 copy.396
  (176 shorter events, 44.4 us)
Async XLA Ops:
  10.7 6.5 copy-start.37
  10.7 6.7 copy-start.34
  10.7 145.2 %all-to-all-start = ((bf16[8,3,256,256]{2,3,1,0:T(8,128)(2,1)}), bf16[8,3,256,256]{2,3,1,0:T(8,128)(2,1)S(1)}, u32[]{:S(2)}, u32[]{:S(2)}) async-start(bf16[8,3,256,256]{2,3,1,0:T(8,128)(2,1)} %copy.363), calls=%async_computation | async-start | bytes 6291456 | tf_op jit(solution)/shard_map/all_to_all | solution.py:1100
  19.9 11.6 %copy-start.30 = (f32[512]{0:T(512)S(1)}, f32[512]{0:T(512)}, u32[]{:S(2)}) copy-start(f32[512]{0:T(512)} %param.27) | copy-start | bytes 6148
  19.9 11.6 %copy-start.31 = (f32[512]{0:T(512)S(1)}, f32[512]{0:T(512)}, u32[]{:S(2)}) copy-start(f32[512]{0:T(512)} %param.26) | copy-start | bytes 6148
  19.9 11.7 %copy-start.32 = (f32[512]{0:T(512)S(1)}, f32[512]{0:T(512)}, u32[]{:S(2)}) copy-start(f32[512]{0:T(512)} %param.25) | copy-start | bytes 6148
  19.9 11.7 %copy-start.33 = (f32[512]{0:T(512)S(1)}, f32[512]{0:T(512)}, u32[]{:S(2)}) copy-start(f32[512]{0:T(512)} %param.24) | copy-start | bytes 6148
  145.8 2.9 copy-start
  153.3 2.0 copy-start.29
  158.7 126.3 %collective-permute-start = (bf16[8,3,256,256]{3,2,0,1:T(8,128)(2,1)}, bf16[8,3,256,256]{3,2,0,1:T(8,128)(2,1)}, u32[]{:S(2)}, u32[]{:S(2)}) collective-permute-start(bf16[8,3,256,256]{3,2,0,1:T(8,128)(2,1)} %copy.364), channel_id=1, source_target_pairs={{0,1},{1,0},{2,3},{3,2},{4,5},{5,4},{6,7},{7,6},{8,9},{9,8},{10,11... | collective-permute-start | bytes 9437192 | tf_op jit(solution)/shard_map/ppermute | solution.py:1027
  182.1 5.8 copy-start.17
  182.1 5.8 copy-start.25
  187.1 12.9 %copy-start.13 = (bf16[16,128,128]{1,2,0:T(8,128)(2,1)S(1)}, bf16[16,128,128]{1,2,0:T(8,128)(2,1)}, u32[]{:S(2)}) copy-start(bf16[16,128,128]{1,2,0:T(8,128)(2,1)} %copy.359) | copy-start | bytes 1572868
  204.3 79.5 %copy-start.6 = (bf16[8,3,256,256]{3,2,0,1:T(8,128)(2,1)S(1)}, bf16[8,3,256,256]{3,2,0,1:T(8,128)(2,1)}, u32[]{:S(2)}) copy-start(bf16[8,3,256,256]{3,2,0,1:T(8,128)(2,1)} %copy.364) | copy-start | bytes 9437188
  289.0 5.0 copy-start.19
  289.0 5.0 copy-start.20
  289.0 5.0 copy-start.35
  294.0 3.9 copy-start.40
  294.0 3.9 copy-start.16
  382.3 4.8 copy-start.4
  382.4 4.8 copy-start.41
  382.4 4.8 copy-start.42
  387.1 11.6 %copy-start.3 = (f32[512,2048]{1,0:T(8,128)}, f32[512,2048]{1,0:T(8,128)S(1)}, u32[]{:S(2)}) copy-start(f32[512,2048]{1,0:T(8,128)S(1)} %fusion.76) | copy-start | bytes 12582916
  390.1 5.0 copy-start.38
  390.1 2.6 copy-start.36
  395.1 4.5 copy-start.8
  397.6 2.0 copy-start.7
  398.2 8.8 %collective-permute-start.3 = (bf16[8,3,256,256]{3,2,1,0:T(8,128)(2,1)S(1)}, bf16[8,3,256,256]{3,2,1,0:T(8,128)(2,1)S(1)}, u32[]{:S(2)}, u32[]{:S(2)}) collective-permute-start(bf16[8,3,256,256]{3,2,1,0:T(8,128)(2,1)S(1)} %pad_maximum_fusion.1), channel_id=1, source_target_pairs={{0,1},{1,0},{2,3},{3,2},{4,5},{5,4},{6,7},{7,6},{8,9},{9,8},{10,11... | collective-permute-start | bytes 9437192 | tf_op jit(solution)/shard_map/ppermute | solution.py:1027
  399.6 1.6 slice-start
  401.4 5.7 slice-start.1
  401.4 5.7 slice-start.2
  409.4 4.6 copy-start.18
  409.4 4.6 copy-start.39
  409.4 302.0 %all-to-all-start.1 = ((bf16[8,3,256,256]{3,2,1,0:T(8,128)(2,1)}), bf16[8,3,256,256]{3,2,1,0:T(8,128)(2,1)}, u32[]{:S(2)}, u32[]{:S(2)}) async-start(bf16[8,3,256,256]{3,2,1,0:T(8,128)(2,1)} %fusion), calls=%async_computation.1 | async-start | bytes 6291456 | tf_op jit(solution)/shard_map/all_to_all | solution.py:1182
  421.7 113.3 %copy-start.12 = (f32[1024,128]{1,0:T(8,128)S(1)}, f32[1024,128]{1,0:T(8,128)}, u32[]{:S(2)}) copy-start(f32[1024,128]{1,0:T(8,128)} %get-tuple-element.44) | copy-start | bytes 1572868
  421.7 113.3 %copy-start.14 = (bf16[16,128,128]{1,2,0:T(8,128)(2,1)S(1)}, bf16[16,128,128]{1,2,0:T(8,128)(2,1)}, u32[]{:S(2)}) copy-start(bf16[16,128,128]{1,2,0:T(8,128)(2,1)} %copy.359) | copy-start | bytes 1572868
  539.1 14.9 %copy-start.11 = (bf16[4,8,2,128,128]{4,3,2,1,0:T(8,128)(2,1)S(1)}, bf16[4,8,2,128,128]{4,3,2,1,0:T(8,128)(2,1)}, u32[]{:S(2)}) copy-start(bf16[4,8,2,128,128]{4,3,2,1,0:T(8,128)(2,1)} %get-tuple-element.38) | copy-start | bytes 6291460
  553.9 9.2 %collective-permute-start.1 = (bf16[1024,256]{1,0:T(8,128)(2,1)}, bf16[1024,256]{1,0:T(8,128)(2,1)}, u32[]{:S(2)}, u32[]{:S(2)}) collective-permute-start(bf16[1024,256]{1,0:T(8,128)(2,1)} %pad_maximum_fusion.15), channel_id=1, source_target_pairs={{0,1},{1,0},{2,3},{3,2},{4,5},{5,4},{6,7},{7,6},{8,9},{9,8},{10,11... | collective-permute-start | bytes 1572872 | tf_op jit(solution)/shard_map/ppermute | solution.py:1027
  557.8 5.3 copy-start.26
  557.8 5.3 copy-start.27
  561.7 2.5 copy-start.21
  561.8 4.4 copy-start.15
  564.3 4.5 copy-start.10
  566.2 3.1 copy-start.2
  566.2 13.0 %copy-start.28 = (f32[16,128]{1,0:T(8,128)S(1)}, f32[16,128]{1,0:T(8,128)}, u32[]{:S(2)}) copy-start(f32[16,128]{1,0:T(8,128)} %get-tuple-element.39) | copy-start | bytes 24580
  568.7 12.9 %copy-start.1 = (bf16[1024,2048]{1,0:T(8,128)(2,1)S(1)}, bf16[1024,2048]{1,0:T(8,128)(2,1)}, u32[]{:S(2)}) copy-start(bf16[1024,2048]{1,0:T(8,128)(2,1)} %get-tuple-element.37) | copy-start | bytes 12582916
  580.9 0.7 copy-start.24
  594.4 46.9 %collective-permute-start.2 = (bf16[8,4,128,128]{3,2,1,0:T(8,128)(2,1)}, bf16[8,4,128,128]{3,2,1,0:T(8,128)(2,1)}, u32[]{:S(2)}, u32[]{:S(2)}) collective-permute-start(bf16[8,4,128,128]{3,2,1,0:T(8,128)(2,1)} %fusion.11), channel_id=1, source_target_pairs={{0,1},{1,0},{2,3},{3,2},{4,5},{5,4},{6,7},{7,6},{8,9},{9,8},{10,11... | collective-permute-start | bytes 3145736 | tf_op jit(solution)/shard_map/ppermute | solution.py:1027
  635.3 6.0 copy-start.5
  720.3 3.0 copy-start.9
  723.4 1.8 copy-start.22
  723.4 2.5 copy-start.23

commit v2 on v1

--- a/solution.py
+++ b/solution.py
@@ -91,7 +91,7 @@
 GATHER_SEMS = [DMA((16,)), DMA((4,)), DMA((4,)), DMA((4,)), DMA((8,))]
 
 
-def gather_plane(me, own_ref, view, sems):
+def gather_plane(me, own_ref, view, sems, between=lambda step: None):
     z, y, x, k = me
     recv, up_send, down_send, a_send, b_send = sems
     a, b, slot, dev_a, dev_b = plane_axes(me)
@@ -134,6 +134,7 @@
             index = slot(near_first(step - 1, z), 1 - a, b)
             landed(index)
             copy(view(index), index, b_send.at[3 + step], dev_b).start()
+        between(step)
     for step in range(4):
         zp = near_first(step, z)
         landed(slot(zp, a, 1 - b))
@@ -158,13 +159,11 @@
 def reduce_scratch(rows, width):
     return [
         pltpu.VMEM((4, 2, rows, width), BF),
-        pltpu.VMEM((4, 2, rows, width), BF),
         pltpu.VMEM((4, rows, width), BF),
         pltpu.VMEM((4, rows, width), BF),
         pltpu.VMEM((4, rows, width), BF),
         pltpu.VMEM((4, rows, width), BF),
         pltpu.VMEM((4, rows, width), BF),
-        DMA((8,)),
         DMA((8,)),
         DMA((8,)),
         DMA((4,)),
@@ -175,16 +174,30 @@
     ]
 
 
-def reduce_plane(me, view, rows, scratch, finish):
+N_REDUCE = 13
+
+
+def strips(rows, work, strip=STRIP):
+    def body(i, carry):
+        work(pl.ds(pl.multiple_of(i * strip, strip), strip))
+        return carry
+
+    lax.fori_loop(0, rows // strip, body, 0)
+
+
+def reduce_plane(me, terms, rows, scratch, produce, finish, after_terms=lambda: None):
     z, y, x, k = me
-    (mine, from_b, to_a, from_a, to_z, from_low, from_high) = scratch[:7]
-    (load_sem, b_send, b_recv, a_send, a_recv, z_send, low_recv, high_recv) = scratch[7:]
+    (from_b, to_a, from_a, to_z, from_low, from_high) = scratch[:6]
+    (b_send, b_recv, a_send, a_recv, z_send, low_recv, high_recv) = scratch[6:]
     a, b, slot, dev_a, dev_b = plane_axes(me)
     order = [near_first(step, z) for step in (3, 2, 1, 0)]
 
+    def start_of(zp, ap, bp):
+        return pl.multiple_of(slot(zp, ap, bp) * rows, rows)
+
     def copy_b(zp, ap):
         return pltpu.make_async_remote_copy(
-            src_ref=view(slot(zp, ap, 1 - b)),
+            src_ref=terms.at[pl.ds(start_of(zp, ap, 1 - b), rows), :],
             dst_ref=from_b.at[zp, ap],
             send_sem=b_send.at[zp * 2 + ap],
             recv_sem=b_recv.at[zp * 2 + ap],
@@ -202,67 +215,52 @@
             device_id_type=MESH,
         )
 
-    def copy_up(zp):
+    def copy_z(zp, target, recv, to):
         return pltpu.make_async_remote_copy(
             src_ref=to_z.at[zp],
-            dst_ref=from_low.at[zp],
+            dst_ref=target.at[zp],
             send_sem=z_send.at[zp],
-            recv_sem=low_recv.at[zp],
-            device_id=(z + 1, y, x, k),
+            recv_sem=recv.at[zp],
+            device_id=(to, y, x, k),
             device_id_type=MESH,
         )
 
+    def copy_up(zp):
+        return copy_z(zp, from_low, low_recv, z + 1)
+
     def copy_down(zp):
-        return pltpu.make_async_remote_copy(
-            src_ref=to_z.at[zp],
-            dst_ref=from_high.at[zp],
-            send_sem=z_send.at[zp],
-            recv_sem=high_recv.at[zp],
-            device_id=(z - 1, y, x, k),
-            device_id_type=MESH,
-        )
-
-    def load(zp, ap):
-        return pltpu.make_async_copy(
-            view(slot(zp, ap, b)), mine.at[zp, ap], load_sem.at[zp * 2 + ap]
-        )
+        return copy_z(zp, from_high, high_recv, z - 1)
+
+    def mine(zp, ap, strip):
+        at = pl.ds(pl.multiple_of(start_of(zp, ap, b) + strip.start, STRIP), STRIP)
+        return terms[at, :].astype(F32)
 
     for zp in order:
+        produce(zp)
         for ap in (1 - a, a):
             copy_b(zp, ap).start()
-    for zp in order:
-        for ap in (1 - a, a):
-            load(zp, ap).start()
-
-    def strips(work):
-        def body(i, carry):
-            work(pl.ds(pl.multiple_of(i * STRIP, STRIP), STRIP))
-            return carry
-
-        lax.fori_loop(0, rows // STRIP, body, 0)
+    after_terms()
 
     for step in range(5):
         if step < 4:
             zp = order[step]
-            load(zp, 1 - a).wait()
             copy_b(zp, 1 - a).wait_recv()
 
             def first(strip, zp=zp):
                 to_a[zp, strip] = (
-                    mine[zp, 1 - a, strip].astype(F32) + from_b[zp, 1 - a, strip].astype(F32)
+                    mine(zp, 1 - a, strip) + from_b[zp, 1 - a, strip].astype(F32)
                 ).astype(BF)
 
-            strips(first)
+            strips(rows, first)
             copy_a(zp).start()
         if step > 0:
             zp = order[step - 1]
-            load(zp, a).wait()
             copy_b(zp, a).wait_recv()
             copy_a(zp).wait_recv()
 
             def own_sum(strip, zp=zp):
                 return (
-                    mine[zp, a, strip].astype(F32)
+                    mine(zp, a, strip)
                     + from_b[zp, a, strip].astype(F32)
                     + from_a[zp, strip].astype(F32)
                 )
@@ -272,42 +270,28 @@
 
                 @pl.when(upward & (z > 0))
                 def _(zp=zp, own_sum=own_sum):
-                    pltpu.make_async_remote_copy(
-                        src_ref=to_z.at[zp],
-                        dst_ref=from_low.at[zp],
-                        send_sem=z_send.at[zp],
-                        recv_sem=low_recv.at[zp],
-                        device_id=(z, y, x, k),
-                        device_id_type=MESH,
-                    ).wait_recv()
+                    copy_up(zp).wait_recv()
 
                     def work(strip):
                         to_z[zp, strip] = (own_sum(strip) + from_low[zp, strip].astype(F32)).astype(BF)
 
-                    strips(work)
+                    strips(rows, work)
 
                 @pl.when(jnp.logical_not(upward) & (z < 3))
                 def _(zp=zp, own_sum=own_sum):
-                    pltpu.make_async_remote_copy(
-                        src_ref=to_z.at[zp],
-                        dst_ref=from_high.at[zp],
-                        send_sem=z_send.at[zp],
-                        recv_sem=high_recv.at[zp],
-                        device_id=(z, y, x, k),
-                        device_id_type=MESH,
-                    ).wait_recv()
+                    copy_down(zp).wait_recv()
 
                     def work(strip):
                         to_z[zp, strip] = (own_sum(strip) + from_high[zp, strip].astype(F32)).astype(BF)
 
-                    strips(work)
+                    strips(rows, work)
 
                 @pl.when((z == 0) | (z == 3))
                 def _(zp=zp, own_sum=own_sum):
                     def work(strip):
                         to_z[zp, strip] = own_sum(strip).astype(BF)
 
-                    strips(work)
+                    strips(rows, work)
 
                 @pl.when(upward)
                 def _(zp=zp):
@@ -322,22 +306,23 @@
                 @pl.when(z == 0)
                 def _():
                     copy_down(z).wait_recv()
-                    strips(lambda s: finish(s, own_sum(s) + from_high[z, s].astype(F32)))
+                    strips(rows, lambda s: finish(s, own_sum(s) + from_high[z, s].astype(F32)))
 
                 @pl.when(z == 3)
                 def _():
                     copy_up(z).wait_recv()
-                    strips(lambda s: finish(s, own_sum(s) + from_low[z, s].astype(F32)))
+                    strips(rows, lambda s: finish(s, own_sum(s) + from_low[z, s].astype(F32)))
 
                 @pl.when((z > 0) & (z < 3))
                 def _():
                     copy_up(z).wait_recv()
                     copy_down(z).wait_recv()
                     strips(
+                        rows,
                         lambda s: finish(
                             s,
                             own_sum(s) + from_low[z, s].astype(F32) + from_high[z, s].astype(F32),
-                        )
+                        ),
                     )
 
     def settle():
@@ -441,18 +426,48 @@
     pl.semaphore_wait(barrier, 17)
 
 
-def open_layer(inputs, cotangent, blob, gains):
+def masked_scores(q, keys, low, high, logical):
+    raw = lax.dot_general(q, keys, (((1,), (1,)), ((), ())), preferred_element_type=F32)
+    allowed = (logical >= low) & (logical <= high)
+    return raw * (1.0 / math.sqrt(HD)), allowed
+
+
+def open_layer(inputs, cotangent, w_query, w_key, w_value, w_out, w_gate, w_up, w_down, gains):
     rows, part = inputs.shape
     half = rows // 2
     quarter = half // 2
-
-    def body(in_ref, cot_ref, blob_ref, gain_ref, full_ref, own_cot_ref, wall_ref, gains_ref, *scratch):
-        shard, cot_half, pair_send, pair_recv, local_sem = scratch[:5]
-        deal_send, deal_recv, share_send, share_recv, gain_send, gain_recv, cot_sems = scratch[5:12]
-        gather_sems = scratch[12:]
+    tokens, width = 8 * half, 4 * part
+    hidden = w_gate.shape[1]
+
+    def body(*refs):
+        (in_ref, cot_ref, wq_ref, wk_ref, wv_ref, wo_ref, wg_ref, wu_ref, wd_ref, gain_ref) = refs[:10]
+        (full_out, own_out, own_cot_ref, wqkv_ref, wout_ref, gains_ref, gu_out, d_out) = refs[10:18]
+        (q_ref, k_ref, v_ref) = refs[18:21]
+        (full_ref, shard, cot_half, qkv_raw, out_raw, gu_raw, d_raw) = refs[21:28]
+        (qkv_stage, out_stage, gu_stage, d_stage) = refs[28:32]
+        (load_sem, pair_send, pair_recv, local_sem, deal_send, deal_recv) = refs[32:38]
+        (share_send, share_recv, gain_send, gain_recv, cot_sems, keep_sem) = refs[38:44]
+        gather_sems = refs[44:]
         me = z, y, x, k = place()
         ctx = own_tile(me)
         sibling = (z, y, x, 1 - k)
+
+        loads = [
+            pltpu.make_async_copy(src, dst, load_sem.at[i])
+            for i, (src, dst) in enumerate(
+                [
+                    (wq_ref, qkv_raw.at[0]),
+                    (wk_ref, qkv_raw.at[1]),
+                    (wv_ref, qkv_raw.at[2]),
+                    (wo_ref, out_raw),
+                    (wg_ref, gu_raw.at[0]),
+                    (wu_ref, gu_raw.at[1]),
+                    (wd_ref, d_raw),
+                ]
+            )
+        ]
+        for load in loads:
+            load.start()
         same_x_greet(me)
 
         def pair_copy(src, dst, number):
@@ -477,33 +492,6 @@
         first = pair_copy(in_ref, shard, 0)
         second = pair_copy(cot_ref, cot_half, 1)
 
-        def deal(e):
-            return pltpu.make_async_remote_copy(
-                src_ref=blob_ref.at[e],
-                dst_ref=wall_ref.at[:, ctx, e % 2],
-                send_sem=deal_send.at[e],
-                recv_sem=deal_recv.at[ctx],
-                device_id=(2 * k + e // 4, (e // 2) % 2, x, e % 2),
-                device_id_type=MESH,
-            )
-
-        def deal_own(e):
-            return pltpu.make_async_copy(
-                blob_ref.at[e], wall_ref.at[:, ctx, k], deal_recv.at[ctx]
-            )
-
-        stays = k == z // 2
-        own_e = (z % 2) * 4 + y * 2 + k
-        for e in range(8):
-
-            @pl.when(jnp.logical_not(stays & (own_e == e)))
-            def _(e=e):
-                deal(e).start()
-
-            @pl.when(stays & (own_e == e))
-            def _(e=e):
-                deal_own(e).start()
-
         def gain_copy(xt, kt, number):
             return pltpu.make_async_remote_copy(
                 src_ref=gain_ref,
@@ -536,8 +524,69 @@
         own_slot = ctx * 2 + x
         own_local = pltpu.make_async_copy(shard, view(own_slot), local_sem.at[3])
         own_local.start()
-        second[0].wait_recv()
-        second[1].wait()
+
+        def deal(e):
+            j, r = e // 2, e % 2
+            return [
+                pltpu.make_async_remote_copy(
+                    src_ref=src,
+                    dst_ref=dst,
+                    send_sem=deal_send.at[i, e],
+                    recv_sem=deal_recv.at[i, ctx],
+                    device_id=(2 * k + e // 4, (e // 2) % 2, x, r),
+                    device_id_type=MESH,
+                )
+                for i, (src, dst) in enumerate(deal_ends(j, r))
+            ]
+
+        def deal_ends(j, r):
+            at = pl.ds(pl.multiple_of(ctx * 2 * HD + r * HD, HD), HD)
+            return (
+                (
+                    qkv_stage.at[:, r * HD : (r + 1) * HD, j * HD : (j + 1) * HD],
+                    wqkv_ref.at[:, at, :],
+                ),
+                (
+                    out_stage.at[j * HD : (j + 1) * HD, r * HD : (r + 1) * HD],
+                    wout_ref.at[:, at],
+                ),
+            )
+
+        stays = k == z // 2
+        own_e = (z % 2) * 4 + y * 2 + k
+
+        def deal_all():
+            for load in loads[:4]:
+                load.wait()
+
+            def round_qkv(s):
+                for i in range(3):
+                    qkv_stage[i, s] = qkv_raw[i, s].astype(BF)
+
+            strips(rows, round_qkv)
+
+            def round_out(s):
+                out_stage[s] = out_raw[s].astype(BF)
+
+            strips(2 * rows, round_out, 32)
+            for e in range(8):
+
+                @pl.when(jnp.logical_not(stays & (own_e == e)))
+                def _(e=e):
+                    for copy in deal(e):
+                        copy.start()
+
+                @pl.when(stays & (own_e == e))
+                def _(e=e):
+                    for i, (src, dst) in enumerate(deal_ends(e // 2, e % 2)):
+                        pltpu.make_async_copy(src, dst, deal_recv.at[i, ctx]).start()
+
+        def cot_begin():
+            second[0].wait_recv()
+            second[1].wait()
+            cot_remote.start()
+            cot_local.start()
+
         wide = pl.ds(pl.multiple_of(x * 2 * part, 2 * part), 2 * part)
         cot_remote = pltpu.make_async_remote_copy(
             src_ref=cot_half.at[pl.ds(pl.multiple_of((1 - x) * quarter, quarter), quarter), :],
@@ -547,38 +596,99 @@
             device_id=(z, y, 1 - x, k),
             device_id_type=MESH,
         )
-        cot_remote.start()
         cot_local = pltpu.make_async_copy(
             cot_half.at[pl.ds(pl.multiple_of(x * quarter, quarter), quarter), :],
             own_cot_ref.at[:, wide],
             cot_sems.at[2],
         )
-        cot_local.start()
-        gather_plane(me, shard, view, gather_sems)
+
+        keeps = [
+            pltpu.make_async_copy(gu_stage.at[0], gu_out.at[0], keep_sem.at[0]),
+            pltpu.make_async_copy(gu_stage.at[1], gu_out.at[1], keep_sem.at[1]),
+            pltpu.make_async_copy(d_stage, d_out, keep_sem.at[2]),
+        ]
+
+        def round_up(i):
+            loads[4 + i].wait()
+
+            def work(s):
+                gu_stage[i, s] = gu_raw[i, s].astype(BF)
+
+            strips(rows, work)
+            keeps[i].start()
+
+        def round_down():
+            loads[6].wait()
+
+            def work(s):
+                d_stage[s] = d_raw[s].astype(BF)
+
+            strips(hidden, work, 128)
+            keeps[2].start()
+
+        between = [
+            deal_all,
+            lambda: (cot_begin(), round_up(0)),
+            lambda: round_up(1),
+            round_down,
+            lambda: None,
+        ]
+        gather_plane(me, shard, view, gather_sems, lambda step: between[step]())
+
+        def deal_wait(c):
+            at = slice(c * 2 * HD, c * 2 * HD + HD)
+            pltpu.make_async_copy(
+                qkv_stage.at[:, :HD, :HD], wqkv_ref.at[:, at, :], deal_recv.at[0, c]
+            ).wait()
+            pltpu.make_async_copy(
+                out_stage.at[:HD, :HD], wout_ref.at[:, at], deal_recv.at[1, c]
+            ).wait()
+
+        def share(c, r):
+            at = pl.ds(pl.multiple_of(c * 2 * HD + r * HD, HD), HD)
+            return [
+                pltpu.make_async_remote_copy(
+                    src_ref=ref,
+                    dst_ref=ref,
+                    send_sem=share_send.at[i, c],
+                    recv_sem=share_recv.at[i, c],
+                    device_id=sibling,
+                    device_id_type=MESH,
+                )
+                for i, ref in enumerate((wqkv_ref.at[:, at, :], wout_ref.at[:, at]))
+            ]
+
         for c in range(8):
-
-            def wait_deal(c=c):
-                pltpu.make_async_copy(
-                    blob_ref.at[0], wall_ref.at[:, c, k], deal_recv.at[c]
-                ).wait()
-
-            wait_deal()
-        share = pltpu.make_async_remote_copy(
-            src_ref=wall_ref.at[:, :, k],
-            dst_ref=wall_ref.at[:, :, k],
-            send_sem=share_send,
-            recv_sem=share_recv,
-            device_id=sibling,
-            device_id_type=MESH,
-        )
-        share.start()
+            deal_wait(c)
+            for copy in share(c, k):
+                copy.start()
+        own_local.wait()
+        full_keep = pltpu.make_async_copy(full_ref, full_out, keep_sem.at[3])
+        full_keep.start()
+        own_rows = pl.ds(pl.multiple_of(own_slot * quarter, quarter), quarter)
+        own_keep = pltpu.make_async_copy(full_ref.at[own_rows, :], own_out, keep_sem.at[4])
+        own_keep.start()
+        for c in range(8):
+            for copy in share(c, 1 - k):
+                copy.wait_recv()
+
+        def project(s):
+            tile = full_ref[s, :]
+            q_ref[s, :] = jnp.dot(tile, wqkv_ref[0], preferred_element_type=F32)
+            k_ref[s, :] = jnp.dot(tile, wqkv_ref[1], preferred_element_type=F32)
+            v_ref[s, :] = jnp.dot(tile, wqkv_ref[2], preferred_element_type=F32).astype(BF)
+
+        strips(tokens, project, 256)
         for e in range(8):
 
             @pl.when(jnp.logical_not(stays & (own_e == e)))
             def _(e=e):
-                deal(e).wait_send()
-
-        own_local.wait()
+                for copy in deal(e):
+                    copy.wait_send()
+
+        for c in range(8):
+            for copy in share(c, k):
+                copy.wait_send()
         first[0].wait_send()
         second[0].wait_send()
         for copy in gain_copies:
@@ -586,15 +696,8 @@
         gain_local.wait()
         cot_remote.wait()
         cot_local.wait()
-        share.wait_send()
-        pltpu.make_async_remote_copy(
-            src_ref=wall_ref.at[:, :, 1 - k],
-            dst_ref=wall_ref.at[:, :, 1 - k],
-            send_sem=share_send,
-            recv_sem=share_recv,
-            device_id=sibling,
-            device_id_type=MESH,
-        ).wait_recv()
+        for keep in (*keeps, full_keep, own_keep):
+            keep.wait()
 
     shape = jax.ShapeDtypeStruct
     return comm_call(
@@ -602,72 +705,139 @@
         "open_layer",
         0,
         (
-            shape((8 * half, 4 * part), BF),
-            shape((quarter, 4 * part), BF),
-            shape((4, 8, 2, HD, HD), BF),
-            shape((4, 4 * part), F32),
+            shape((tokens, width), BF),
+            shape((quarter, width), BF),
+            shape((quarter, width), BF),
+            shape((3, width, HD), BF),
+            shape((HD, width), BF),
+            shape((4, width), F32),
+            shape((2, rows, hidden), BF),
+            shape((hidden, rows), BF),
+            shape((tokens, HD), F32),
+            shape((tokens, HD), F32),
+            shape((tokens, HD), BF),
         ),
-        [ANY, ANY, ANY, ANY],
-        (ANY, ANY, ANY, ANY),
+        [ANY] * 10,
+        (ANY, ANY, ANY, VMEM, VMEM, ANY, ANY, ANY, VMEM, VMEM, VMEM),
         [
+            pltpu.VMEM((tokens, width), BF),
             pltpu.VMEM((half, 2 * part), BF),
             pltpu.VMEM((half, 2 * part), BF),
+            pltpu.VMEM((3, rows, part), F32),
+            pltpu.VMEM((part, rows), F32),
+            pltpu.VMEM((2, rows, hidden), F32),
+            pltpu.VMEM((hidden, rows), F32),
+            pltpu.VMEM((3, rows, part), BF),
+            pltpu.VMEM((part, rows), BF),
+            pltpu.VMEM((2, rows, hidden), BF),
+            pltpu.VMEM((hidden, rows), BF),
+            DMA((7,)),
             DMA((2,)),
             DMA((2,)),
             DMA((4,)),
-            DMA((8,)),
-            DMA((8,)),
-            DMA,
-            DMA,
+            DMA((2, 8)),
+            DMA((2, 8)),
+            DMA((2, 8)),
+            DMA((2, 8)),
             DMA((3,)),
             DMA((3,)),
             DMA((3,)),
+            DMA((5,)),
             *GATHER_SEMS,
         ],
-    )(inputs, cotangent, blob, gains)
-
-
-def plane_totals(terms, number, share=None):
-    count = terms.shape[0]
+    )(inputs, cotangent, w_query, w_key, w_value, w_out, w_gate, w_up, w_down, gains)
+
+
+def eye_mask():
+    return lax.broadcasted_iota(jnp.int32, (HD, HD), 0) == lax.broadcasted_iota(
+        jnp.int32, (HD, HD), 1
+    )
+
+
+def column_to_row(column, eye):
+    return jnp.sum(jnp.where(eye, column, 0.0), axis=0, keepdims=True)
+
+
+def row_to_column(row, eye):
+    return jnp.sum(jnp.where(eye, row, 0.0), axis=1, keepdims=True)
+
+
+def plane_peer(me, i):
+    z, y, x, k = me
+    other = lax.rem(z * 4 + y * 2 + x + i, 16)
+    return other, (other // 4, (other // 2) % 2, other % 2, k)
+
+
+def plane_greet_all(me, others):
+    barrier = pltpu.get_barrier_semaphore()
+
+    def call(i, carry):
+        pl.semaphore_signal(barrier, inc=1, device_id=plane_peer(me, i)[1], device_id_type=MESH)
+        return carry
+
+    lax.fori_loop(1, 16, call, 0)
+    for other in others:
+        pl.semaphore_signal(barrier, inc=1, device_id=other, device_id_type=MESH)
+    pl.semaphore_wait(barrier, 15 + len(others))
+
+
+def sum_over_plane(me, slots, send, recv):
+    own = me[0] * 4 + me[1] * 2 + me[2]
+
+    def copy(i, slot):
+        return pltpu.make_async_remote_copy(
+            src_ref=slots.at[slot],
+            dst_ref=slots.at[slot],
+            send_sem=send.at[i],
+            recv_sem=recv.at[slot],
+            device_id=plane_peer(me, i)[1],
+            device_id_type=MESH,
+        )
+
+    def begin(i, carry):
+        copy(i, own).start()
+        return carry
+
+    lax.fori_loop(1, 16, begin, 0)
+
+    def landed(i, carry):
+        copy(i, plane_peer(me, i)[0]).wait_recv()
+        return carry
+
+    lax.fori_loop(1, 16, landed, 0)
+
+    def sent(i, carry):
+        copy(i, own).wait_send()
+        return carry
+
+    lax.fori_loop(1, 16, sent, 0)
+    total = slots[0]
+    for i in range(1, 16):
+        total = total + slots[i]
+    return total
+
+
+def attention_forward(
+    query, key, value, tables, bounds, logical, source, out_weight, gains, attn_gain, gu_stage, d_stage
+):
+    tokens, width = query.shape[0], source.shape[1]
+    rows = tokens // 16
+    group = tokens // 4
+    hidden = gu_stage.shape[2] // 8
+    part = width // 8
 
     def body(*refs):
-        if share is None:
-            term_ref, total_ref, buffer, send, recv, local = refs
-        else:
-            term_ref, a_ref, b_ref, total_ref, other_ref, a_out, b_out, buffer, send, recv, local, pair_send, pair_recv = refs
+        (q_in, k_in, v_in, cos_ref, sin_ref, low_ref, high_ref, log_ref, source_ref, wout_ref, gain_ref, attn_ref) = refs[:12]
+        (gu_ref, d_ref) = refs[12:14]
+        (full_ref, own_ref, branch_ref, wgu_ref, wd_ref, qrot_ref, keys_ref, values_ref, o_ref, lse_ref, scale_ref) = refs[14:25]
+        (terms, shard, slots, tot_send, tot_recv, pair_send, pair_recv, local) = refs[25:33]
+        (ffn_send, ffn_recv, share_send, share_recv, ffn_local) = refs[33:38]
+        rest = refs[38:]
         me = z, y, x, k = place()
-        own = z * 4 + y * 2 + x
+        ctx = own_tile(me)
+        sibling = (z, y, x, 1 - k)
         barrier = pltpu.get_barrier_semaphore()
-
-        def device(i):
-            other = lax.rem(own + i, 16)
-            return (other // 4, (other // 2) % 2, other % 2, k)
-
-        def call(i, carry):
-            pl.semaphore_signal(barrier, inc=1, device_id=device(i), device_id_type=MESH)
-            return carry
-
-        lax.fori_loop(1, 16, call, 0)
-        sibling = (z, y, x, 1 - k)
-        if share is not None:
-            pl.semaphore_signal(barrier, inc=1, device_id=sibling, device_id_type=MESH)
-        pl.semaphore_wait(barrier, 15 if share is None else 16)
-
-        def copy(i):
-            return pltpu.make_async_remote_copy(
-                src_ref=term_ref,
-                dst_ref=buffer.at[own],
-                send_sem=send.at[i],
-                recv_sem=recv.at[own],
-                device_id=device(i),
-                device_id_type=MESH,
-            )
-
-        def begin(i, carry):
-            copy(i).start()
-            return carry
-
-        lax.fori_loop(1, 16, begin, 0)
+        plane_greet_all(me, [sibling])
 
         def pair(src, dst, n):
             return pltpu.make_async_remote_copy(
@@ -679,93 +849,195 @@
                 device_id_type=MESH,
             )
 
-        if share is not None:
-            pairs = [pair(a_ref, a_out, 0), pair(b_ref, b_out, 1)]
-            for c in pairs:
-                c.start()
-
-        total_ref[...] = term_ref[...]
-
-        def add(i, carry):
-            other = lax.rem(own + i, 16)
-            pltpu.make_async_remote_copy(
-                src_ref=term_ref,
-                dst_ref=buffer.at[other],
-                send_sem=send.at[0],
-                recv_sem=recv.at[other],
-                device_id=device(i),
-                device_id_type=MESH,
-            ).wait_recv()
-            total_ref[...] += buffer[other]
-            return carry
-
-        lax.fori_loop(1, 16, add, 0)
-        if share is not None:
-            last = pair(total_ref.at[pl.ds(count // 2, count // 2), :], other_ref, 2)
-            last.start()
-            for c in (*pairs, last):
-                c.wait()
-
-        def finish(i, carry):
-            copy(i).wait_send()
-            return carry
-
-        lax.fori_loop(1, 16, finish, 0)
-
-    shape = jax.ShapeDtypeStruct
-    scratch = [pltpu.VMEM((16, count, 128), F32), DMA((16,)), DMA((16,)), DMA]
-    if share is None:
-        return comm_call(
-            body, "plane_totals", number, shape(terms.shape, F32), [VMEM], VMEM, scratch
-        )(terms)
-    return comm_call(
-        body,
-        "plane_totals_keys",
-        number,
-        (
-            shape(terms.shape, F32),
-            shape((count // 2, 128), F32),
-            shape(share[0].shape, share[0].dtype),
-            shape(share[1].shape, share[1].dtype),
-        ),
-        [VMEM, ANY, ANY],
-        (VMEM, VMEM, ANY, ANY),
-        [*scratch, DMA((3,)), DMA((3,))],
-    )(terms, *share)
-
-
-def after_attention(terms, source, gain):
-    tokens, width = terms.shape
-    rows = tokens // 16
-
-    def body(term_ref, source_ref, gain_ref, full_ref, own_ref, branch_ref, shard, local, *scratch):
-        me = place()
-        greet_plane(me)
+        eye = eye_mask()
+        own = z * 4 + y * 2 + x
+        for i in range(8):
+            piece = slice(i * HD, (i + 1) * HD)
+            for side, ref in enumerate((q_in, k_in)):
+                values = ref[piece, :]
+                column = jnp.sum(values * values, axis=1, keepdims=True)
+                slots[own, side * 8 + i : side * 8 + i + 1, :] = column_to_row(column, eye)
+        values_ref[:tokens, :] = v_in[...]
+        other_half = pl.ds(tokens, tokens)
+        v_copy = pair(v_in, values_ref.at[other_half, :], 0)
+        v_copy.start()
+
+        def ffn_copy(t):
+            to = ctx + t - 8 * ((ctx + t) // 8)
+            device = (to // 2, to % 2, x, k)
+            at = pl.ds(pl.multiple_of(to * hidden, hidden), hidden)
+            from_at = pl.ds(pl.multiple_of(ctx * part, part), part)
+            ends = (
+                (gu_ref.at[:, :, at], wgu_ref.at[:, from_at, :hidden]),
+                (d_ref.at[at, :], wd_ref.at[:hidden, from_at]),
+            )
+            return [
+                pltpu.make_async_remote_copy(
+                    src_ref=src,
+                    dst_ref=dst,
+                    send_sem=ffn_send.at[i, t],
+                    recv_sem=ffn_recv.at[i, t],
+                    device_id=device,
+                    device_id_type=MESH,
+                )
+                for i, (src, dst) in enumerate(ends)
+            ]
+
+        def ffn_ends(c):
+            at = pl.ds(pl.multiple_of(c * part, part), part)
+            return (
+                (wgu_ref.at[:, at, :hidden], wgu_ref.at[:, at, hidden:]),
+                (wd_ref.at[:hidden, at], wd_ref.at[hidden:, at]),
+            )
+
+        own_at = pl.ds(pl.multiple_of(ctx * hidden, hidden), hidden)
+        ffn_own = [
+            pltpu.make_async_copy(src, dst[0], ffn_local.at[i])
+            for i, (src, dst) in enumerate(
+                zip((gu_ref.at[:, :, own_at], d_ref.at[own_at, :]), ffn_ends(ctx), strict=True)
+            )
+        ]
+        for copy in ffn_own:
+            copy.start()
+
+        total = sum_over_plane(me, slots, tot_send, tot_recv)
+        for t in range(1, 8):
+            for copy in ffn_copy(t):
+                copy.start()
+        scales = lax.rsqrt(total / width + EPSILON)
+        scale_ref[...] = scales
+
+        def rotated(values, piece):
+            return values * cos_ref[piece, :] + pltpu.roll(values, HD // 2, 1) * sin_ref[piece, :]
+
+        for i in range(8):
+            piece = slice(i * HD, (i + 1) * HD)
+            factor = row_to_column(scales[8 + i : 9 + i, :], eye)
+            keys_ref[piece, :] = rotated(k_in[piece, :] * factor * gain_ref[1:2, :], piece).astype(BF)
+        k_copy = pair(keys_ref.at[:tokens, :], keys_ref.at[other_half, :], 1)
+        k_copy.start()
+        for i in range(8):
+            piece = slice(i * HD, (i + 1) * HD)
+            factor = row_to_column(scales[i : i + 1, :], eye)
+            qrot_ref[piece, :] = rotated(q_in[piece, :] * factor * gain_ref[0:1, :], piece).astype(BF)
+        v_copy.wait()
+        k_copy.wait()
+
+        def produce(zp):
+            at = pl.ds(pl.multiple_of(zp * group, group), group)
+            raw, allowed = masked_scores(
+                qrot_ref[at, :], keys_ref[...], low_ref[at, :], high_ref[at, :], log_ref[...]
+            )
+            raw = jnp.where(allowed, raw, MASKED)
+            top = jnp.max(raw, axis=1, keepdims=True)
+            weights = jnp.where(allowed, jnp.exp(raw - top), 0.0)
+            total_weight = jnp.sum(weights, axis=1, keepdims=True)
+            weights = (weights / total_weight).astype(BF)
+            out = jnp.dot(weights, values_ref[...], preferred_element_type=F32)
+            o_ref[at, :] = out
+            lse_ref[at, :] = top + jnp.log(total_weight)
+            terms[at, :] = jnp.dot(
+                out.astype(BF), wout_ref[...], preferred_element_type=F32
+            ).astype(BF)
 
         def finish(strip, total):
             branch_ref[strip] = total
-            h = source_ref[strip].astype(F32) + total * row_scale(total) * gain_ref[...]
+            h = source_ref[strip].astype(F32) + total * row_scale(total) * attn_ref[...]
             own_ref[strip] = h
             shard[strip] = h.astype(BF)
 
-        settle = reduce_plane(me, gather_view(term_ref, rows), rows, scratch[:15], finish)
+        settle = reduce_plane(me, terms, rows, rest[:N_REDUCE], produce, finish)
         view = gather_view(full_ref, rows)
-        keep = pltpu.make_async_copy(shard, view(me[0] * 4 + me[1] * 2 + me[2]), local)
+        keep = pltpu.make_async_copy(shard, view(own), local)
         keep.start()
-        gather_plane(me, shard, view, scratch[15:])
+
+        def share(t):
+            c = ctx + 8 - t - 8 * ((ctx + 8 - t) // 8)
+            return [
+                pltpu.make_async_remote_copy(
+                    src_ref=src,
+                    dst_ref=dst,
+                    send_sem=share_send.at[i, t],
+                    recv_sem=share_recv.at[i, t],
+                    device_id=sibling,
+                    device_id_type=MESH,
+                )
+                for i, (src, dst) in enumerate(ffn_ends(c))
+            ]
+
+        def ffn_landed(t):
+            c = ctx + 8 - t - 8 * ((ctx + 8 - t) // 8)
+            for i, ends in enumerate(ffn_ends(c)):
+                pltpu.make_async_remote_copy(
+                    src_ref=ends[0],
+                    dst_ref=ends[0],
+                    send_sem=ffn_send.at[i, t],
+                    recv_sem=ffn_recv.at[i, t],
+                    device_id=sibling,
+                    device_id_type=MESH,
+                ).wait_recv()
+
+        def between(step):
+            for t in (2 * step, 2 * step + 1):
+                if t == 0:
+                    for copy in ffn_own:
+                        copy.wait()
+                elif t < 8:
+                    ffn_landed(t)
+                if t < 8:
+                    for copy in share(t):
+                        copy.start()
+
+        gather_plane(me, shard, view, rest[N_REDUCE:])
+        for step in range(4):
+            between(step)
         keep.wait()
         settle()
+        for t in range(8):
+            for copy in share(t):
+                copy.wait()
+            if t > 0:
+                for copy in ffn_copy(t):
+                    copy.wait_send()
 
     shape = jax.ShapeDtypeStruct
     return comm_call(
         body,
-        "after_attention",
-        2,
-        (shape((tokens, width), BF), shape((rows, width), F32), shape((rows, width), F32)),
-        [ANY, VMEM, VMEM],
-        (ANY, VMEM, VMEM),
-        [pltpu.VMEM((rows, width), BF), DMA, *reduce_scratch(rows, width), *GATHER_SEMS],
-    )(terms, source, gain)
+        "attention_forward",
+        1,
+        (
+            shape((tokens, width), BF),
+            shape((rows, width), F32),
+            shape((rows, width), F32),
+            shape((2, width, 2 * hidden), BF),
+            shape((2 * hidden, width), BF),
+            shape((tokens, HD), BF),
+            shape((2 * tokens, HD), BF),
+            shape((2 * tokens, HD), BF),
+            shape((tokens, HD), F32),
+            shape((tokens, 1), F32),
+            shape((16, HD), F32),
+        ),
+        [VMEM] * 12 + [ANY, ANY],
+        (ANY, VMEM, VMEM, ANY, ANY, VMEM, VMEM, VMEM, VMEM, VMEM, VMEM),
+        [
+            pltpu.VMEM((tokens, width), BF),
+            pltpu.VMEM((rows, width), BF),
+            pltpu.VMEM((16, 16, HD), F32),
+            DMA((16,)),
+            DMA((16,)),
+            DMA((2,)),
+            DMA((2,)),
+            DMA,
+            DMA((2, 8)),
+            DMA((2, 8)),
+            DMA((2, 8)),
+            DMA((2, 8)),
+            DMA((2,)),
+            *reduce_scratch(rows, width),
+            *GATHER_SEMS,
+        ],
+    )(query, key, value, *tables, *bounds, logical, source, out_weight, gains, attn_gain, gu_stage, d_stage)
 
 
 def after_ffn(terms, residual, cotangent, gain):
@@ -785,7 +1057,7 @@
             gg_ref[...] += term
             shard[strip] = back.astype(BF)
 
-        settle = reduce_plane(me, gather_view(term_ref, rows), rows, scratch[:15], finish)
+        settle = reduce_plane(me, term_ref, rows, scratch[:N_REDUCE], lambda zp: None, finish)
         view = gather_view(full_ref, rows)
         keep = pltpu.make_async_copy(shard, view(me[0] * 4 + me[1] * 2 + me[2]), local)
         keep.start()
@@ -793,7 +1065,7 @@
         for copy in copies:
             copy.start()
         own.start()
-        gather_plane(me, shard, view, scratch[15:])
+        gather_plane(me, shard, view, scratch[N_REDUCE:])
         keep.wait()
         settle()
         own.wait()
@@ -806,7 +1078,7 @@
         "after_ffn",
         3,
         (shape((tokens, width), BF), shape((rows * 4, width // 4), BF), shape((8, width), F32)),
-        [ANY, VMEM, VMEM, VMEM],
+        [VMEM, VMEM, VMEM, VMEM],
         (ANY, ANY, VMEM),
         [
             pltpu.VMEM((rows, width), BF),
@@ -836,11 +1108,11 @@
             gg_ref[...] += term
             shard[strip] = back.astype(BF)
 
-        settle = reduce_plane(me, gather_view(term_ref, rows), rows, scratch[:15], finish)
+        settle = reduce_plane(me, term_ref, rows, scratch[:N_REDUCE], lambda zp: None, finish)
         view = gather_view(full_ref, rows)
         keep = pltpu.make_async_copy(shard, view(me[0] * 4 + me[1] * 2 + me[2]), local)
         keep.start()
-        gather_plane(me, shard, view, scratch[15:])
+        gather_plane(me, shard, view, scratch[N_REDUCE:])
         keep.wait()
         settle()
 
@@ -850,56 +1122,333 @@
         "after_ffn_back",
         4,
         (shape((tokens, width), BF), shape((rows, width), F32), shape((8, width), F32)),
-        [ANY, VMEM, VMEM, VMEM],
+        [VMEM, VMEM, VMEM, VMEM],
         (ANY, VMEM, VMEM),
         [pltpu.VMEM((rows, width), BF), DMA, *reduce_scratch(rows, width), *GATHER_SEMS],
     )(terms, cotangent, branch, gain)
 
 
-def close_layer(terms, grad, blob):
-    tokens, width = terms.shape
-    rows = tokens // 16
-
-    def body(term_ref, grad_ref, blob_ref, out_ref, back_ref, result, out_send, out_recv, deal_send, deal_recv, *scratch):
+def close_greet(me):
+    z, y, x, k = me
+    barrier = pltpu.get_barrier_semaphore()
+
+    def plane(i, carry):
+        pl.semaphore_signal(barrier, inc=1, device_id=plane_peer(me, i)[1], device_id_type=MESH)
+        return carry
+
+    def others(i, carry):
+        pl.semaphore_signal(
+            barrier, inc=1, device_id=(i // 2, i % 2, x, 1 - k), device_id_type=MESH
+        )
+        return carry
+
+    lax.fori_loop(1, 16, plane, 0)
+    lax.fori_loop(0, 8, others, 0)
+    pl.semaphore_signal(barrier, inc=1, device_id=(z, y, 1 - x, 1 - k), device_id_type=MESH)
+    pl.semaphore_wait(barrier, 24)
+
+
+def attention_backward(
+    grad_attn,
+    full_in,
+    query,
+    key,
+    query_rot,
+    keys,
+    values,
+    attended,
+    lse,
+    tables,
+    bounds,
+    logical,
+    scales,
+    head_gains,
+    qkv_w,
+    out_w,
+    grad_own,
+    attn_term,
+    ffn_term,
+):
+    tokens, width = grad_attn.shape
+    rows, group = tokens // 16, tokens // 4
+    part = width // 4
+    scaling = 1.0 / math.sqrt(HD)
+
+    def body(*refs):
+        (da_any, x_any) = refs[:2]
+        (q_ref, k_ref, qrot_ref, keys_ref, values_ref, o_ref, lse_ref, cos_ref, sin_ref) = refs[2:11]
+        (low_ref, high_ref, log_ref, scale_ref, gain_ref, wqkv_ref, wout_ref) = refs[11:18]
+        (grad_ref, attn_ref, ffn_ref) = refs[18:21]
+        (in_grad_ref, gq_ref, gk_ref, gv_ref, gout_ref, gains_ref) = refs[21:27]
+        (da, xs, terms, do_ref, delta_ref, dq_ref, dk_ref, dv_ref) = refs[27:35]
+        (pair_out, pair_in, dqkv, slots, result) = refs[35:40]
+        (wall_grad, wall_out, wall_in, deal_out, deal_in) = refs[40:45]
+        (gain_out, gain_in, gain_own, gain_slots) = refs[45:49]
+        (load_sem, pair_send, pair_recv, tot_send, tot_recv, out_send, out_recv) = refs[49:56]
+        (deal_send, deal_recv, gain_send, gain_recv) = refs[56:60]
+        scratch = refs[60:]
         me = z, y, x, k = place()
-        same_x_greet(me)
-        head = z // 2
+        ctx = own_tile(me)
+        own = ctx * 2 + x
+        sibling = (z, y, x, 1 - k)
+
+        da_loads = [
+            pltpu.make_async_copy(
+                da_any.at[g * group : (g + 1) * group, :],
+                da.at[g * group : (g + 1) * group, :],
+                load_sem.at[g],
+            )
+            for g in range(4)
+        ]
+        x_load = pltpu.make_async_copy(x_any, xs, load_sem.at[4])
+        for load in (*da_loads, x_load):
+            load.start()
+        close_greet(me)
+
+        def pair(n):
+            return pltpu.make_async_remote_copy(
+                src_ref=(pair_out.at[0], pair_out.at[1], wall_out, gain_out)[n],
+                dst_ref=(pair_in.at[0], pair_in.at[1], wall_in, gain_in)[n],
+                send_sem=pair_send.at[n],
+                recv_sem=pair_recv.at[n],
+                device_id=sibling,
+                device_id_type=MESH,
+            )
+
+        for g in range(4):
+            at = slice(g * group, (g + 1) * group)
+            da_loads[g].wait()
+            do = lax.dot_general(
+                da[at, :], wout_ref[...], (((1,), (1,)), ((), ())), preferred_element_type=F32
+            ).astype(BF)
+            do_ref[at, :] = do
+            delta_ref[at, :] = jnp.sum(do.astype(F32) * o_ref[at, :], axis=1, keepdims=True)
+
+        across = (((0,), (0,)), ((), ()))
+        for half in (1, 0):
+            key_at = slice(half * tokens, (half + 1) * tokens)
+            dk_ref[...] = jnp.zeros_like(dk_ref)
+            dv_ref[...] = jnp.zeros_like(dv_ref)
+
+            def work(at, half=half, key_at=key_at):
+                q, g, key_part = qrot_ref[at, :], do_ref[at, :], keys_ref[key_at, :]
+                raw, allowed = masked_scores(
+                    q, key_part, low_ref[at, :], high_ref[at, :], log_ref[:, key_at]
+                )
+                weights = jnp.where(allowed, jnp.exp(raw - lse_ref[at, :]), 0.0)
+                dp = lax.dot_general(
+                    g, values_ref[key_at, :], (((1,), (1,)), ((), ())), preferred_element_type=F32
+                )
+                ds = (weights * (dp - delta_ref[at, :])).astype(BF)
+                dq = jnp.dot(ds, key_part, preferred_element_type=F32) * scaling
+                if half == 1:
+                    dq_ref[at, :] = dq
+                else:
+                    dq_ref[at, :] += dq
+                dk_ref[...] += (
+                    lax.dot_general(ds, q, across, preferred_element_type=F32) * scaling
+                )
+                dv_ref[...] += lax.dot_general(
+                    weights.astype(BF), g, across, preferred_element_type=F32
+                )
+
+            strips(tokens, work, group)
+            if half == 1:
+                pair_out[0] = dk_ref[...].astype(BF)
+                pair_out[1] = dv_ref[...].astype(BF)
+                pair(0).start()
+                pair(1).start()
+
+        eye = eye_mask()
+
+        def normed_grad(values, piece):
+            return values * cos_ref[piece, :] - pltpu.roll(values, HD // 2, 1) * sin_ref[piece, :]
+
+        def side_dots(side, source, grads, proj):
+            gain_sum = jnp.zeros((8, HD), F32)
+            for i in range(8):
+                piece = slice(i * HD, (i + 1) * HD)
+                factor = row_to_column(scale_ref[side * 8 + i : side * 8 + i + 1, :], eye)
+                back = normed_grad(source(piece), piece)
+                term = back * proj[piece, :] * factor
+                for j in range(0, HD, 8):
+                    gain_sum = gain_sum + term[j : j + 8, :]
+                weighted = back * gain_ref[side : side + 1, :]
+                grads[piece, :] = weighted
+                dot = jnp.sum(weighted * proj[piece, :], axis=1, keepdims=True)
+                slots[own, side * 8 + i : side * 8 + i + 1, :] = column_to_row(dot, eye)
+            return jnp.sum(gain_sum, axis=0, keepdims=True)
+
+        query_gain = side_dots(0, lambda piece: dq_ref[piece, :], dq_ref, q_ref)
+        pair(0).wait_recv()
+        pair(1).wait_recv()
+        key_gain = side_dots(
+            1, lambda piece: dk_ref[piece, :] + pair_in[0, piece, :].astype(F32), dk_ref, k_ref
+        )
+        dqkv[:, 2 * HD :] = (dv_ref[...] + pair_in[1].astype(F32)).astype(BF)
+
+        attn_sum = jnp.sum(attn_ref[...], axis=0, keepdims=True)
+        ffn_sum = jnp.sum(ffn_ref[...], axis=0, keepdims=True)
+        head_core = z // 2
+        head_at = pl.ds(pl.multiple_of(((z % 2) * 2 + y) * HD, HD), HD)
+        for mine, target in ((True, gain_own), (False, gain_out)):
+            target[...] = jnp.zeros_like(target)
+            for xt in range(2):
+                for kt in range(2):
+
+                    @pl.when((kt == k) if mine else (kt != k))
+                    def _(xt=xt, kt=kt, target=target):
+                        block = slice((2 * xt + kt) * part, (2 * xt + kt + 1) * part)
+                        target[xt, 2:3, :] = attn_sum[:, block]
+                        target[xt, 3:4, :] = ffn_sum[:, block]
+
+            @pl.when((head_core == k) if mine else (head_core != k))
+            def _(target=target):
+                target[x, 0:1, head_at] = query_gain
+                target[x, 1:2, head_at] = key_gain
+
+        pair(3).start()
+
+        total = sum_over_plane(me, slots, tot_send, tot_recv)
+        for side, grads, proj in ((0, dq_ref, q_ref), (1, dk_ref, k_ref)):
+            for i in range(8):
+                piece = slice(i * HD, (i + 1) * HD)
+                row = scale_ref[side * 8 + i : side * 8 + i + 1, :]
+                factor = row_to_column(row, eye)
+                cubed = row * row * row * total[side * 8 + i : side * 8 + i + 1, :] / width
+                dqkv[piece, side * HD : (side + 1) * HD] = (
+                    factor * grads[piece, :] - proj[piece, :] * row_to_column(cubed, eye)
+                ).astype(BF)
+
+        def produce(zp):
+            at = pl.ds(pl.multiple_of(zp * group, group), group)
+            term = jnp.zeros((group, width), F32)
+            for i in range(3):
+                term = term + lax.dot_general(
+                    dqkv[at, i * HD : (i + 1) * HD],
+                    wqkv_ref[i],
+                    (((1,), (1,)), ((), ())),
+                    preferred_element_type=F32,
+                )
+            terms[at, :] = term.astype(BF)
+
+        gain_copies = []
+
+        def gain_copy(i):
+            other, device = plane_peer(me, i)
+            return pltpu.make_async_remote_copy(
+                src_ref=gain_own.at[other % 2],
+                dst_ref=gain_slots.at[own],
+                send_sem=gain_send.at[i],
+                recv_sem=gain_recv.at[own],
+                device_id=device,
+                device_id_type=MESH,
+            )
+
         number = ((z % 2) * 2 + y) * 2 + k
 
         def deal(c):
             return pltpu.make_async_remote_copy(
-                src_ref=blob_ref.at[c],
-                dst_ref=back_ref.at[number],
+                src_ref=deal_out.at[c],
+                dst_ref=deal_in.at[number],
                 send_sem=deal_send.at[c],
                 recv_sem=deal_recv.at[number],
-                device_id=(c // 2, c % 2, x, head),
+                device_id=(c // 2, c % 2, x, head_core),
                 device_id_type=MESH,
             )
 
-        stays = k == z // 2
-        ctx = own_tile(me)
-        for c in range(8):
-
-            @pl.when(jnp.logical_not(stays & (ctx == c)))
-            def _(c=c):
-                deal(c).start()
-
-            @pl.when(stays & (ctx == c))
-            def _(c=c):
-                pltpu.make_async_copy(
-                    blob_ref.at[c], back_ref.at[number], deal_recv.at[number]
-                ).start()
+        stays = k == head_core
+
+        def after_terms():
+            pair(3).wait_recv()
+            gain_own[...] += gain_in[...]
+            gain_slots[own] = gain_own[x]
+
+            def begin(i, carry):
+                gain_copy(i).start()
+                return carry
+
+            lax.fori_loop(1, 16, begin, 0)
+            x_load.wait()
+            for c in range(8):
+                grads = lax.dot_general(
+                    xs[:, c * 2 * HD : (c + 1) * 2 * HD],
+                    dqkv[...],
+                    across,
+                    preferred_element_type=F32,
+                )
+                for i in range(3):
+                    for r in range(2):
+                        wall_grad[r, c, i] = grads[r * HD : (r + 1) * HD, i * HD : (i + 1) * HD]
+                out_grad = lax.dot_general(
+                    o_ref[...].astype(BF),
+                    da[:, c * 2 * HD : (c + 1) * 2 * HD],
+                    across,
+                    preferred_element_type=F32,
+                )
+                for r in range(2):
+                    wall_grad[r, c, 3] = out_grad[:, r * HD : (r + 1) * HD]
+
+            def to_other(c, carry):
+                wall_out[c] = wall_grad[1 - k, c].astype(BF)
+                return carry
+
+            lax.fori_loop(0, 8, to_other, 0)
+            pair(2).start()
+            pair(2).wait_recv()
+
+            def to_owner(c, carry):
+                deal_out[c] = (wall_grad[k, c] + wall_in[c].astype(F32)).astype(BF)
+                return carry
+
+            lax.fori_loop(0, 8, to_owner, 0)
+            for c in range(8):
+
+                @pl.when(jnp.logical_not(stays & (ctx == c)))
+                def _(c=c):
+                    deal(c).start()
+
+                @pl.when(stays & (ctx == c))
+                def _(c=c):
+                    pltpu.make_async_copy(
+                        deal_out.at[c], deal_in.at[number], deal_recv.at[number]
+                    ).start()
 
         def finish(strip, total):
             result[strip] = (grad_ref[strip] + total).astype(BF)
 
-        settle = reduce_plane(me, gather_view(term_ref, rows), rows, scratch, finish)
-        copies, own = hand_out_copies(me, result, out_ref, out_send, out_recv)
+        settle = reduce_plane(me, terms, rows, scratch, produce, finish, after_terms)
+        copies, own_copy = hand_out_copies(me, result, in_grad_ref, out_send, out_recv)
         for copy in copies:
             copy.start()
-        own.start()
+        own_copy.start()
+        for n in range(8):
+            pltpu.make_async_copy(deal_out.at[n], deal_in.at[n], deal_recv.at[n]).wait()
+            j, r = n // 2, n % 2
+            for i, ref in enumerate((gq_ref, gk_ref, gv_ref)):
+                ref[r * HD : (r + 1) * HD, j * HD : (j + 1) * HD] = deal_in[n, i].astype(F32)
+            gout_ref[j * HD : (j + 1) * HD, r * HD : (r + 1) * HD] = deal_in[n, 3].astype(F32)
+
+        def gain_landed(i, carry):
+            other, device = plane_peer(me, i)
+            pltpu.make_async_remote_copy(
+                src_ref=gain_slots.at[other],
+                dst_ref=gain_slots.at[other],
+                send_sem=gain_send.at[i],
+                recv_sem=gain_recv.at[other],
+                device_id=device,
+                device_id_type=MESH,
+            ).wait_recv()
+            gain_copy(i).wait_send()
+            return carry
+
+        lax.fori_loop(1, 16, gain_landed, 0)
+        gain_total = gain_slots[0]
+        for i in range(1, 16):
+            gain_total = gain_total + gain_slots[i]
+        gains_ref[...] = gain_total
         settle()
-        own.wait()
+        own_copy.wait()
         for copy in copies:
             copy.wait()
         for c in range(8):
@@ -908,118 +1457,92 @@
             def _(c=c):
                 deal(c).wait_send()
 
-            pltpu.make_async_copy(blob_ref.at[c], back_ref.at[c], deal_recv.at[c]).wait()
+        for n in range(4):
+            pair(n).wait_send()
 
     shape = jax.ShapeDtypeStruct
+    vmem = pltpu.VMEM
     return comm_call(
         body,
-        "close_layer",
+        "attention_backward",
         5,
-        (shape((rows * 4, width // 4), BF), shape(blob.shape, BF)),
-        [ANY, VMEM, ANY],
-        (ANY, ANY),
+        (
+            shape((rows * 4, part), BF),
+            shape((rows * 4, part), F32),
+            shape((rows * 4, part), F32),
+            shape((rows * 4, part), F32),
+            shape((part, rows * 4), F32),
+            shape((4, part), F32),
+        ),
+        [ANY, ANY, *[VMEM] * 19],
+        (ANY, VMEM, VMEM, VMEM, VMEM, VMEM),
         [
-            pltpu.VMEM((rows, width), BF),
+            vmem((tokens, width), BF),
+            vmem((tokens, width), BF),
+            vmem((tokens, width), BF),
+            vmem((tokens, HD), BF),
+            vmem((tokens, 1), F32),
+            vmem((tokens, HD), F32),
+            vmem((tokens, HD), F32),
+            vmem((tokens, HD), F32),
+            vmem((2, tokens, HD), BF),
+            vmem((2, tokens, HD), BF),
+            vmem((tokens, 3 * HD), BF),
+            vmem((16, 16, HD), F32),
+            vmem((rows, width), BF),
+            vmem((2, 8, 4, HD, HD), F32),
+            vmem((8, 4, HD, HD), BF),
+            vmem((8, 4, HD, HD), BF),
+            vmem((8, 4, HD, HD), BF),
+            vmem((8, 4, HD, HD), BF),
+            vmem((2, 4, part), F32),
+            vmem((2, 4, part), F32),
+            vmem((2, 4, part), F32),
+            vmem((16, 4, part), F32),
+            DMA((5,)),
+            DMA((4,)),
+            DMA((4,)),
+            DMA((16,)),
+            DMA((16,)),
             DMA((3,)),
             DMA((4,)),
             DMA((8,)),
             DMA((8,)),
+            DMA((16,)),
+            DMA((16,)),
             *reduce_scratch(rows, width),
         ],
-    )(terms, grad, blob)
-
-
-QUERY_ROWS = 256
-
-
-def masked_scores(q, keys, low, high, logical):
-    raw = lax.dot_general(q, keys, (((1,), (1,)), ((), ())), preferred_element_type=F32)
-    allowed = (logical >= low) & (logical <= high)
-    return raw * (1.0 / math.sqrt(HD)), allowed
-
-
-def attend(query, keys, values, low, high, logical):
-    tokens, total = query.shape[0], keys.shape[0]
-
-    def body(q_ref, k_ref, v_ref, low_ref, high_ref, log_ref, out_ref, lse_ref):
-        raw, allowed = masked_scores(q_ref[...], k_ref[...], low_ref[...], high_ref[...], log_ref[...])
-        raw = jnp.where(allowed, raw, MASKED)
-        top = jnp.max(raw, axis=1, keepdims=True)
-        weights = jnp.where(allowed, jnp.exp(raw - top), 0.0)
-        total_weight = jnp.sum(weights, axis=1, keepdims=True)
-        weights = (weights / total_weight).astype(BF)
-        out_ref[...] = jnp.dot(weights, v_ref[...], preferred_element_type=F32)
-        lse_ref[...] = top + jnp.log(total_weight)
-
-    row = pl.BlockSpec((QUERY_ROWS, HD), lambda i: (i, 0))
-    single = pl.BlockSpec((QUERY_ROWS, 1), lambda i: (i, 0))
-    whole = pl.BlockSpec((total, HD), lambda i: (0, 0))
-    line = pl.BlockSpec((1, total), lambda i: (0, 0))
-    return pl.pallas_call(
-        body,
-        name="attend",
-        grid=(tokens // QUERY_ROWS,),
-        out_shape=(
-            jax.ShapeDtypeStruct((tokens, HD), F32),
-            jax.ShapeDtypeStruct((tokens, 1), F32),
-        ),
-        in_specs=[row, whole, whole, single, single, line],
-        out_specs=(row, single),
-        compiler_params=pltpu.CompilerParams(vmem_limit_bytes=BIG_VMEM),
-    )(query, keys, values, low, high, logical)
-
-
-def attend_back(query, keys, values, low, high, logical, lse, grad, delta):
-    tokens, total = query.shape[0], keys.shape[0]
-
-    def body(q_ref, k_ref, v_ref, low_ref, high_ref, log_ref, lse_ref, g_ref, d_ref, dq_ref, dk_ref, dv_ref):
-        @pl.when(pl.program_id(0) == 0)
-        def _():
-            dk_ref[...] = jnp.zeros_like(dk_ref)
-            dv_ref[...] = jnp.zeros_like(dv_ref)
-
-        q, keys_all, g = q_ref[...], k_ref[...], g_ref[...]
-        raw, allowed = masked_scores(q, keys_all, low_ref[...], high_ref[...], log_ref[...])
-        weights = jnp.where(allowed, jnp.exp(raw - lse_ref[...]), 0.0)
-        dp = lax.dot_general(g, v_ref[...], (((1,), (1,)), ((), ())), preferred_element_type=F32)
-        ds = (weights * (dp - d_ref[...])).astype(BF)
-        scaling = 1.0 / math.sqrt(HD)
-        dq_ref[...] = jnp.dot(ds, keys_all, preferred_element_type=F32) * scaling
-        across = (((0,), (0,)), ((), ()))
-        dk_ref[...] += lax.dot_general(ds, q, across, preferred_element_type=F32) * scaling
-        dv_ref[...] += lax.dot_general(weights.astype(BF), g, across, preferred_element_type=F32)
-
-    row = pl.BlockSpec((QUERY_ROWS, HD), lambda i: (i, 0))
-    single = pl.BlockSpec((QUERY_ROWS, 1), lambda i: (i, 0))
-    whole = pl.BlockSpec((total, HD), lambda i: (0, 0))
-    line = pl.BlockSpec((1, total), lambda i: (0, 0))
-    return pl.pallas_call(
-        body,
-        name="attend_back",
-        grid=(tokens // QUERY_ROWS,),
-        out_shape=(
-            jax.ShapeDtypeStruct((tokens, HD), F32),
-            jax.ShapeDtypeStruct((total, HD), F32),
-            jax.ShapeDtypeStruct((total, HD), F32),
-        ),
-        in_specs=[row, whole, whole, single, single, line, single, row, single],
-        out_specs=(row, whole, whole),
-        compiler_params=pltpu.CompilerParams(vmem_limit_bytes=BIG_VMEM),
-    )(query, keys, values, low, high, logical, lse, grad, delta)
+    )(
+        grad_attn,
+        full_in,
+        query,
+        key,
+        query_rot,
+        keys,
+        values,
+        attended,
+        lse,
+        *tables,
+        *bounds,
+        logical,
+        scales,
+        head_gains,
+        qkv_w,
+        out_w,
+        grad_own,
+        attn_term,
+        ffn_term,
+    )
 
 
 def rotary_tables(offset):
     half_dim = HD // 2
     inverse = jnp.power(ROPE_THETA, -jnp.arange(half_dim, dtype=F32) * 2.0 / HD)
     angles = offset.astype(F32)[:, None] * inverse[None, :]
-    return jnp.cos(angles), jnp.sin(angles)
-
-
-def turn(values, tables, sign):
-    cosine, sine_part = tables
-    first, second = values[:, : HD // 2], sign * values[:, HD // 2 :]
-    return jnp.concatenate(
-        [first * cosine - second * sine_part, (second * cosine + first * sine_part) * sign], axis=1
+    cosine, sine_part = jnp.cos(angles), jnp.sin(angles)
+    return (
+        jnp.concatenate([cosine, cosine], axis=1),
+        jnp.concatenate([-sine_part, sine_part], axis=1),
     )
 
 
@@ -1066,81 +1589,46 @@
 
     logical_own, logical_other = logical_of(k), logical_of(1 - k)
     offset_own = sequence_tables(logical_own, lengths)[1]
-    offset_other = sequence_tables(logical_other, lengths)[1]
-    tables_own, tables_other = rotary_tables(offset_own), rotary_tables(offset_other)
+    tables = rotary_tables(offset_own)
     low = (logical_own - offset_own)[:, None]
     high = logical_own[:, None]
     logical_keys = jnp.concatenate([logical_own, logical_other])[None, :]
 
-    def columns(weight):
-        return jnp.transpose(weight.astype(BF).reshape(2, HD, 4, HD), (2, 0, 1, 3))
-
-    out_part = jnp.transpose(w_out.astype(BF).reshape(4, HD, 2, HD), (0, 2, 1, 3))
-    blob = jnp.stack([columns(w_query), columns(w_key), columns(w_value), out_part], axis=2)
     gains = jnp.stack([query_gain, key_gain, attn_gain, ffn_gain])
-    full_in, own_cot, wall, gains_full = open_layer(
-        inputs, cotangent, blob.reshape(8, 4, HD, HD), gains
+    full_in, source_own, own_cot, qkv_w, out_w, gains_full, gu_stage, d_stage, query_proj, key_proj, value_low = open_layer(
+        inputs, cotangent, w_query, w_key, w_value, w_out, w_gate, w_up, w_down, gains
     )
     head = x * 8 + ctx
     attn_gain_row, ffn_gain_row = gains_full[2:3], gains_full[3:4]
-    query_gain_row = lax.dynamic_slice_in_dim(gains_full[0], head * HD, HD)[None, :]
-    key_gain_row = lax.dynamic_slice_in_dim(gains_full[1], head * HD, HD)[None, :]
-
-    def ffn_columns(weight):
-        return jnp.transpose(weight.astype(BF).reshape(-1, 8, hidden), (1, 0, 2))
-
-    ffn_blob = jnp.stack(
-        [
-            ffn_columns(w_gate),
-            ffn_columns(w_up),
-            w_down.astype(BF).reshape(8, hidden, -1),
-        ],
-        axis=1,
-    )
-    ffn_mine = lax.all_to_all(ffn_blob, CTX, split_axis=0, concat_axis=0, tiled=True)
-    ffn_other = swap_cores(ffn_mine)
-
-    def up_like(i):
-        return jnp.concatenate(
-            [ffn_mine[:, i].reshape(D, hidden), ffn_other[:, i].reshape(D, hidden)], axis=1
-        )
-
-    gate_w, up_w = up_like(0), up_like(1)
-    down_w = jnp.concatenate(
-        [
-            jnp.transpose(ffn_mine[:, 2], (1, 0, 2)).reshape(hidden, D),
-            jnp.transpose(ffn_other[:, 2], (1, 0, 2)).reshape(hidden, D),
-        ],
-        axis=0,
-    )
-
-    qkv_w = wall[:3].reshape(3, D, HD)
-    out_w = jnp.transpose(wall[3].reshape(16, HD, HD), (1, 0, 2)).reshape(HD, D)
+    head_gains = lax.dynamic_slice_in_dim(gains_full[:2], head * HD, HD, 1)
+    (
+        residual_full,
+        residual_own,
+        branch_own,
+        gu_w,
+        down_w,
+        query_rot,
+        keys_all,
+        values_all,
+        attended,
+        lse,
+        scales,
+    ) = attention_forward(
+        query_proj,
+        key_proj,
+        value_low,
+        tables,
+        (low, high),
+        logical_keys,
+        source_own,
+        out_w,
+        head_gains,
+        attn_gain_row,
+        gu_stage,
+        d_stage,
+    )
+    gate_w, up_w = gu_w[0], gu_w[1]
     rows_dims = ((1,), (0,))
-    query_proj = dotf(full_in, qkv_w[0], rows_dims)
-    key_proj = dotf(full_in, qkv_w[1], rows_dims)
-    value_low = dotf(full_in, qkv_w[2], rows_dims).astype(BF)
-    squares = jnp.concatenate(
-        [jnp.sum(query_proj * query_proj, axis=1), jnp.sum(key_proj * key_proj, axis=1)]
-    ).reshape(-1, 128)
-    totals, key_total_other, key_other, value_other = plane_totals(
-        squares, 1, (key_proj, value_low)
-    )
-    totals = totals.reshape(2, tokens)
-    query_scale = lax.rsqrt(totals[0] / D + EPSILON)[:, None]
-    key_scale = lax.rsqrt(totals[1] / D + EPSILON)[:, None]
-    key_scale_other = lax.rsqrt(key_total_other.reshape(tokens) / D + EPSILON)[:, None]
-    query_rot = turn(query_proj * query_scale * query_gain_row, tables_own, 1.0).astype(BF)
-    key_rot = turn(key_proj * key_scale * key_gain_row, tables_own, 1.0).astype(BF)
-    key_rot_other = turn(key_other * key_scale_other * key_gain_row, tables_other, 1.0).astype(BF)
-    keys_all = jnp.concatenate([key_rot, key_rot_other], axis=0)
-    values_all = jnp.concatenate([value_low, value_other], axis=0)
-    attended, lse = attend(query_rot, keys_all, values_all, low, high, logical_keys)
-    attended_low = attended.astype(BF)
-    source_own = lax.dynamic_slice_in_dim(full_in, (ctx * 2 + x) * (tokens // 16), tokens // 16)
-    residual_full, residual_own, branch_own = after_attention(
-        dotf(attended_low, out_w, rows_dims).astype(BF), source_own, attn_gain_row
-    )
 
     gate_proj = dotf(residual_full, gate_w, rows_dims)
     up_proj = dotf(residual_full, up_w, rows_dims)
@@ -1184,76 +1672,33 @@
     grad_w_up = jnp.transpose(ffn_back[:, 1], (1, 0, 2)).reshape(w_up.shape)
     grad_w_down = ffn_back[:, 2].reshape(w_down.shape)
 
-    grad_heads = dotf(grad_attn, out_w, turned).astype(BF)
-    delta = jnp.sum(grad_heads.astype(F32) * attended, axis=1, keepdims=True)
-    grad_query_rot, grad_keys, grad_values = attend_back(
-        query_rot, keys_all, values_all, low, high, logical_keys, lse, grad_heads, delta
-    )
-    both = jnp.concatenate([grad_keys[tokens:], grad_values[tokens:]], axis=1).astype(BF)
-    received = swap_cores(both).astype(F32)
-    grad_key_rot = grad_keys[:tokens] + received[:, :HD]
-    grad_value_low = (grad_values[:tokens] + received[:, HD:]).astype(BF)
-    grad_query_normed = turn(grad_query_rot, tables_own, -1.0)
-    grad_key_normed = turn(grad_key_rot, tables_own, -1.0)
-    query_gain_term = jnp.sum(grad_query_normed * query_proj * query_scale, axis=0)
-    key_gain_term = jnp.sum(grad_key_normed * key_proj * key_scale, axis=0)
-    weighted_query = grad_query_normed * query_gain_row
-    weighted_key = grad_key_normed * key_gain_row
-    dots = jnp.concatenate(
-        [jnp.sum(weighted_query * query_proj, axis=1), jnp.sum(weighted_key * key_proj, axis=1)]
-    ).reshape(-1, 128)
-    dots = plane_totals(dots, 6).reshape(2, tokens, 1)
-    grad_query_low = (
-        query_scale * weighted_query - query_proj * (query_scale * query_scale * query_scale * dots[0] / D)
-    ).astype(BF)
-    grad_key_low = (
-        key_scale * weighted_key - key_proj * (key_scale * key_scale * key_scale * dots[1] / D)
-    ).astype(BF)
-    grad_qkv = jnp.concatenate([grad_query_low, grad_key_low, grad_value_low], axis=1)
-    input_term = dotf(grad_qkv, jnp.transpose(qkv_w, (1, 0, 2)).reshape(D, 3 * HD), turned)
-    qkv_grad = dotf(full_in, grad_qkv, sum_rows)
-    out_grad = dotf(attended_low, grad_attn, sum_rows)
-    wall_grad = jnp.concatenate(
-        [
-            jnp.transpose(qkv_grad.reshape(8, 2, HD, 3, HD), (1, 0, 3, 2, 4)),
-            jnp.transpose(out_grad.reshape(HD, 8, 2, HD), (2, 1, 0, 3))[:, :, None],
-        ],
-        axis=2,
-    )
-    to_other = lax.dynamic_index_in_dim(wall_grad, 1 - k, 0, keepdims=False).astype(BF)
-    to_owner = (
-        lax.dynamic_index_in_dim(wall_grad, k, 0, keepdims=False)
-        + swap_cores(to_other).astype(F32)
-    ).astype(BF)
-    input_grad, wall_back = close_layer(input_term.astype(BF), grad_own, to_owner)
-    wall_back = wall_back.astype(F32).reshape(4, 2, 4, HD, HD)
-
-    def columns_back(i):
-        return jnp.transpose(wall_back[:, :, i], (1, 2, 0, 3)).reshape(w_query.shape)
-
-    grad_w_out = jnp.transpose(wall_back[:, :, 3], (0, 2, 1, 3)).reshape(w_out.shape)
-
-    def all_features(term):
-        return lax.dynamic_update_slice_in_dim(jnp.zeros((D,), F32), term, head * HD, 0)
-
-    gain_totals = lax.psum(
-        jnp.stack(
-            [
-                all_features(query_gain_term),
-                all_features(key_gain_term),
-                jnp.sum(attn_gain_term, axis=0),
-                jnp.sum(ffn_gain_term, axis=0),
-            ]
-        ),
-        AXES,
-    )
-    gain_grads = lax.dynamic_slice_in_dim(gain_totals, (2 * x + k) * width_part, width_part, 1)
+    input_grad, grad_query, grad_key, grad_value, grad_w_out, gain_grads = attention_backward(
+        grad_attn,
+        full_in,
+        query_proj,
+        key_proj,
+        query_rot,
+        keys_all,
+        values_all,
+        attended,
+        lse,
+        tables,
+        (low, high),
+        logical_keys,
+        scales,
+        head_gains,
+        qkv_w,
+        out_w,
+        grad_own,
+        attn_gain_term,
+        ffn_gain_term,
+    )
     return (
         outputs,
         input_grad,
-        columns_back(0),
-        columns_back(1),
-        columns_back(2),
+        grad_query,
+        grad_key,
+        grad_value,
         grad_w_out,
         grad_w_gate,
         grad_w_up,

time: 738 us -> 575 us (0.78)
  local copies, waits for them, and re-layouts: 82.2 us -> 30.4 us
  blocking collectives: 38.9 us -> 0 us
  other arithmetic: 41.8 us -> 8.39 us
  matrix products: 66.7 us -> 34.7 us
    psum x1 -> x0, blocking collectives: 38.9 us -> none  [plane_layer(): lax.psum(jnp.stack([all_features(query_gain_term), all_features(key_gain_...]
    dot_general x17 -> x9, matrix products: 66.7 us -> 34.7 us  [dotf(): lax.dot_general(left, right, (dims, ((), ())), preferred_element_type=F32)]
    reshape x12 -> x0, local copies, waits for them, and re-layouts: 20.9 us -> none  [the longest x2 7.82 us: plane_layer(): qkv_grad.reshape(8, 2, HD, 3, HD)]
    convert_element_type x10 -> x0, other arithmetic: 12.7 us -> none  [the longest x3 3.23 us: columns(): return jnp.transpose(weight.astype(BF).reshape(2, HD, 4, HD), (2, 0, 1, 3))]
    another operation x5 -> x1, other arithmetic: 8.87 us -> 0.18 us
    slice x6 -> x1, local copies, waits for them, and re-layouts: 8.36 us -> 0.77 us  [plane_layer(): head_gains = lax.dynamic_slice_in_dim(gains_full[:2], head * HD, HD, 1)]
    unnamed x96 -> x50, local copies, waits for them, and re-layouts: 17.1 us -> 11.6 us
    pallas_call x7 -> x3, Pallas kernels: 289 us -> 294 us  [the longest x1 139 us: attention_forward(): comm_call(body, 'attention_forward', 1, (shape((tokens, width), BF), shap...]
  transfers between devices with their start and end apart: 6 -> 2, of which waited for: 0 -> 1; matrix products, arithmetic and copies ran while one was open for 17% -> 2% of each run, Pallas kernels for 55% -> 34%
where the time goes in v2:
time: 575 us; the launch traced here: 570 us
  Pallas kernels  486 us (85%)
  matrix products  34.7 us (6%)
  local copies, waits for them, and re-layouts  30.4 us (5%)
  other arithmetic  8.39 us (1%)
  starting transfers between devices  6.25 us (1%)
    pallas_call x1, Pallas kernels, attention_forward(): comm_call(body, 'attention_forward', 1, (shape((tokens, width), BF), shap...  139 us
    pallas_call x1, Pallas kernels, after_ffn_back(): comm_call(body, 'after_ffn_back', 4, (shape((tokens, width), BF), shape((...  111 us
    pallas_call x1, Pallas kernels, attention_backward(): comm_call(body, 'attention_backward', 5, (shape((rows * 4, part), BF), sh...  84.4 us
    pallas_call x1, Pallas kernels, after_ffn(): comm_call(body, 'after_ffn', 3, (shape((tokens, width), BF), shape((rows...  80.6 us
    pallas_call x1, Pallas kernels, open_layer(): comm_call(body, 'open_layer', 0, (shape((tokens, width), BF), shape((quar...  70.5 us
    dot_general x9, matrix products, dotf(): lax.dot_general(left, right, (dims, ((), ())), preferred_element_type=F32)  34.7 us
    unnamed x50, local copies, waits for them, and re-layouts  11.6 us
  transfers between devices with their start and end apart: 2, of which 1 were waited for; matrix products, arithmetic and copies ran while one was open for 2% of the time, Pallas kernels for 34%

profile of v2, /device:TPU:1, one launch (start us, length us, event | category | flops | bytes accessed | tf_op | source)
XLA Modules:
  0.0 570.4 jit_solution(11545335046111586849)
XLA Ops:
  0.7 0.7 reshape.135
  1.5 0.1 mul.72
  1.5 0.1 iota_add_fusion.1
  1.6 0.1 add.81
  1.7 1.3 add.95.refs_6_.refs_12_
  3.0 1.3 pad_maximum_fusion.3.refs_9_
  4.4 70.5 %open_layer.1 = (bf16[1024,2048]{1,0:T(8,128)(2,1)}, bf16[64,2048]{1,0:T(8,128)(2,1)}, bf16[64,2048]{1,0:T(8,128)(2,1)}, bf16[3,2048,128]{2,1,0:T(8,128)(2,1)}, ...) custom-call(bf16[256,512]{1,0:T(8,128)(2,1)} %refs_0_.1, ...), custom_call_target="tpu_custom_call" | custom-call | tf_op jit(solution)/shard_map/open_layer/pallas_call | solution.py:703
  74.9 0.8 slice.57
  75.6 1.5 fusion.14
  77.1 0.2 reduce-window.8
  77.3 0.1 mul.77
  77.4 0.1 convert_reduce_fusion
  77.4 0.1 select_reduce_fusion
  77.5 0.1 iota_add_fusion
  77.6 0.1 add.87
  77.7 0.6 pad_add_fusion
  78.3 1.0 copy.77.refs_5_.refs_11_
  79.3 1.9 fusion.12
  81.2 0.6 constant_dynamic-slice_fusion.refs_10_.refs_15_
  81.8 1.3 pad_maximum_fusion.1
  83.1 138.8 %attention_forward.1 = (bf16[1024,2048]{1,0:T(8,128)(2,1)}, f32[64,2048]{1,0:T(8,128)}, f32[64,2048]{1,0:T(8,128)}, bf16[2,2048,512]{2,1,0:T(8,128)(2,1)}, bf16[...) custom-call(f32[1024,128]{1,0:T(8,128)} %get-tuple-element.47.refs_0, ...), custom_call_target="tpu_custom_call" | custom-call | tf_op jit(solution)/shard_map/attention_forward/pallas_call | solution.py:1004
  221.9 5.3 fusion.6
  227.2 0.0 copy-start.18
  227.3 3.9 multiply_convert_fusion.2
  231.1 4.3 convolution_convert_fusion.term_ref
  235.4 80.6 %after_ffn.1 = (bf16[1024,2048]{1,0:T(8,128)(2,1)}, bf16[256,512]{1,0:T(8,128)(2,1)}, f32[8,2048]{1,0:T(8,128)}) custom-call(bf16[1024,2048]{1,0:T(8,128)(2,1)} %convolution_convert_fusion.term_ref, f32[64,2048]{1,0:T(8,128)} %get-tuple-element.58.res_ref, bf16[64,2048]{1,0:T(8,128)(2,1)} %get-tuple-element.59.cot_ref, f32[1,2048]{1,0:T(1,128)} %get-tuple-element.127.gain_ref), custom_call_target="tpu_custom_call" | custom-call | tf_op jit(solution)/shard_map/after_ffn/pallas_call | solution.py:1076
  316.0 0.0 copy-start.19
  316.0 0.0 copy-start.20
  316.1 4.8 fusion.18
  320.9 3.0 multiply_convert_fusion
  323.9 0.0 copy-start.14
  323.9 0.0 copy-start.16
  323.9 0.1 slice.103
  324.1 0.1 copy.96
  324.2 2.5 fusion.17
  326.7 2.5 fusion.16
  329.2 0.1 slice.105
  329.3 0.1 slice.104
  329.5 0.3 pad_maximum_fusion
  329.8 1.4 collective-permute-start
  331.2 0.0 slice-start.1
  331.3 1.6 slice-done
  332.8 0.2 copy.95
  333.0 3.5 collective-permute-done
  336.5 2.4 fusion
  338.9 4.8 all-to-all-start
  343.7 0.0 copy-start.15
  343.7 4.1 fusion.4
  347.9 4.4 add_convert_fusion.term_ref
  352.2 111.3 %after_ffn_back.1 = (bf16[1024,2048]{1,0:T(8,128)(2,1)}, f32[64,2048]{1,0:T(8,128)}, f32[8,2048]{1,0:T(8,128)}) custom-call(bf16[1024,2048]{1,0:T(8,128)(2,1)} %add_convert_fusion.term_ref, bf16[64,2048]{1,0:T(8,128)(2,1)} %get-tuple-element.59.cot_ref, f32[64,2048]{1,0:T(8,128)} %get-tuple-element.62.branch_ref, f32[1,2048]{1,0:T(1,128)} %get-tuple-element.128.refs_11_.gain_ref), custom_call_target="tpu_custom_call" | custom-call | tf_op jit(solution)/shard_map/after_ffn_back/pallas_call | solution.py:1120
  463.6 84.4 %attention_backward.1 = (bf16[256,512]{1,0:T(8,128)(2,1)}, f32[256,512]{1,0:T(8,128)}, f32[256,512]{1,0:T(8,128)}, f32[256,512]{1,0:T(8,128)}, f32[512,256]{1,0:T(8,128)}, /*index=5*/f32[4,512]{1,0:T(4,128)}) custom-call(bf16[1024,2048]{1,0:T(8,128)(2,1)} %get-tuple-element.63.refs_0_, bf16[1024,2048]{1,0:T(8,128)(2,1)} %get-tuple-element.64.refs_1_, ...), custom_call_target="tpu_custom_call" | custom-call | tf_op jit(solution)/shard_map/attention_backward/pallas_call | solution.py:1465
  548.0 1.4 fusion.15
  549.5 0.0 all-to-all-done
  549.5 3.2 copy.87
  552.7 2.9 fusion.13
  555.6 2.9 copy.88
  558.5 3.0 copy.90
  561.5 1.8 copy.89
  563.3 0.7 copy.103
  564.0 1.7 copy.104
  565.7 1.9 copy.105
  567.6 0.8 copy.106
  568.4 0.8 copy.107
  569.2 0.8 copy.108
  (44 shorter events, 0.1 us)
Async XLA Ops:
  4.4 72.7 %copy-start.13 = (s32[4]{0:T(128)S(1)}, s32[4]{0:T(128)}, u32[]{:S(2)}) copy-start(s32[4]{0:T(128)} %param.28) | copy-start | bytes 52
  221.9 5.3 copy-start.9
  221.9 5.3 copy-start.11
  227.2 3.9 copy-start.18
  227.3 3.9 copy-start.12
  316.0 4.8 copy-start.1
  316.0 4.8 copy-start.19
  316.0 4.8 copy-start.20
  320.9 10.4 %copy-start = (f32[512,2048]{1,0:T(8,128)}, f32[512,2048]{1,0:T(8,128)S(1)}, u32[]{:S(2)}) copy-start(f32[512,2048]{1,0:T(8,128)S(1)} %fusion.18) | copy-start | bytes 12582916
  323.9 2.7 copy-start.14
  323.9 2.7 copy-start.16
  326.7 4.6 copy-start.3
  329.2 2.1 copy-start.2
  329.8 6.7 %collective-permute-start = (bf16[8,3,256,256]{3,2,1,0:T(8,128)(2,1)S(1)}, bf16[8,3,256,256]{3,2,1,0:T(8,128)(2,1)S(1)}, u32[]{:S(2)}, u32[]{:S(2)}) collective-permute-start(bf16[8,3,256,256]{3,2,1,0:T(8,128)(2,1)S(1)} %pad_maximum_fusion), channel_id=1, source_target_pairs={{0,1},{1,0},{2,3},{3,2},{4,5},{5,4},{6,7},{7,6},{8,9},{9,8},{10,11... | collective-permute-start | bytes 9437192 | tf_op jit(solution)/shard_map/ppermute | solution.py:1550
  331.2 1.6 slice-start
  331.2 5.3 slice-start.1
  331.3 5.3 slice-start.2
  338.9 4.8 copy-start.17
  338.9 210.6 %all-to-all-start = ((bf16[8,3,256,256]{3,2,1,0:T(8,128)(2,1)}), bf16[8,3,256,256]{3,2,1,0:T(8,128)(2,1)}, u32[]{:S(2)}, u32[]{:S(2)}) async-start(bf16[8,3,256,256]{3,2,1,0:T(8,128)(2,1)} %fusion), calls=%async_computation | async-start | bytes 6291456 | tf_op jit(solution)/shard_map/all_to_all | solution.py:1670
  343.7 4.1 copy-start.10
  343.7 4.1 copy-start.15
  558.5 3.0 copy-start.4
  561.5 1.8 copy-start.8
  561.5 6.1 %copy-start.7 = (f32[256,512]{1,0:T(8,128)S(1)}, f32[256,512]{1,0:T(8,128)}, u32[]{:S(2)}) copy-start(f32[256,512]{1,0:T(8,128)} %get-tuple-element.156) | copy-start | bytes 1572868
  561.5 6.9 %copy-start.6 = (f32[256,512]{1,0:T(8,128)S(1)}, f32[256,512]{1,0:T(8,128)}, u32[]{:S(2)}) copy-start(f32[256,512]{1,0:T(8,128)} %get-tuple-element.157) | copy-start | bytes 1572868
  563.3 5.8 %copy-start.5 = (f32[512,256]{1,0:T(8,128)S(1)}, f32[512,256]{1,0:T(8,128)}, u32[]{:S(2)}) copy-start(f32[512,256]{1,0:T(8,128)} %get-tuple-element.158) | copy-start | bytes 1572868

commit v3 on v2

--- a/solution.py
+++ b/solution.py
@@ -1040,14 +1040,47 @@
     )(query, key, value, *tables, *bounds, logical, source, out_weight, gains, attn_gain, gu_stage, d_stage)
 
 
-def after_ffn(terms, residual, cotangent, gain):
-    tokens, width = terms.shape
-    rows = tokens // 16
-
-    def body(term_ref, res_ref, cot_ref, gain_ref, full_ref, out_ref, gg_ref, shard, result, local, out_send, out_recv, *scratch):
-        me = place()
+def ffn_forward(source, gu_w, down_w, residual, cotangent, gain):
+    tokens, width = source.shape
+    rows, group = tokens // 16, tokens // 4
+    hidden = down_w.shape[0]
+
+    def body(*refs):
+        (h_any, gu_any, d_any, res_ref, cot_ref, gain_ref) = refs[:6]
+        (full_ref, out_ref, gg_ref, for_gate_ref, for_up_ref, m_ref) = refs[6:12]
+        (hs, gu, dw, terms, shard, result, load_sem, local, out_send, out_recv) = refs[12:22]
+        scratch = refs[22:]
+        me = z, y, x, k = place()
+
+        def h_load(zp):
+            at = pl.ds(pl.multiple_of(zp * group, group), group)
+            return pltpu.make_async_copy(h_any.at[at, :], hs.at[at, :], load_sem.at[zp])
+
+        order = [near_first(step, z) for step in (3, 2, 1, 0)]
+        gu_load = pltpu.make_async_copy(gu_any, gu, load_sem.at[4])
+        d_load = pltpu.make_async_copy(d_any, dw, load_sem.at[5])
+        h_load(order[0]).start()
+        gu_load.start()
+        d_load.start()
+        for zp in order[1:]:
+            h_load(zp).start()
         greet_plane(me, pair_devices(me))
         gg_ref[...] = jnp.zeros_like(gg_ref)
+        gu_load.wait()
+
+        def produce(zp):
+            at = pl.ds(pl.multiple_of(zp * group, group), group)
+            h_load(zp).wait()
+            tile = hs[at, :]
+            gate = jnp.dot(tile, gu[0], preferred_element_type=F32)
+            up = jnp.dot(tile, gu[1], preferred_element_type=F32)
+            sig = jax.nn.sigmoid(gate)
+            silu = gate * sig
+            mixed = (silu * up).astype(BF)
+            for_gate_ref[at, :] = up * sig * (1.0 + gate * (1.0 - sig))
+            for_up_ref[at, :] = silu
+            m_ref[at, :] = mixed
+            terms[at, :] = jnp.dot(mixed, dw[...], preferred_element_type=F32).astype(BF)
 
         def finish(strip, total):
             gain_row = gain_ref[...]
@@ -1057,7 +1090,8 @@
             gg_ref[...] += term
             shard[strip] = back.astype(BF)
 
-        settle = reduce_plane(me, term_ref, rows, scratch[:N_REDUCE], lambda zp: None, finish)
+        d_load.wait()
+        settle = reduce_plane(me, terms, rows, scratch[:N_REDUCE], produce, finish)
         view = gather_view(full_ref, rows)
         keep = pltpu.make_async_copy(shard, view(me[0] * 4 + me[1] * 2 + me[2]), local)
         keep.start()
@@ -1075,31 +1109,136 @@
     shape = jax.ShapeDtypeStruct
     return comm_call(
         body,
-        "after_ffn",
+        "ffn_forward",
         3,
-        (shape((tokens, width), BF), shape((rows * 4, width // 4), BF), shape((8, width), F32)),
-        [VMEM, VMEM, VMEM, VMEM],
-        (ANY, ANY, VMEM),
+        (
+            shape((tokens, width), BF),
+            shape((rows * 4, width // 4), BF),
+            shape((8, width), F32),
+            shape((tokens, hidden), F32),
+            shape((tokens, hidden), F32),
+            shape((tokens, hidden), BF),
+        ),
+        [ANY, ANY, ANY, VMEM, VMEM, VMEM],
+        (ANY, ANY, VMEM, VMEM, VMEM, VMEM),
         [
+            pltpu.VMEM((tokens, width), BF),
+            pltpu.VMEM((2, width, hidden), BF),
+            pltpu.VMEM((hidden, width), BF),
+            pltpu.VMEM((tokens, width), BF),
             pltpu.VMEM((rows, width), BF),
             pltpu.VMEM((rows, width), BF),
+            DMA((6,)),
             DMA,
             DMA((3,)),
             DMA((4,)),
             *reduce_scratch(rows, width),
             *GATHER_SEMS,
         ],
-    )(terms, residual, cotangent, gain)
-
-
-def after_ffn_back(terms, cotangent, branch, gain):
-    tokens, width = terms.shape
-    rows = tokens // 16
-
-    def body(term_ref, cot_ref, branch_ref, gain_ref, full_ref, own_ref, gg_ref, shard, local, *scratch):
-        me = place()
-        greet_plane(me)
+    )(source, gu_w, down_w, residual, cotangent, gain)
+
+
+EARLY = 4
+
+
+def grad_copy(me, src, dst, send, recv, t):
+    ctx = own_tile(me)
+    to = ctx + t - 8 * ((ctx + t) // 8)
+    return pltpu.make_async_remote_copy(
+        src_ref=src,
+        dst_ref=dst.at[ctx],
+        send_sem=send.at[t],
+        recv_sem=recv.at[t],
+        device_id=(to // 2, to % 2, me[2], me[3]),
+        device_id_type=MESH,
+    )
+
+
+def grad_landed(me, dst, send, recv, t):
+    ctx = own_tile(me)
+    c = ctx + 8 - t - 8 * ((ctx + 8 - t) // 8)
+    pltpu.make_async_remote_copy(
+        src_ref=dst.at[c],
+        dst_ref=dst.at[c],
+        send_sem=send.at[t],
+        recv_sem=recv.at[t],
+        device_id=(me[0], me[1], me[2], 1 - me[3]),
+        device_id_type=MESH,
+    ).wait_recv()
+
+
+def ctx_greet(me, others):
+    z, y, x, k = me
+    barrier = pltpu.get_barrier_semaphore()
+
+    def call(i, carry):
+        to = lax.rem(z * 2 + y + i, 8)
+        pl.semaphore_signal(
+            barrier, inc=1, device_id=(to // 2, to % 2, x, k), device_id_type=MESH
+        )
+        return carry
+
+    lax.fori_loop(1, 8, call, 0)
+    for target in [(z, y, 1 - x, k), *others]:
+        pl.semaphore_signal(barrier, inc=1, device_id=target, device_id_type=MESH)
+    pl.semaphore_wait(barrier, 8 + len(others))
+
+
+def ffn_backward(grad_ffn, source, gu_w, down_w, for_gate, for_up, mixed, cotangent, branch, gain):
+    tokens, width = grad_ffn.shape
+    rows, group = tokens // 16, tokens // 4
+    hidden = down_w.shape[0]
+    part = hidden // 2
+    across = (((0,), (0,)), ((), ()))
+    turned = (((1,), (1,)), ((), ()))
+
+    def body(*refs):
+        (df_any, h_any, gu_any, d_any, fg_any, fu_any, m_any, cot_ref, branch_ref, gain_ref) = refs[:10]
+        (full_ref, own_ref, gg_ref, in_ref, rest_ref) = refs[10:15]
+        (df, hs, gu, dw, fg, fu, ms, dgu, terms, shard) = refs[15:25]
+        (mine, to_core, from_core, to_ctx) = refs[25:29]
+        (load_sem, local, core_send, core_recv, grad_send, grad_recv, rest_sem) = refs[29:36]
+        scratch = refs[36:]
+        me = z, y, x, k = place()
+        ctx = own_tile(me)
+        order = [near_first(step, z) for step in (3, 2, 1, 0)]
+
+        def group_load(zp):
+            at = pl.ds(pl.multiple_of(zp * group, group), group)
+            return [
+                pltpu.make_async_copy(src.at[at, :], dst.at[at, :], load_sem.at[i, zp])
+                for i, (src, dst) in enumerate(((df_any, df), (fg_any, fg), (fu_any, fu)))
+            ]
+
+        d_load = pltpu.make_async_copy(d_any, dw, load_sem.at[3, 0])
+        gu_load = pltpu.make_async_copy(gu_any, gu, load_sem.at[3, 1])
+        h_load = pltpu.make_async_copy(h_any, hs, load_sem.at[3, 2])
+        m_load = pltpu.make_async_copy(m_any, ms, load_sem.at[3, 3])
+        for load in (*group_load(order[0]), d_load, gu_load):
+            load.start()
+        for zp in order[1:]:
+            for load in group_load(zp):
+                load.start()
+        h_load.start()
+        m_load.start()
+        sibling = (z, y, x, 1 - k)
+        ctx_greet(me, [sibling])
         gg_ref[...] = jnp.zeros_like(gg_ref)
+        d_load.wait()
+
+        def produce(zp):
+            at = pl.ds(pl.multiple_of(zp * group, group), group)
+            for load in group_load(zp):
+                load.wait()
+            dm = lax.dot_general(df[at, :], dw[...], turned, preferred_element_type=F32)
+            dg = (dm * fg[at, :]).astype(BF)
+            du = (dm * fu[at, :]).astype(BF)
+            dgu[at, :hidden] = dg
+            dgu[at, hidden:] = du
+            terms[at, :] = (
+                lax.dot_general(dg, gu[0], turned, preferred_element_type=F32)
+                + lax.dot_general(du, gu[1], turned, preferred_element_type=F32)
+            ).astype(BF)
 
         def finish(strip, total):
             grad = cot_ref[strip].astype(F32) + total
@@ -1108,24 +1247,197 @@
             gg_ref[...] += term
             shard[strip] = back.astype(BF)
 
-        settle = reduce_plane(me, term_ref, rows, scratch[:N_REDUCE], lambda zp: None, finish)
+        def core_copy(t):
+            return pltpu.make_async_remote_copy(
+                src_ref=to_core.at[t],
+                dst_ref=from_core.at[t],
+                send_sem=core_send.at[t],
+                recv_sem=core_recv.at[t],
+                device_id=sibling,
+                device_id_type=MESH,
+            )
+
+        def compute(t):
+            c = ctx + t - 8 * ((ctx + t) // 8)
+            at = pl.ds(pl.multiple_of(c * part, part), part)
+            up_like = lax.dot_general(hs[:, at], dgu[...], across, preferred_element_type=F32)
+            down_like = lax.dot_general(ms[...], df[:, at], across, preferred_element_type=F32)
+            slot = t % 2
+            for i in range(2):
+                mine[slot, i] = up_like[:, 2 * i * part : (2 * i + 1) * part]
+                to_core[t, i] = up_like[:, (2 * i + 1) * part : (2 * i + 2) * part].astype(BF)
+            mine[slot, 2] = down_like[:part]
+            to_core[t, 2] = down_like[part:].astype(BF)
+            core_copy(t).start()
+
+        def send(t):
+            core_copy(t).wait_recv()
+            to_ctx[t] = (mine[t % 2] + from_core[t].astype(F32)).astype(BF)
+            if t == 0:
+                pltpu.make_async_copy(to_ctx.at[0], in_ref.at[ctx], rest_sem.at[0]).start()
+            elif t <= EARLY:
+                grad_copy(me, to_ctx.at[t], in_ref, grad_send, grad_recv, t).start()
+            else:
+                pltpu.make_async_copy(
+                    to_ctx.at[t], rest_ref.at[t - EARLY - 1], rest_sem.at[t - EARLY]
+                ).start()
+
+        def grads(first, last):
+            for t in range(first, last):
+                compute(t)
+                if t > 0:
+                    send(t - 1)
+
+        def after_terms():
+            h_load.wait()
+            m_load.wait()
+            grads(0, 3)
+
+        between = [
+            lambda: grads(3, 5),
+            lambda: grads(5, 6),
+            lambda: grads(6, 7),
+            lambda: grads(7, 8),
+            lambda: send(7),
+        ]
+        gu_load.wait()
+        settle = reduce_plane(me, terms, rows, scratch[:N_REDUCE], produce, finish, after_terms)
         view = gather_view(full_ref, rows)
         keep = pltpu.make_async_copy(shard, view(me[0] * 4 + me[1] * 2 + me[2]), local)
         keep.start()
-        gather_plane(me, shard, view, scratch[N_REDUCE:])
+        gather_plane(me, shard, view, scratch[N_REDUCE:], lambda step: between[step]())
         keep.wait()
         settle()
+        for t in range(8):
+            core_copy(t).wait_send()
+        pltpu.make_async_copy(to_ctx.at[0], in_ref.at[ctx], rest_sem.at[0]).wait()
+        for t in range(1, 8):
+            if t <= EARLY:
+                grad_landed(me, in_ref, grad_send, grad_recv, t)
+                grad_copy(me, to_ctx.at[t], in_ref, grad_send, grad_recv, t).wait_send()
+            else:
+                pltpu.make_async_copy(
+                    to_ctx.at[t], rest_ref.at[t - EARLY - 1], rest_sem.at[t - EARLY]
+                ).wait()
 
     shape = jax.ShapeDtypeStruct
+    vmem = pltpu.VMEM
     return comm_call(
         body,
-        "after_ffn_back",
+        "ffn_backward",
         4,
-        (shape((tokens, width), BF), shape((rows, width), F32), shape((8, width), F32)),
-        [VMEM, VMEM, VMEM, VMEM],
-        (ANY, VMEM, VMEM),
-        [pltpu.VMEM((rows, width), BF), DMA, *reduce_scratch(rows, width), *GATHER_SEMS],
-    )(terms, cotangent, branch, gain)
+        (
+            shape((tokens, width), BF),
+            shape((rows, width), F32),
+            shape((8, width), F32),
+            shape((8, 3, part, part), BF),
+            shape((7 - EARLY, 3, part, part), BF),
+        ),
+        [*[ANY] * 7, VMEM, VMEM, VMEM],
+        (ANY, VMEM, VMEM, ANY, ANY),
+        [
+            vmem((tokens, width), BF),
+            vmem((tokens, width), BF),
+            vmem((2, width, hidden), BF),
+            vmem((hidden, width), BF),
+            vmem((tokens, hidden), F32),
+            vmem((tokens, hidden), F32),
+            vmem((tokens, hidden), BF),
+            vmem((tokens, 2 * hidden), BF),
+            vmem((tokens, width), BF),
+            vmem((rows, width), BF),
+            vmem((2, 3, part, part), F32),
+            vmem((8, 3, part, part), BF),
+            vmem((8, 3, part, part), BF),
+            vmem((8, 3, part, part), BF),
+            DMA((4, 4)),
+            DMA,
+            DMA((8,)),
+            DMA((8,)),
+            DMA((8,)),
+            DMA((8,)),
+            DMA((8,)),
+            *reduce_scratch(rows, width),
+            *GATHER_SEMS,
+        ],
+    )(grad_ffn, source, gu_w, down_w, for_gate, for_up, mixed, cotangent, branch, gain)
+
+
+def write_results(early, late, wall, outputs, input_grad, gains):
+    part = early.shape[2]
+
+    def body(early_ref, late_ref, wall_ref, out_ref, in_ref, gain_ref, *results):
+        (out_to, in_to, gq, gk, gv, go, gg, gu, gd, gains_to) = results
+        c = pl.program_id(0)
+        ctx = lax.axis_index("z") * 2 + lax.axis_index("y")
+        t = lax.rem(ctx + 8 - c, 8)
+
+        @pl.when(c == 0)
+        def _():
+            out_to[...] = out_ref[...]
+            in_to[...] = in_ref[...]
+            gains_to[...] = gain_ref[...]
+
+        for i, ref in enumerate((gq, gk, gv, go)):
+            ref[...] = wall_ref[0, i].astype(F32)
+
+        @pl.when(t <= EARLY)
+        def _():
+            for i, ref in enumerate((gg, gu, gd)):
+                ref[...] = early_ref[0, i].astype(F32)
+
+        @pl.when(t > EARLY)
+        def _():
+            for i, ref in enumerate((gg, gu, gd)):
+                ref[...] = late_ref[0, i].astype(F32)
+
+    shape = jax.ShapeDtypeStruct
+    spec = pl.BlockSpec
+    blob = spec((1, 3, part, part), lambda c: (c, 0, 0, 0))
+    rows, columns = outputs.shape
+    whole = spec((rows, columns), lambda c: (0, 0))
+    in_row = spec((HD, HD), lambda c: (c % 2, c // 2))
+    in_column = spec((HD, HD), lambda c: (c // 2, c % 2))
+    side = spec((part, part), lambda c: (0, c))
+    gain_spec = spec(gains.shape, lambda c: (0, 0))
+    return pl.pallas_call(
+        body,
+        name="write_results",
+        grid=(8,),
+        out_shape=(
+            shape((rows, columns), BF),
+            shape((rows, columns), BF),
+            shape((2 * HD, 4 * HD), F32),
+            shape((2 * HD, 4 * HD), F32),
+            shape((2 * HD, 4 * HD), F32),
+            shape((4 * HD, 2 * HD), F32),
+            shape((part, 8 * part), F32),
+            shape((part, 8 * part), F32),
+            shape((8 * part, part), F32),
+            shape(gains.shape, F32),
+        ),
+        in_specs=[
+            blob,
+            blob,
+            spec((1, 4, HD, HD), lambda c: (c, 0, 0, 0)),
+            whole,
+            whole,
+            gain_spec,
+        ],
+        out_specs=(
+            whole,
+            whole,
+            in_row,
+            in_row,
+            in_row,
+            in_column,
+            side,
+            side,
+            spec((part, part), lambda c: (c, 0)),
+            gain_spec,
+        ),
+        compiler_params=pltpu.CompilerParams(vmem_limit_bytes=BIG_VMEM),
+    )(early, late, wall, outputs, input_grad, gains)
 
 
 def close_greet(me):
@@ -1168,6 +1480,7 @@
     grad_own,
     attn_term,
     ffn_term,
+    grads_left,
 ):
     tokens, width = grad_attn.shape
     rows, group = tokens // 16, tokens // 4
@@ -1178,14 +1491,14 @@
         (da_any, x_any) = refs[:2]
         (q_ref, k_ref, qrot_ref, keys_ref, values_ref, o_ref, lse_ref, cos_ref, sin_ref) = refs[2:11]
         (low_ref, high_ref, log_ref, scale_ref, gain_ref, wqkv_ref, wout_ref) = refs[11:18]
-        (grad_ref, attn_ref, ffn_ref) = refs[18:21]
-        (in_grad_ref, gq_ref, gk_ref, gv_ref, gout_ref, gains_ref) = refs[21:27]
-        (da, xs, terms, do_ref, delta_ref, dq_ref, dk_ref, dv_ref) = refs[27:35]
-        (pair_out, pair_in, dqkv, slots, result) = refs[35:40]
-        (wall_grad, wall_out, wall_in, deal_out, deal_in) = refs[40:45]
-        (gain_out, gain_in, gain_own, gain_slots) = refs[45:49]
-        (load_sem, pair_send, pair_recv, tot_send, tot_recv, out_send, out_recv) = refs[49:56]
-        (deal_send, deal_recv, gain_send, gain_recv) = refs[56:60]
+        (grad_ref, attn_ref, ffn_ref, left_ref) = refs[18:22]
+        (in_grad_ref, deal_in, gains_ref, ffn_in) = refs[22:26]
+        (da, xs, terms, do_ref, delta_ref, dq_ref, dk_ref, dv_ref) = refs[26:34]
+        (pair_out, pair_in, dqkv, slots, result) = refs[34:39]
+        (wall_grad, wall_out, wall_in, deal_out) = refs[39:43]
+        (gain_out, gain_in, gain_own, gain_slots) = refs[43:47]
+        (load_sem, pair_send, pair_recv, tot_send, tot_recv, out_send, out_recv) = refs[47:54]
+        (deal_send, deal_recv, gain_send, gain_recv, grad_send, grad_recv) = refs[54:60]
         scratch = refs[60:]
         me = z, y, x, k = place()
         ctx = own_tile(me)
@@ -1204,6 +1517,8 @@
         for load in (*da_loads, x_load):
             load.start()
         close_greet(me)
+        for t in range(EARLY + 1, 8):
+            grad_copy(me, left_ref.at[t - EARLY - 1], ffn_in, grad_send, grad_recv, t).start()
 
         def pair(n):
             return pltpu.make_async_remote_copy(
@@ -1424,10 +1739,6 @@
         own_copy.start()
         for n in range(8):
             pltpu.make_async_copy(deal_out.at[n], deal_in.at[n], deal_recv.at[n]).wait()
-            j, r = n // 2, n % 2
-            for i, ref in enumerate((gq_ref, gk_ref, gv_ref)):
-                ref[r * HD : (r + 1) * HD, j * HD : (j + 1) * HD] = deal_in[n, i].astype(F32)
-            gout_ref[j * HD : (j + 1) * HD, r * HD : (r + 1) * HD] = deal_in[n, 3].astype(F32)
 
         def gain_landed(i, carry):
             other, device = plane_peer(me, i)
@@ -1459,6 +1770,11 @@
 
         for n in range(4):
             pair(n).wait_send()
+        for t in range(EARLY + 1, 8):
+            grad_landed(me, ffn_in, grad_send, grad_recv, t)
+            grad_copy(
+                me, left_ref.at[t - EARLY - 1], ffn_in, grad_send, grad_recv, t
+            ).wait_send()
 
     shape = jax.ShapeDtypeStruct
     vmem = pltpu.VMEM
@@ -1468,14 +1784,12 @@
         5,
         (
             shape((rows * 4, part), BF),
-            shape((rows * 4, part), F32),
-            shape((rows * 4, part), F32),
-            shape((rows * 4, part), F32),
-            shape((part, rows * 4), F32),
+            shape((8, 4, HD, HD), BF),
             shape((4, part), F32),
+            shape((8, *grads_left.shape[1:]), BF),
         ),
-        [ANY, ANY, *[VMEM] * 19],
-        (ANY, VMEM, VMEM, VMEM, VMEM, VMEM),
+        [ANY, ANY, *[VMEM] * 19, ANY],
+        (ANY, ANY, VMEM, ANY),
         [
             vmem((tokens, width), BF),
             vmem((tokens, width), BF),
@@ -1494,7 +1808,6 @@
             vmem((8, 4, HD, HD), BF),
             vmem((8, 4, HD, HD), BF),
             vmem((8, 4, HD, HD), BF),
-            vmem((8, 4, HD, HD), BF),
             vmem((2, 4, part), F32),
             vmem((2, 4, part), F32),
             vmem((2, 4, part), F32),
@@ -1510,6 +1823,8 @@
             DMA((8,)),
             DMA((16,)),
             DMA((16,)),
+            DMA((8,)),
+            DMA((8,)),
             *reduce_scratch(rows, width),
         ],
     )(
@@ -1532,6 +1847,7 @@
         grad_own,
         attn_term,
         ffn_term,
+        grads_left,
     )
 
 
@@ -1544,14 +1860,6 @@
         jnp.concatenate([cosine, cosine], axis=1),
         jnp.concatenate([-sine_part, sine_part], axis=1),
     )
-
-
-def swap_cores(values):
-    return lax.ppermute(values, "core", [(0, 1), (1, 0)])
-
-
-def dotf(left, right, dims):
-    return lax.dot_general(left, right, (dims, ((), ())), preferred_element_type=F32)
 
 
 def plane_layer(
@@ -1576,7 +1884,6 @@
     tok_rows, width_part = inputs.shape
     plane_rows = tok_rows // 2
     tokens = 8 * plane_rows
-    hidden = w_gate.shape[1] // 8
 
     order = block_order.reshape(8, 2, -1)
     block_rows = plane_rows // order.shape[2]
@@ -1627,52 +1934,22 @@
         gu_stage,
         d_stage,
     )
-    gate_w, up_w = gu_w[0], gu_w[1]
-    rows_dims = ((1,), (0,))
-
-    gate_proj = dotf(residual_full, gate_w, rows_dims)
-    up_proj = dotf(residual_full, up_w, rows_dims)
-    gate_sigmoid = jax.nn.sigmoid(gate_proj)
-    mixed = (gate_proj * gate_sigmoid * up_proj).astype(BF)
-    grad_ffn, outputs, ffn_gain_term = after_ffn(
-        dotf(mixed, down_w, rows_dims).astype(BF), residual_own, own_cot, ffn_gain_row
-    )
-
-    sum_rows = ((0,), (0,))
-    turned = ((1,), (1,))
-    grad_mixed = dotf(grad_ffn, down_w, turned)
-    grad_gate = (
-        grad_mixed * up_proj * gate_sigmoid * (1.0 + gate_proj * (1.0 - gate_sigmoid))
-    ).astype(BF)
-    grad_up = (grad_mixed * gate_proj * gate_sigmoid).astype(BF)
-    resid_term = dotf(grad_gate, gate_w, turned) + dotf(grad_up, up_w, turned)
-    grad_attn, grad_own, attn_gain_term = after_ffn_back(
-        resid_term.astype(BF), own_cot, branch_own, attn_gain_row
-    )
-    gate_grad = dotf(residual_full, grad_gate, sum_rows)
-    up_grad = dotf(residual_full, grad_up, sum_rows)
-    down_grad = dotf(mixed, grad_ffn, sum_rows)
-    mine_grads = (gate_grad[:, :hidden], up_grad[:, :hidden], down_grad[:hidden])
-    other_grads = (gate_grad[:, hidden:], up_grad[:, hidden:], down_grad[hidden:])
-
-    def ffn_stack(grads):
-        return jnp.stack(
-            [
-                grads[0].reshape(8, -1, hidden),
-                grads[1].reshape(8, -1, hidden),
-                jnp.transpose(grads[2].reshape(hidden, 8, -1), (1, 0, 2)),
-            ],
-            axis=1,
-        )
-
-    from_other = swap_cores(ffn_stack(other_grads).astype(BF))
-    ffn_sum = (ffn_stack(mine_grads) + from_other.astype(F32)).astype(BF)
-    ffn_back = lax.all_to_all(ffn_sum, CTX, split_axis=0, concat_axis=0, tiled=True).astype(F32)
-    grad_w_gate = jnp.transpose(ffn_back[:, 0], (1, 0, 2)).reshape(w_gate.shape)
-    grad_w_up = jnp.transpose(ffn_back[:, 1], (1, 0, 2)).reshape(w_up.shape)
-    grad_w_down = ffn_back[:, 2].reshape(w_down.shape)
-
-    input_grad, grad_query, grad_key, grad_value, grad_w_out, gain_grads = attention_backward(
+    grad_ffn, outputs, ffn_gain_term, for_gate, for_up, mixed = ffn_forward(
+        residual_full, gu_w, down_w, residual_own, own_cot, ffn_gain_row
+    )
+    grad_attn, grad_own, attn_gain_term, ffn_early, ffn_left = ffn_backward(
+        grad_ffn,
+        residual_full,
+        gu_w,
+        down_w,
+        for_gate,
+        for_up,
+        mixed,
+        own_cot,
+        branch_own,
+        attn_gain_row,
+    )
+    input_grad, wall_grads, gain_grads, ffn_late = attention_backward(
         grad_attn,
         full_in,
         query_proj,
@@ -1692,22 +1969,12 @@
         grad_own,
         attn_gain_term,
         ffn_gain_term,
-    )
-    return (
-        outputs,
-        input_grad,
-        grad_query,
-        grad_key,
-        grad_value,
-        grad_w_out,
-        grad_w_gate,
-        grad_w_up,
-        grad_w_down,
-        gain_grads[0],
-        gain_grads[1],
-        gain_grads[2],
-        gain_grads[3],
-    )
+        ffn_left,
+    )
+    *results, gains_out = write_results(
+        ffn_early, ffn_late, wall_grads, outputs, input_grad, gain_grads
+    )
+    return (*results, *gains_out)
 
 
 def full_rows(piece):

time: 575 us -> 550 us (0.957)
  Pallas kernels: 486 us -> 531 us
  matrix products: 34.7 us -> 0 us
  local copies, waits for them, and re-layouts: 30.4 us -> 7.63 us
  starting transfers between devices: 6.25 us -> 0 us
    dot_general x9 -> x0, matrix products: 34.7 us -> none  [dotf(): lax.dot_general(left, right, (dims, ((), ())), preferred_element_type=F32)]
    pallas_call x2 -> x3, Pallas kernels: 192 us -> 219 us  [the longest x1 123 us: ffn_backward(): comm_call(body, 'ffn_backward', 4, (shape((tokens, width), BF), shape((ro...]
    pallas_call x1, Pallas kernels: 84.4 us -> 103 us  [attention_backward(): comm_call(body, 'attention_backward', 5, (shape((rows * 4, part), BF), sh...]
    unnamed x50 -> x0, local copies, waits for them, and re-layouts: 11.6 us -> none
    slice x12 -> x0, local copies, waits for them, and re-layouts: 9.24 us -> none  [the longest x2 5.8 us: plane_layer(): grad_w_down = ffn_back[:, 2].reshape(w_down.shape)]
  transfers between devices with their start and end apart: 2 -> 0, of which waited for: 1 -> 0; matrix products, arithmetic and copies ran while one was open for 2% -> 0% of each run, Pallas kernels for 34% -> 0%
where the time goes in v3:
time: 550 us; the launch traced here: 546 us
  Pallas kernels  531 us (97%)
  local copies, waits for them, and re-layouts  7.63 us (1%)
  other arithmetic  7.01 us (1%)
    pallas_call x1, Pallas kernels, attention_forward(): comm_call(body, 'attention_forward', 1, (shape((tokens, width), BF), shap...  138 us
    pallas_call x1, Pallas kernels, ffn_backward(): comm_call(body, 'ffn_backward', 4, (shape((tokens, width), BF), shape((ro...  123 us
    pallas_call x1, Pallas kernels, attention_backward(): comm_call(body, 'attention_backward', 5, (shape((rows * 4, part), BF), sh...  103 us
    pallas_call x1, Pallas kernels, ffn_forward(): comm_call(body, 'ffn_forward', 3, (shape((tokens, width), BF), shape((row...  86.9 us
    pallas_call x1, Pallas kernels, open_layer(): comm_call(body, 'open_layer', 0, (shape((tokens, width), BF), shape((quar...  70.3 us

profile of v3, /device:TPU:1, one launch (start us, length us, event | category | flops | bytes accessed | tf_op | source)
XLA Modules:
  0.0 546.2 jit_solution(3162357490299897536)
XLA Ops:
  0.7 0.8 reduce-window.8
  1.5 0.7 bitcast_subtract_fusion
  2.2 1.3 pad_maximum_fusion.2.refs_9_
  3.5 0.7 reshape.122
  4.3 0.1 mul.53
  4.4 0.1 mul.48
  4.4 0.1 iota_add_fusion.1
  4.5 0.1 add.69
  4.6 0.1 convert_reduce_fusion
  4.7 0.1 select_reduce_fusion
  4.8 0.1 iota_add_fusion
  4.9 0.1 add.75
  4.9 0.6 pad_add_fusion
  5.5 1.3 add.79.refs_6_.refs_12_
  6.9 1.0 copy.32.refs_5_.refs_11_
  7.9 1.9 fusion
  9.8 1.3 pad_maximum_fusion
  11.1 70.3 %open_layer.1 = (bf16[1024,2048]{1,0:T(8,128)(2,1)}, bf16[64,2048]{1,0:T(8,128)(2,1)}, bf16[64,2048]{1,0:T(8,128)(2,1)}, bf16[3,2048,128]{2,1,0:T(8,128)(2,1)}, ...) custom-call(bf16[256,512]{1,0:T(8,128)(2,1)} %refs_0_.1, ...), custom_call_target="tpu_custom_call" | custom-call | tf_op jit(solution)/shard_map/open_layer/pallas_call | solution.py:703
  81.4 0.8 slice.9
  82.2 1.5 fusion.1
  83.6 0.6 constant_dynamic-slice_fusion.refs_10_.refs_15_
  84.2 138.1 %attention_forward.1 = (bf16[1024,2048]{1,0:T(8,128)(2,1)}, f32[64,2048]{1,0:T(8,128)}, f32[64,2048]{1,0:T(8,128)}, bf16[2,2048,512]{2,1,0:T(8,128)(2,1)}, bf16[...) custom-call(f32[1024,128]{1,0:T(8,128)} %get-tuple-element.60.refs_0, ...), custom_call_target="tpu_custom_call" | custom-call | tf_op jit(solution)/shard_map/attention_forward/pallas_call | solution.py:1004
  222.3 86.9 %ffn_forward.1 = (bf16[1024,2048]{1,0:T(8,128)(2,1)}, bf16[256,512]{1,0:T(8,128)(2,1)}, f32[8,2048]{1,0:T(8,128)}, f32[1024,512]{1,0:T(8,128)}, f32[1024,512]{1,0:T(8,128)}, /*index=5*/bf16[1024,512]{1,0:T(8,128)(2,1)}) custom-call(bf16[1024,2048]{1,0:T(8,128)(2,1)} %get-tuple-element.68.refs_0_.refs_1_, ...), custom_call_target="tpu_custom_call" | custom-call | tf_op jit(solution)/shard_map/ffn_forward/pallas_call | solution.py:1110
  309.2 123.1 %ffn_backward.1 = (bf16[1024,2048]{1,0:T(8,128)(2,1)}, f32[64,2048]{1,0:T(8,128)}, f32[8,2048]{1,0:T(8,128)}, bf16[8,3,256,256]{3,2,1,0:T(8,128)(2,1)}, bf16[3,3,256,256]{3,2,1,0:T(8,128)(2,1)}) custom-call(bf16[1024,2048]{1,0:T(8,128)(2,1)} %get-tuple-element.73.refs_0_, bf16[1024,2048]{1,0:T(8,128)(2,1)} %get-tuple-element.68.refs_0_.refs_1_, ...), custom_call_target="tpu_custom_call" | custom-call | tf_op jit(solution)/shard_map/ffn_backward/pallas_call | solution.py:1325
  432.4 103.0 %attention_backward.1 = (bf16[256,512]{1,0:T(8,128)(2,1)}, bf16[8,4,128,128]{3,2,1,0:T(8,128)(2,1)}, f32[4,512]{1,0:T(4,128)}, bf16[8,3,256,256]{3,2,1,0:T(8,128)(2,1)}) custom-call(bf16[1024,2048]{1,0:T(8,128)(2,1)} %get-tuple-element.79.refs_0_, bf16[1024,2048]{1,0:T(8,128)(2,1)} %get-tuple-element.80.refs_1_, ...), custom_call_target="tpu_custom_call" | custom-call | tf_op jit(solution)/shard_map/attention_backward/pallas_call | solution.py:1781
  535.4 9.1 %write_results.1 = (bf16[256,512]{1,0:T(8,128)(2,1)}, bf16[256,512]{1,0:T(8,128)(2,1)}, f32[256,512]{1,0:T(8,128)}, f32[256,512]{1,0:T(8,128)}, f32[256,512]{1,0...) custom-call(bf16[8,3,256,256]{3,2,1,0:T(8,128)(2,1)} %get-tuple-elem, ...), custom_call_target="tpu_custom_call" | custom-call | tf_op jit(solution)/shard_map/write_results/pallas_call | solution.py:1403
  544.5 1.4 fusion.2
  (3 shorter events, 0.1 us)

commit v4 on v3

--- a/solution.py
+++ b/solution.py
@@ -2,6 +2,7 @@
 
 import jax
 import jax.numpy as jnp
+import numpy as np
 from jax import lax
 from jax.experimental import pallas as pl
 from jax.experimental.pallas import tpu as pltpu
@@ -26,7 +27,7 @@
 ANY = pl.BlockSpec(memory_space=pl.ANY)
 VMEM = pl.BlockSpec(memory_space=pltpu.VMEM)
 DMA = pltpu.SemaphoreType.DMA
-BIG_VMEM = 56 * 1024 * 1024
+BIG_VMEM = 60 * 1024 * 1024
 
 
 def place():
@@ -47,26 +48,32 @@
     return value + high * (3 - 2 * value)
 
 
-def plane_axes(me):
+def plane_axes(me, turn):
     z, y, x, k = me
-    a = x * (1 - k) + y * k
-    b = y * (1 - k) + x * k
+    a = x * (1 - turn) + y * turn
+    b = y * (1 - turn) + x * turn
 
     def slot(zp, ap, bp):
-        yp = bp * (1 - k) + ap * k
-        xp = ap * (1 - k) + bp * k
+        yp = bp * (1 - turn) + ap * turn
+        xp = ap * (1 - turn) + bp * turn
         return zp * 4 + yp * 2 + xp
 
-    dev_a = (z, y * (1 - k) + (1 - y) * k, (1 - x) * (1 - k) + x * k, k)
-    dev_b = (z, (1 - y) * (1 - k) + y * k, x * (1 - k) + (1 - x) * k, k)
+    dev_a = (z, y * (1 - turn) + (1 - y) * turn, (1 - x) * (1 - turn) + x * turn, k)
+    dev_b = (z, (1 - y) * (1 - turn) + y * turn, x * (1 - turn) + (1 - x) * turn, k)
     return a, b, slot, dev_a, dev_b
 
 
-def plane_neighbours(me):
-    z, y, x, k = me
-    up = z + 1 - 2 * (z // 3)
-    down = z - 1 + 2 * ((3 - z) // 3)
-    return [(z, 1 - y, x, k), (z, y, 1 - x, k)], up, down
+EVEN = ((0, 1),) * 4
+MORE_X = ((0, 1), (1, 1)) * 2
+ALL_X = ((1, 1),) * 4
+TURNS_OPEN = ALL_X
+TURNS_ATTENTION = (MORE_X, EVEN)
+TURNS_FFN_BACK = (EVEN, EVEN)
+TURNS_CLOSE = ALL_X
+
+
+def layer_axes(me, turns):
+    return [plane_axes(me, t0 + me[3] * (t1 - t0)) for t0, t1 in turns]
 
 
 def greet_plane(me, others=()):
@@ -91,11 +98,48 @@
 GATHER_SEMS = [DMA((16,)), DMA((4,)), DMA((4,)), DMA((4,)), DMA((8,))]
 
 
-def gather_plane(me, own_ref, view, sems, between=lambda step: None):
+DEAL_ORDER = (4, 1, 5, 2, 6, 3, 7)
+OPEN_RATE = 2
+DEALT_FIRST = 5
+FORWARD_RATE = 1
+BACK_RATE = 1
+CLOSE_FIRST = 0
+CLOSE_NEXT = 4
+SUM_LAG = 1
+BACK_LAG = 1
+CLOSE_LAG = 3
+CLOSE_RATE = 1
+
+
+class Trickle:
+    def __init__(self):
+        self.waiting = []
+
+    def add(self, copies):
+        self.waiting.extend(copies)
+
+    def tick(self, count=1):
+        for start in self.waiting[:count]:
+            start()
+        self.waiting = self.waiting[count:]
+
+    def flush(self):
+        self.tick(len(self.waiting))
+
+
+def gather_plane(
+    me,
+    own_ref,
+    view,
+    sems,
+    turns,
+    between=lambda step: None,
+    arrived=lambda step: None,
+    tick=lambda: None,
+):
     z, y, x, k = me
     recv, up_send, down_send, a_send, b_send = sems
-    a, b, slot, dev_a, dev_b = plane_axes(me)
-    own = slot(z, a, b)
+    axes = layer_axes(me, turns)
 
     def copy(src, index, send_sem, device):
         return pltpu.make_async_remote_copy(
@@ -108,10 +152,19 @@
         )
 
     def landed(index):
-        copy(view(index), index, a_send.at[0], dev_a).wait_recv()
+        copy(view(index), index, a_send.at[0], axes[0][3]).wait_recv()
+
+    def layer_landed(step):
+        tick()
+        a, b, slot, dev_a, dev_b = axes[step]
+        zp = near_first(step, z)
+        landed(slot(zp, a, 1 - b))
+        landed(slot(zp, 1 - a, 1 - b))
+        arrived(step)
 
     for step in range(5):
         if step < 4:
+            a, b, slot, dev_a, dev_b = axes[step]
             zp = near_first(step, z)
             index = slot(zp, a, b)
             if step == 0:
@@ -130,16 +183,19 @@
 
             copy(src, index, a_send.at[step], dev_a).start()
             copy(src, index, b_send.at[step], dev_b).start()
+            tick()
         if step > 0:
+            a, b, slot, dev_a, dev_b = axes[step - 1]
             index = slot(near_first(step - 1, z), 1 - a, b)
             landed(index)
             copy(view(index), index, b_send.at[3 + step], dev_b).start()
+            tick()
         between(step)
+        if step >= 2:
+            layer_landed(step - 2)
+    layer_landed(3)
     for step in range(4):
-        zp = near_first(step, z)
-        landed(slot(zp, a, 1 - b))
-        landed(slot(zp, 1 - a, 1 - b))
-    for step in range(4):
+        a, b, slot, dev_a, dev_b = axes[step]
         zp = near_first(step, z)
         for ap, number in ((a, step), (1 - a, 4 + step)):
             index = slot(zp, ap, b)
@@ -185,19 +241,31 @@
     lax.fori_loop(0, rows // strip, body, 0)
 
 
-def reduce_plane(me, terms, rows, scratch, produce, finish, after_terms=lambda: None):
+def reduce_plane(
+    me,
+    terms,
+    rows,
+    scratch,
+    turns,
+    produce,
+    finish,
+    after_terms=lambda: None,
+    tick=lambda: None,
+):
     z, y, x, k = me
     (from_b, to_a, from_a, to_z, from_low, from_high) = scratch[:6]
     (b_send, b_recv, a_send, a_recv, z_send, low_recv, high_recv) = scratch[6:]
-    a, b, slot, dev_a, dev_b = plane_axes(me)
+    axes = layer_axes(me, turns)[::-1]
     order = [near_first(step, z) for step in (3, 2, 1, 0)]
 
-    def start_of(zp, ap, bp):
-        return pl.multiple_of(slot(zp, ap, bp) * rows, rows)
-
-    def copy_b(zp, ap):
+    def start_of(step, ap, bp):
+        return pl.multiple_of(axes[step][2](order[step], ap, bp) * rows, rows)
+
+    def copy_b(step, flip):
+        a, b, slot, dev_a, dev_b = axes[step]
+        zp, ap = order[step], (1 - a if flip else a)
         return pltpu.make_async_remote_copy(
-            src_ref=terms.at[pl.ds(start_of(zp, ap, 1 - b), rows), :],
+            src_ref=terms.at[pl.ds(start_of(step, ap, 1 - b), rows), :],
             dst_ref=from_b.at[zp, ap],
             send_sem=b_send.at[zp * 2 + ap],
             recv_sem=b_recv.at[zp * 2 + ap],
@@ -205,7 +273,8 @@
             device_id_type=MESH,
         )
 
-    def copy_a(zp):
+    def copy_a(step):
+        zp, dev_a = order[step], axes[step][3]
         return pltpu.make_async_remote_copy(
             src_ref=to_a.at[zp],
             dst_ref=from_a.at[zp],
@@ -231,41 +300,47 @@
     def copy_down(zp):
         return copy_z(zp, from_high, high_recv, z - 1)
 
-    def mine(zp, ap, strip):
-        at = pl.ds(pl.multiple_of(start_of(zp, ap, b) + strip.start, STRIP), STRIP)
-        return terms[at, :].astype(F32)
-
-    for zp in order:
-        produce(zp)
-        for ap in (1 - a, a):
-            copy_b(zp, ap).start()
+    def mine(step, flip, strip):
+        a, b = axes[step][:2]
+        at = start_of(step, 1 - a if flip else a, b) + strip.start
+        return terms[pl.ds(pl.multiple_of(at, STRIP), STRIP), :].astype(F32)
+
+    for step in range(4):
+        produce(order[step])
+        for flip in (True, False):
+            copy_b(step, flip).start()
+        tick()
     after_terms()
 
-    for step in range(5):
+    for step in range(4 + SUM_LAG):
         if step < 4:
-            zp = order[step]
-            copy_b(zp, 1 - a).wait_recv()
-
-            def first(strip, zp=zp):
+            copy_b(step, True).wait_recv()
+
+            def first(strip, step=step):
+                zp, ap = order[step], 1 - axes[step][0]
                 to_a[zp, strip] = (
-                    mine(zp, 1 - a, strip) + from_b[zp, 1 - a, strip].astype(F32)
+                    mine(step, True, strip) + from_b[zp, ap, strip].astype(F32)
                 ).astype(BF)
 
             strips(rows, first)
-            copy_a(zp).start()
-        if step > 0:
-            zp = order[step - 1]
-            copy_b(zp, a).wait_recv()
-            copy_a(zp).wait_recv()
-
-            def own_sum(strip, zp=zp):
+            copy_a(step).start()
+            tick()
+        if step >= SUM_LAG:
+            done = step - SUM_LAG
+            tick()
+            copy_b(done, False).wait_recv()
+            copy_a(done).wait_recv()
+
+            def own_sum(strip, last=done):
+                zp, ap = order[last], axes[last][0]
                 return (
-                    mine(zp, a, strip)
-                    + from_b[zp, a, strip].astype(F32)
+                    mine(last, False, strip)
+                    + from_b[zp, ap, strip].astype(F32)
                     + from_a[zp, strip].astype(F32)
                 )
 
-            if step < 4:
+            if done < 3:
+                zp = order[done]
                 upward = zp > z
 
                 @pl.when(upward & (z > 0))
@@ -326,10 +401,10 @@
                     )
 
     def settle():
-        for zp in order:
-            copy_b(zp, 0).wait_send()
-            copy_b(zp, 1).wait_send()
-            copy_a(zp).wait_send()
+        for step in range(4):
+            copy_b(step, True).wait_send()
+            copy_b(step, False).wait_send()
+            copy_a(step).wait_send()
         for zp in order[:3]:
             copy_up(zp).wait_send()
 
@@ -432,22 +507,60 @@
     return raw * (1.0 / math.sqrt(HD)), allowed
 
 
-def open_layer(inputs, cotangent, w_query, w_key, w_value, w_out, w_gate, w_up, w_down, gains):
+def eye_mask():
+    return lax.broadcasted_iota(jnp.int32, (HD, HD), 0) == lax.broadcasted_iota(
+        jnp.int32, (HD, HD), 1
+    )
+
+
+def column_to_row(column, eye):
+    return jnp.sum(jnp.where(eye, column, 0.0), axis=0, keepdims=True)
+
+
+def row_to_column(row, eye):
+    return jnp.sum(jnp.where(eye, row, 0.0), axis=1, keepdims=True)
+
+
+def open_layer(
+    inputs,
+    cotangent,
+    w_query,
+    w_key,
+    w_value,
+    w_out,
+    w_gate,
+    w_up,
+    w_down,
+    query_gain,
+    key_gain,
+    attn_gain,
+    ffn_gain,
+    order,
+    lengths,
+    frequency,
+):
     rows, part = inputs.shape
     half = rows // 2
     quarter = half // 2
     tokens, width = 8 * half, 4 * part
     hidden = w_gate.shape[1]
+    down = hidden // 8
 
     def body(*refs):
-        (in_ref, cot_ref, wq_ref, wk_ref, wv_ref, wo_ref, wg_ref, wu_ref, wd_ref, gain_ref) = refs[:10]
-        (full_out, own_out, own_cot_ref, wqkv_ref, wout_ref, gains_ref, gu_out, d_out) = refs[10:18]
+        (in_ref, cot_ref, wq_ref, wk_ref, wv_ref, wo_ref, wg_ref, wu_ref, wd_ref) = refs[:9]
+        gain_parts = refs[9:13]
+        (order_ref, lengths_ref, frequency_ref) = refs[13:16]
+        (cos_ref, sin_ref, low_ref, high_ref, log_ref) = refs[27:32]
+        gain_ref = refs[-1]
+        refs = refs[:10] + refs[16:27] + refs[32:-1]
+        (full_out, own_out, own_cot_ref, wqkv_ref, wout_ref, gains_ref, gu_out, down_ref) = refs[10:18]
         (q_ref, k_ref, v_ref) = refs[18:21]
         (full_ref, shard, cot_half, qkv_raw, out_raw, gu_raw, d_raw) = refs[21:28]
         (qkv_stage, out_stage, gu_stage, d_stage) = refs[28:32]
         (load_sem, pair_send, pair_recv, local_sem, deal_send, deal_recv) = refs[32:38]
         (share_send, share_recv, gain_send, gain_recv, cot_sems, keep_sem) = refs[38:44]
-        gather_sems = refs[44:]
+        (down_send, down_recv) = refs[44:46]
+        gather_sems = refs[46:]
         me = z, y, x, k = place()
         ctx = own_tile(me)
         sibling = (z, y, x, 1 - k)
@@ -492,6 +605,9 @@
         first = pair_copy(in_ref, shard, 0)
         second = pair_copy(cot_ref, cot_half, 1)
 
+        for i, gain_part in enumerate(gain_parts):
+            gain_ref[i : i + 1, :] = gain_part[...]
+
         def gain_copy(xt, kt, number):
             return pltpu.make_async_remote_copy(
                 src_ref=gain_ref,
@@ -552,6 +668,7 @@
                 ),
             )
 
+        trickle = Trickle()
         stays = k == z // 2
         own_e = (z % 2) * 4 + y * 2 + k
 
@@ -569,17 +686,18 @@
                 out_stage[s] = out_raw[s].astype(BF)
 
             strips(2 * rows, round_out, 32)
-            for e in range(8):
-
-                @pl.when(jnp.logical_not(stays & (own_e == e)))
-                def _(e=e):
-                    for copy in deal(e):
-                        copy.start()
-
-                @pl.when(stays & (own_e == e))
-                def _(e=e):
-                    for i, (src, dst) in enumerate(deal_ends(e // 2, e % 2)):
-                        pltpu.make_async_copy(src, dst, deal_recv.at[i, ctx]).start()
+            trickle.add([lambda e=e: deal_start(e) for e in range(8)])
+
+        def deal_start(e):
+            @pl.when(jnp.logical_not(stays & (own_e == e)))
+            def _():
+                for copy in deal(e):
+                    copy.start()
+
+            @pl.when(stays & (own_e == e))
+            def _():
+                for i, (src, dst) in enumerate(deal_ends(e // 2, e % 2)):
+                    pltpu.make_async_copy(src, dst, deal_recv.at[i, ctx]).start()
 
         def cot_begin():
             second[0].wait_recv()
@@ -605,8 +723,38 @@
         keeps = [
             pltpu.make_async_copy(gu_stage.at[0], gu_out.at[0], keep_sem.at[0]),
             pltpu.make_async_copy(gu_stage.at[1], gu_out.at[1], keep_sem.at[1]),
-            pltpu.make_async_copy(d_stage, d_out, keep_sem.at[2]),
+            pltpu.make_async_copy(
+                d_stage.at[pl.ds(pl.multiple_of(ctx * down, down), down), :],
+                down_ref.at[:, pl.ds(pl.multiple_of(ctx * rows, rows), rows)],
+                keep_sem.at[2],
+            ),
         ]
+
+        def down_copy(t):
+            to = ctx + t - 8 * ((ctx + t) // 8)
+            return pltpu.make_async_remote_copy(
+                src_ref=d_stage.at[pl.ds(pl.multiple_of(to * down, down), down), :],
+                dst_ref=down_ref.at[:, pl.ds(pl.multiple_of(ctx * rows, rows), rows)],
+                send_sem=down_send.at[t],
+                recv_sem=down_recv.at[t],
+                device_id=(to // 2, to % 2, x, k),
+                device_id_type=MESH,
+            )
+
+        def down_landed(t):
+            c = ctx + 8 - t - 8 * ((ctx + 8 - t) // 8)
+            part_of = down_ref.at[:, pl.ds(pl.multiple_of(c * rows, rows), rows)]
+            pltpu.make_async_remote_copy(
+                src_ref=part_of,
+                dst_ref=part_of,
+                send_sem=down_send.at[t],
+                recv_sem=down_recv.at[t],
+                device_id=sibling,
+                device_id_type=MESH,
+            ).wait_recv()
+
+        def deal_down():
+            trickle.add([lambda t=t: down_copy(t).start() for t in DEAL_ORDER])
 
         def round_up(i):
             loads[4 + i].wait()
@@ -626,14 +774,61 @@
             strips(hidden, work, 128)
             keeps[2].start()
 
+        def positions():
+            blocks = order_ref.shape[1]
+            square = lax.broadcasted_iota(jnp.int32, (blocks, blocks), 0)
+            square = square == lax.broadcasted_iota(jnp.int32, (blocks, blocks), 1)
+            column = row_to_column(order_ref[...].astype(F32), square)
+            lane = lax.broadcasted_iota(jnp.int32, (1, 2 * tokens), 1)
+            other = (lane >= tokens).astype(jnp.int32)
+            core = k + other - 2 * k * other
+            lane = lane - tokens * other
+            in_half = lane & (half - 1)
+            block_rows = 2 * tokens // blocks
+            block = (lane - in_half) // half * (2 * half // block_rows)
+            block = block + core * (half // block_rows)
+            block = block + (in_half - (in_half & (block_rows - 1))) // block_rows
+            match = lax.broadcasted_iota(jnp.int32, (blocks, 2 * tokens), 0) == block
+            first_of = jnp.sum(jnp.where(match, column, 0.0), axis=0, keepdims=True) * block_rows
+            logical = first_of + (in_half & (block_rows - 1)).astype(F32)
+            log_ref[...] = logical
+            own = logical[:, :tokens]
+            begin = jnp.zeros_like(own)
+            end = jnp.zeros((1, 1), F32)
+            for j in range(lengths_ref.shape[1]):
+                length = lengths_ref[:, j : j + 1].astype(F32)
+                end = end + length
+                begin = begin + jnp.where(own >= end, length, 0.0)
+            eye = eye_mask()
+            for i in range(tokens // HD):
+                piece = slice(i * HD, (i + 1) * HD)
+                low = row_to_column(begin[:, piece], eye)
+                high = row_to_column(own[:, piece], eye)
+                low_ref[piece, :] = low
+                high_ref[piece, :] = high
+                angles = (high - low) * frequency_ref[...]
+                cos_ref[piece, :] = jnp.cos(angles)
+                sine = jnp.sin(angles)
+                left = lax.broadcasted_iota(jnp.int32, (HD, HD), 1) < HD // 2
+                sin_ref[piece, :] = jnp.where(left, -sine, sine)
+
         between = [
             deal_all,
-            lambda: (cot_begin(), round_up(0)),
-            lambda: round_up(1),
-            round_down,
+            lambda: (cot_begin(), round_down(), deal_down()),
+            lambda: (round_up(0), round_up(1)),
+            positions,
             lambda: None,
         ]
-        gather_plane(me, shard, view, gather_sems, lambda step: between[step]())
+        gather_plane(
+            me,
+            shard,
+            view,
+            gather_sems,
+            TURNS_OPEN,
+            lambda step: between[step](),
+            tick=lambda: trickle.tick(OPEN_RATE),
+        )
+        trickle.flush()
 
         def deal_wait(c):
             at = slice(c * 2 * HD, c * 2 * HD + HD)
@@ -698,6 +893,9 @@
         cot_local.wait()
         for keep in (*keeps, full_keep, own_keep):
             keep.wait()
+        for t in range(1, 8):
+            down_landed(t)
+            down_copy(t).wait_send()
 
     shape = jax.ShapeDtypeStruct
     return comm_call(
@@ -712,13 +910,18 @@
             shape((HD, width), BF),
             shape((4, width), F32),
             shape((2, rows, hidden), BF),
-            shape((hidden, rows), BF),
+            shape((down, width), BF),
             shape((tokens, HD), F32),
             shape((tokens, HD), F32),
             shape((tokens, HD), BF),
+            shape((tokens, HD), F32),
+            shape((tokens, HD), F32),
+            shape((tokens, 1), F32),
+            shape((tokens, 1), F32),
+            shape((1, 2 * tokens), F32),
         ),
-        [ANY] * 10,
-        (ANY, ANY, ANY, VMEM, VMEM, ANY, ANY, ANY, VMEM, VMEM, VMEM),
+        [*[ANY] * 9, *[VMEM] * 7],
+        (ANY, ANY, ANY, VMEM, VMEM, ANY, ANY, ANY, VMEM, VMEM, VMEM, *[VMEM] * 5),
         [
             pltpu.VMEM((tokens, width), BF),
             pltpu.VMEM((half, 2 * part), BF),
@@ -743,23 +946,29 @@
             DMA((3,)),
             DMA((3,)),
             DMA((5,)),
+            DMA((8,)),
+            DMA((8,)),
             *GATHER_SEMS,
+            pltpu.VMEM((4, part), F32),
         ],
-    )(inputs, cotangent, w_query, w_key, w_value, w_out, w_gate, w_up, w_down, gains)
-
-
-def eye_mask():
-    return lax.broadcasted_iota(jnp.int32, (HD, HD), 0) == lax.broadcasted_iota(
-        jnp.int32, (HD, HD), 1
-    )
-
-
-def column_to_row(column, eye):
-    return jnp.sum(jnp.where(eye, column, 0.0), axis=0, keepdims=True)
-
-
-def row_to_column(row, eye):
-    return jnp.sum(jnp.where(eye, row, 0.0), axis=1, keepdims=True)
+    )(
+        inputs,
+        cotangent,
+        w_query,
+        w_key,
+        w_value,
+        w_out,
+        w_gate,
+        w_up,
+        w_down,
+        query_gain,
+        key_gain,
+        attn_gain,
+        ffn_gain,
+        order,
+        lengths,
+        frequency,
+    )
 
 
 def plane_peer(me, i):
@@ -781,7 +990,7 @@
     pl.semaphore_wait(barrier, 15 + len(others))
 
 
-def sum_over_plane(me, slots, send, recv):
+def sum_begin(me, slots, send, recv):
     own = me[0] * 4 + me[1] * 2 + me[2]
 
     def copy(i, slot):
@@ -798,27 +1007,29 @@
         copy(i, own).start()
         return carry
 
-    lax.fori_loop(1, 16, begin, 0)
-
     def landed(i, carry):
         copy(i, plane_peer(me, i)[0]).wait_recv()
         return carry
 
-    lax.fori_loop(1, 16, landed, 0)
-
     def sent(i, carry):
         copy(i, own).wait_send()
         return carry
 
-    lax.fori_loop(1, 16, sent, 0)
-    total = slots[0]
-    for i in range(1, 16):
-        total = total + slots[i]
-    return total
+    lax.fori_loop(1, 16, begin, 0)
+
+    def end():
+        lax.fori_loop(1, 16, landed, 0)
+        lax.fori_loop(1, 16, sent, 0)
+        total = slots[0]
+        for i in range(1, 16):
+            total = total + slots[i]
+        return total
+
+    return end
 
 
 def attention_forward(
-    query, key, value, tables, bounds, logical, source, out_weight, gains, attn_gain, gu_stage, d_stage
+    query, key, value, tables, bounds, logical, source, out_weight, gains, gu_stage, down_own
 ):
     tokens, width = query.shape[0], source.shape[1]
     rows = tokens // 16
@@ -827,14 +1038,16 @@
     part = width // 8
 
     def body(*refs):
-        (q_in, k_in, v_in, cos_ref, sin_ref, low_ref, high_ref, log_ref, source_ref, wout_ref, gain_ref, attn_ref) = refs[:12]
-        (gu_ref, d_ref) = refs[12:14]
-        (full_ref, own_ref, branch_ref, wgu_ref, wd_ref, qrot_ref, keys_ref, values_ref, o_ref, lse_ref, scale_ref) = refs[14:25]
-        (terms, shard, slots, tot_send, tot_recv, pair_send, pair_recv, local) = refs[25:33]
-        (ffn_send, ffn_recv, share_send, share_recv, ffn_local) = refs[33:38]
-        rest = refs[38:]
+        (q_in, k_in, v_in, cos_ref, sin_ref, low_ref, high_ref, log_ref, source_ref, wout_ref, gain_ref) = refs[:11]
+        (gu_ref, d_ref) = refs[11:13]
+        (full_ref, own_ref, branch_ref, wgu_ref, d_other_ref, qrot_ref, keys_ref, values_ref, o_ref, lse_ref, scale_ref) = refs[13:24]
+        (terms, shard, slots, tot_send, tot_recv, pair_send, pair_recv, local) = refs[24:32]
+        (ffn_send, ffn_recv, share_send, share_recv, ffn_local) = refs[32:37]
+        rest = refs[37:]
         me = z, y, x, k = place()
         ctx = own_tile(me)
+        head_at = pl.ds(pl.multiple_of((x * 8 + ctx) * HD, HD), HD)
+        query_gain, key_gain = gain_ref[0:1, head_at], gain_ref[1:2, head_at]
         sibling = (z, y, x, 1 - k)
         barrier = pltpu.get_barrier_semaphore()
         plane_greet_all(me, [sibling])
@@ -862,48 +1075,34 @@
         v_copy = pair(v_in, values_ref.at[other_half, :], 0)
         v_copy.start()
 
-        def ffn_copy(t):
+        def ffn_copy(t, i):
             to = ctx + t - 8 * ((ctx + t) // 8)
-            device = (to // 2, to % 2, x, k)
             at = pl.ds(pl.multiple_of(to * hidden, hidden), hidden)
             from_at = pl.ds(pl.multiple_of(ctx * part, part), part)
-            ends = (
-                (gu_ref.at[:, :, at], wgu_ref.at[:, from_at, :hidden]),
-                (d_ref.at[at, :], wd_ref.at[:hidden, from_at]),
+            return pltpu.make_async_remote_copy(
+                src_ref=gu_ref.at[i, :, at],
+                dst_ref=wgu_ref.at[i, from_at, :hidden],
+                send_sem=ffn_send.at[i, t],
+                recv_sem=ffn_recv.at[i, t],
+                device_id=(to // 2, to % 2, x, k),
+                device_id_type=MESH,
             )
-            return [
-                pltpu.make_async_remote_copy(
-                    src_ref=src,
-                    dst_ref=dst,
-                    send_sem=ffn_send.at[i, t],
-                    recv_sem=ffn_recv.at[i, t],
-                    device_id=device,
-                    device_id_type=MESH,
-                )
-                for i, (src, dst) in enumerate(ends)
-            ]
-
-        def ffn_ends(c):
+
+        def ffn_ends(t):
+            c = ctx + 8 - t - 8 * ((ctx + 8 - t) // 8)
             at = pl.ds(pl.multiple_of(c * part, part), part)
-            return (
-                (wgu_ref.at[:, at, :hidden], wgu_ref.at[:, at, hidden:]),
-                (wd_ref.at[:hidden, at], wd_ref.at[hidden:, at]),
-            )
+            return wgu_ref.at[:, at, :hidden], wgu_ref.at[:, at, hidden:]
 
         own_at = pl.ds(pl.multiple_of(ctx * hidden, hidden), hidden)
-        ffn_own = [
-            pltpu.make_async_copy(src, dst[0], ffn_local.at[i])
-            for i, (src, dst) in enumerate(
-                zip((gu_ref.at[:, :, own_at], d_ref.at[own_at, :]), ffn_ends(ctx), strict=True)
-            )
-        ]
-        for copy in ffn_own:
-            copy.start()
-
-        total = sum_over_plane(me, slots, tot_send, tot_recv)
-        for t in range(1, 8):
-            for copy in ffn_copy(t):
-                copy.start()
+        ffn_own = pltpu.make_async_copy(gu_ref.at[:, :, own_at], ffn_ends(0)[0], ffn_local)
+        ffn_own.start()
+        down_copy = pair(d_ref, d_other_ref, 2)
+        down_copy.start()
+
+        total = sum_begin(me, slots, tot_send, tot_recv)()
+        trickle = Trickle()
+        trickle.add([lambda t=t, i=i: ffn_copy(t, i).start() for t in DEAL_ORDER for i in range(2)])
+        trickle.tick(DEALT_FIRST)
         scales = lax.rsqrt(total / width + EPSILON)
         scale_ref[...] = scales
 
@@ -913,13 +1112,13 @@
         for i in range(8):
             piece = slice(i * HD, (i + 1) * HD)
             factor = row_to_column(scales[8 + i : 9 + i, :], eye)
-            keys_ref[piece, :] = rotated(k_in[piece, :] * factor * gain_ref[1:2, :], piece).astype(BF)
+            keys_ref[piece, :] = rotated(k_in[piece, :] * factor * key_gain, piece).astype(BF)
         k_copy = pair(keys_ref.at[:tokens, :], keys_ref.at[other_half, :], 1)
         k_copy.start()
         for i in range(8):
             piece = slice(i * HD, (i + 1) * HD)
             factor = row_to_column(scales[i : i + 1, :], eye)
-            qrot_ref[piece, :] = rotated(q_in[piece, :] * factor * gain_ref[0:1, :], piece).astype(BF)
+            qrot_ref[piece, :] = rotated(q_in[piece, :] * factor * query_gain, piece).astype(BF)
         v_copy.wait()
         k_copy.wait()
 
@@ -942,63 +1141,69 @@
 
         def finish(strip, total):
             branch_ref[strip] = total
-            h = source_ref[strip].astype(F32) + total * row_scale(total) * attn_ref[...]
+            h = source_ref[strip].astype(F32) + total * row_scale(total) * gain_ref[2:3, :]
             own_ref[strip] = h
             shard[strip] = h.astype(BF)
 
-        settle = reduce_plane(me, terms, rows, rest[:N_REDUCE], produce, finish)
+        settle = reduce_plane(
+            me,
+            terms,
+            rows,
+            rest[:N_REDUCE],
+            TURNS_ATTENTION[0],
+            produce,
+            finish,
+            tick=lambda: trickle.tick(FORWARD_RATE),
+        )
         view = gather_view(full_ref, rows)
         keep = pltpu.make_async_copy(shard, view(own), local)
         keep.start()
 
         def share(t):
-            c = ctx + 8 - t - 8 * ((ctx + 8 - t) // 8)
-            return [
+            src, dst = ffn_ends(t)
+            return pltpu.make_async_remote_copy(
+                src_ref=src,
+                dst_ref=dst,
+                send_sem=share_send.at[t],
+                recv_sem=share_recv.at[t],
+                device_id=sibling,
+                device_id_type=MESH,
+            )
+
+        def ffn_landed(t):
+            for i in range(2):
+                src = ffn_ends(t)[0].at[i]
                 pltpu.make_async_remote_copy(
                     src_ref=src,
-                    dst_ref=dst,
-                    send_sem=share_send.at[i, t],
-                    recv_sem=share_recv.at[i, t],
-                    device_id=sibling,
-                    device_id_type=MESH,
-                )
-                for i, (src, dst) in enumerate(ffn_ends(c))
-            ]
-
-        def ffn_landed(t):
-            c = ctx + 8 - t - 8 * ((ctx + 8 - t) // 8)
-            for i, ends in enumerate(ffn_ends(c)):
-                pltpu.make_async_remote_copy(
-                    src_ref=ends[0],
-                    dst_ref=ends[0],
+                    dst_ref=src,
                     send_sem=ffn_send.at[i, t],
                     recv_sem=ffn_recv.at[i, t],
                     device_id=sibling,
                     device_id_type=MESH,
                 ).wait_recv()
 
-        def between(step):
-            for t in (2 * step, 2 * step + 1):
-                if t == 0:
-                    for copy in ffn_own:
-                        copy.wait()
-                elif t < 8:
-                    ffn_landed(t)
-                if t < 8:
-                    for copy in share(t):
-                        copy.start()
-
-        gather_plane(me, shard, view, rest[N_REDUCE:])
-        for step in range(4):
-            between(step)
+        gather_plane(
+            me,
+            shard,
+            view,
+            rest[N_REDUCE:],
+            TURNS_ATTENTION[1],
+            tick=lambda: trickle.tick(FORWARD_RATE),
+        )
+        trickle.flush()
+        ffn_own.wait()
+        share(0).start()
+        for t in DEAL_ORDER:
+            ffn_landed(t)
+            share(t).start()
         keep.wait()
         settle()
         for t in range(8):
-            for copy in share(t):
-                copy.wait()
-            if t > 0:
-                for copy in ffn_copy(t):
-                    copy.wait_send()
+            share(t).wait()
+            for i in range(2):
+                if t > 0:
+                    ffn_copy(t, i).wait_send()
+        down_copy.wait()
 
     shape = jax.ShapeDtypeStruct
     return comm_call(
@@ -1010,7 +1215,7 @@
             shape((rows, width), F32),
             shape((rows, width), F32),
             shape((2, width, 2 * hidden), BF),
-            shape((2 * hidden, width), BF),
+            shape((hidden, width), BF),
             shape((tokens, HD), BF),
             shape((2 * tokens, HD), BF),
             shape((2 * tokens, HD), BF),
@@ -1018,7 +1223,7 @@
             shape((tokens, 1), F32),
             shape((16, HD), F32),
         ),
-        [VMEM] * 12 + [ANY, ANY],
+        [VMEM] * 11 + [ANY, ANY],
         (ANY, VMEM, VMEM, ANY, ANY, VMEM, VMEM, VMEM, VMEM, VMEM, VMEM),
         [
             pltpu.VMEM((tokens, width), BF),
@@ -1026,30 +1231,30 @@
             pltpu.VMEM((16, 16, HD), F32),
             DMA((16,)),
             DMA((16,)),
-            DMA((2,)),
-            DMA((2,)),
+            DMA((3,)),
+            DMA((3,)),
             DMA,
             DMA((2, 8)),
             DMA((2, 8)),
-            DMA((2, 8)),
-            DMA((2, 8)),
-            DMA((2,)),
+            DMA((8,)),
+            DMA((8,)),
+            DMA,
             *reduce_scratch(rows, width),
             *GATHER_SEMS,
         ],
-    )(query, key, value, *tables, *bounds, logical, source, out_weight, gains, attn_gain, gu_stage, d_stage)
+    )(query, key, value, *tables, *bounds, logical, source, out_weight, gains, gu_stage, down_own)
 
 
 def ffn_forward(source, gu_w, down_w, residual, cotangent, gain):
     tokens, width = source.shape
     rows, group = tokens // 16, tokens // 4
-    hidden = down_w.shape[0]
+    hidden = 2 * down_w[0].shape[0]
 
     def body(*refs):
-        (h_any, gu_any, d_any, res_ref, cot_ref, gain_ref) = refs[:6]
-        (full_ref, out_ref, gg_ref, for_gate_ref, for_up_ref, m_ref) = refs[6:12]
-        (hs, gu, dw, terms, shard, result, load_sem, local, out_send, out_recv) = refs[12:22]
-        scratch = refs[22:]
+        (h_any, gu_any, d_any, d_any2, res_ref, cot_ref, gain_ref) = refs[:7]
+        (full_ref, out_ref, gg_ref, for_gate_ref, for_up_ref, m_ref) = refs[7:13]
+        (hs, gu, dw, terms, shard, result, load_sem, local, out_send, out_recv) = refs[13:23]
+        scratch = refs[23:]
         me = z, y, x, k = place()
 
         def h_load(zp):
@@ -1058,10 +1263,12 @@
 
         order = [near_first(step, z) for step in (3, 2, 1, 0)]
         gu_load = pltpu.make_async_copy(gu_any, gu, load_sem.at[4])
-        d_load = pltpu.make_async_copy(d_any, dw, load_sem.at[5])
-        h_load(order[0]).start()
-        gu_load.start()
-        d_load.start()
+        d_loads = [
+            pltpu.make_async_copy(d_any, dw.at[: hidden // 2, :], load_sem.at[5]),
+            pltpu.make_async_copy(d_any2, dw.at[hidden // 2 :, :], load_sem.at[6]),
+        ]
+        for load in (h_load(order[0]), gu_load, *d_loads):
+            load.start()
         for zp in order[1:]:
             h_load(zp).start()
         greet_plane(me, pair_devices(me))
@@ -1083,15 +1290,16 @@
             terms[at, :] = jnp.dot(mixed, dw[...], preferred_element_type=F32).astype(BF)
 
         def finish(strip, total):
-            gain_row = gain_ref[...]
+            gain_row = gain_ref[3:4, :]
             out = res_ref[strip] + total * row_scale(total) * gain_row
             result[strip] = out.astype(BF)
             back, term = norm_back_strip(cot_ref[strip].astype(F32), total, gain_row)
             gg_ref[...] += term
             shard[strip] = back.astype(BF)
 
-        d_load.wait()
-        settle = reduce_plane(me, terms, rows, scratch[:N_REDUCE], produce, finish)
+        for load in d_loads:
+            load.wait()
+        settle = reduce_plane(me, terms, rows, scratch[:N_REDUCE], EVEN, produce, finish)
         view = gather_view(full_ref, rows)
         keep = pltpu.make_async_copy(shard, view(me[0] * 4 + me[1] * 2 + me[2]), local)
         keep.start()
@@ -1099,7 +1307,7 @@
         for copy in copies:
             copy.start()
         own.start()
-        gather_plane(me, shard, view, scratch[N_REDUCE:])
+        gather_plane(me, shard, view, scratch[N_REDUCE:], EVEN)
         keep.wait()
         settle()
         own.wait()
@@ -1119,7 +1327,7 @@
             shape((tokens, hidden), F32),
             shape((tokens, hidden), BF),
         ),
-        [ANY, ANY, ANY, VMEM, VMEM, VMEM],
+        [ANY, ANY, ANY, ANY, VMEM, VMEM, VMEM],
         (ANY, ANY, VMEM, VMEM, VMEM, VMEM),
         [
             pltpu.VMEM((tokens, width), BF),
@@ -1128,43 +1336,48 @@
             pltpu.VMEM((tokens, width), BF),
             pltpu.VMEM((rows, width), BF),
             pltpu.VMEM((rows, width), BF),
-            DMA((6,)),
+            DMA((7,)),
             DMA,
             DMA((3,)),
             DMA((4,)),
             *reduce_scratch(rows, width),
             *GATHER_SEMS,
         ],
-    )(source, gu_w, down_w, residual, cotangent, gain)
-
-
-EARLY = 4
-
-
-def grad_copy(me, src, dst, send, recv, t):
+    )(source, gu_w, *down_w, residual, cotangent, gain)
+
+
+EARLY = 5
+GRADS_FIRST = 6
+
+
+def grad_copies(me, src, dst, send, recv, t):
     ctx = own_tile(me)
     to = ctx + t - 8 * ((ctx + t) // 8)
-    return pltpu.make_async_remote_copy(
-        src_ref=src,
-        dst_ref=dst.at[ctx],
-        send_sem=send.at[t],
-        recv_sem=recv.at[t],
-        device_id=(to // 2, to % 2, me[2], me[3]),
-        device_id_type=MESH,
-    )
+    return [
+        pltpu.make_async_remote_copy(
+            src_ref=src.at[i],
+            dst_ref=dst.at[ctx, i],
+            send_sem=send.at[t, i],
+            recv_sem=recv.at[t, i],
+            device_id=(to // 2, to % 2, me[2], me[3]),
+            device_id_type=MESH,
+        )
+        for i in range(3)
+    ]
 
 
 def grad_landed(me, dst, send, recv, t):
     ctx = own_tile(me)
     c = ctx + 8 - t - 8 * ((ctx + 8 - t) // 8)
-    pltpu.make_async_remote_copy(
-        src_ref=dst.at[c],
-        dst_ref=dst.at[c],
-        send_sem=send.at[t],
-        recv_sem=recv.at[t],
-        device_id=(me[0], me[1], me[2], 1 - me[3]),
-        device_id_type=MESH,
-    ).wait_recv()
+    for i in range(3):
+        pltpu.make_async_remote_copy(
+            src_ref=dst.at[c, i],
+            dst_ref=dst.at[c, i],
+            send_sem=send.at[t, i],
+            recv_sem=recv.at[t, i],
+            device_id=(me[0], me[1], me[2], 1 - me[3]),
+            device_id_type=MESH,
+        ).wait_recv()
 
 
 def ctx_greet(me, others):
@@ -1184,21 +1397,27 @@
     pl.semaphore_wait(barrier, 8 + len(others))
 
 
-def ffn_backward(grad_ffn, source, gu_w, down_w, for_gate, for_up, mixed, cotangent, branch, gain):
+def ffn_backward(
+    grad_ffn, source, gu_w, down_w, for_gate, for_up, mixed, cotangent, branch, gain, attention
+):
     tokens, width = grad_ffn.shape
     rows, group = tokens // 16, tokens // 4
-    hidden = down_w.shape[0]
+    hidden = 2 * down_w[0].shape[0]
     part = hidden // 2
     across = (((0,), (0,)), ((), ()))
     turned = (((1,), (1,)), ((), ()))
+    scaling = 1.0 / math.sqrt(HD)
 
     def body(*refs):
-        (df_any, h_any, gu_any, d_any, fg_any, fu_any, m_any, cot_ref, branch_ref, gain_ref) = refs[:10]
-        (full_ref, own_ref, gg_ref, in_ref, rest_ref) = refs[10:15]
-        (df, hs, gu, dw, fg, fu, ms, dgu, terms, shard) = refs[15:25]
-        (mine, to_core, from_core, to_ctx) = refs[25:29]
-        (load_sem, local, core_send, core_recv, grad_send, grad_recv, rest_sem) = refs[29:36]
-        scratch = refs[36:]
+        (df_any, h_any, gu_any, d_any, d_any2, fg_any, fu_any, m_any, cot_ref, branch_ref, gain_ref) = refs[:11]
+        (wout_ref, qrot_ref, keys_ref, values_ref, o_ref, lse_ref, low_ref, high_ref, log_ref) = refs[11:20]
+        (full_ref, own_ref, gg_ref, in_ref, rest_ref, dq_ref, dk_ref, dv_ref) = refs[20:28]
+        (df, hs, gu, dw, fg, fu, ms, dgu, terms, shard) = refs[28:38]
+        (to_core, from_core, to_ctx) = refs[38:41]
+        (da, dk_all, dv_all, pair_out, pair_in) = refs[41:46]
+        (load_sem, local, core_send, core_recv, grad_send, grad_recv, rest_sem) = refs[46:53]
+        (da_sem, pair_send, pair_recv) = refs[53:56]
+        scratch = refs[56:]
         me = z, y, x, k = place()
         ctx = own_tile(me)
         order = [near_first(step, z) for step in (3, 2, 1, 0)]
@@ -1210,11 +1429,12 @@
                 for i, (src, dst) in enumerate(((df_any, df), (fg_any, fg), (fu_any, fu)))
             ]
 
-        d_load = pltpu.make_async_copy(d_any, dw, load_sem.at[3, 0])
+        d_load = pltpu.make_async_copy(d_any, dw.at[:part, :], load_sem.at[3, 0])
+        d_load2 = pltpu.make_async_copy(d_any2, dw.at[part:, :], load_sem.at[4, 0])
         gu_load = pltpu.make_async_copy(gu_any, gu, load_sem.at[3, 1])
         h_load = pltpu.make_async_copy(h_any, hs, load_sem.at[3, 2])
         m_load = pltpu.make_async_copy(m_any, ms, load_sem.at[3, 3])
-        for load in (*group_load(order[0]), d_load, gu_load):
+        for load in (*group_load(order[0]), d_load, d_load2, gu_load):
             load.start()
         for zp in order[1:]:
             for load in group_load(zp):
@@ -1225,6 +1445,7 @@
         ctx_greet(me, [sibling])
         gg_ref[...] = jnp.zeros_like(gg_ref)
         d_load.wait()
+        d_load2.wait()
 
         def produce(zp):
             at = pl.ds(pl.multiple_of(zp * group, group), group)
@@ -1243,7 +1464,7 @@
         def finish(strip, total):
             grad = cot_ref[strip].astype(F32) + total
             own_ref[strip] = grad
-            back, term = norm_back_strip(grad, branch_ref[strip], gain_ref[...])
+            back, term = norm_back_strip(grad, branch_ref[strip], gain_ref[2:3, :])
             gg_ref[...] += term
             shard[strip] = back.astype(BF)
 
@@ -1257,67 +1478,160 @@
                 device_id_type=MESH,
             )
 
-        def compute(t):
+        parts = (*DEAL_ORDER, 0)
+
+        def compute(n):
+            t = parts[n]
             c = ctx + t - 8 * ((ctx + t) // 8)
             at = pl.ds(pl.multiple_of(c * part, part), part)
             up_like = lax.dot_general(hs[:, at], dgu[...], across, preferred_element_type=F32)
             down_like = lax.dot_general(ms[...], df[:, at], across, preferred_element_type=F32)
-            slot = t % 2
             for i in range(2):
-                mine[slot, i] = up_like[:, 2 * i * part : (2 * i + 1) * part]
+                to_ctx[t, i] = up_like[:, 2 * i * part : (2 * i + 1) * part].astype(BF)
                 to_core[t, i] = up_like[:, (2 * i + 1) * part : (2 * i + 2) * part].astype(BF)
-            mine[slot, 2] = down_like[:part]
+            to_ctx[t, 2] = down_like[:part].astype(BF)
             to_core[t, 2] = down_like[part:].astype(BF)
             core_copy(t).start()
 
-        def send(t):
+        trickle = Trickle()
+
+        def send(n):
+            t = parts[n]
             core_copy(t).wait_recv()
-            to_ctx[t] = (mine[t % 2] + from_core[t].astype(F32)).astype(BF)
+            to_ctx[t] = (to_ctx[t].astype(F32) + from_core[t].astype(F32)).astype(BF)
             if t == 0:
                 pltpu.make_async_copy(to_ctx.at[0], in_ref.at[ctx], rest_sem.at[0]).start()
-            elif t <= EARLY:
-                grad_copy(me, to_ctx.at[t], in_ref, grad_send, grad_recv, t).start()
+            elif n < EARLY:
+                trickle.add(
+                    [
+                        copy.start
+                        for copy in grad_copies(me, to_ctx.at[t], in_ref, grad_send, grad_recv, t)
+                    ]
+                )
             else:
                 pltpu.make_async_copy(
-                    to_ctx.at[t], rest_ref.at[t - EARLY - 1], rest_sem.at[t - EARLY]
+                    to_ctx.at[t], rest_ref.at[n - EARLY], rest_sem.at[n - EARLY + 1]
                 ).start()
 
-        def grads(first, last):
-            for t in range(first, last):
-                compute(t)
-                if t > 0:
-                    send(t - 1)
+        begun = []
+
+        def next_part():
+            n = len(begun)
+            begun.append(n)
+            if n < 8:
+                compute(n)
+            if BACK_LAG <= n < 8 + BACK_LAG:
+                send(n - BACK_LAG)
+
+        def tick():
+            if begun:
+                next_part()
+            trickle.tick(BACK_RATE)
+
+        def da_load(step):
+            at = pl.ds(pl.multiple_of(near_first(step, z) * group, group), group)
+            return pltpu.make_async_copy(full_ref.at[at, :], da.at[step % 2], da_sem.at[step % 2])
+
+        def attend_back(step):
+            at = pl.ds(pl.multiple_of(near_first(step, z) * group, group), group)
+            da_load(step).wait()
+            grad = lax.dot_general(
+                da[step % 2], wout_ref[...], turned, preferred_element_type=F32
+            ).astype(BF)
+            delta = jnp.sum(grad.astype(F32) * o_ref[at, :], axis=1, keepdims=True)
+            q, low, high, lse = qrot_ref[at, :], low_ref[at, :], high_ref[at, :], lse_ref[at, :]
+            dq_ref[at, :] = jnp.zeros((group, HD), F32)
+
+            def work(key_at):
+                key_part = keys_ref[key_at, :]
+                raw, allowed = masked_scores(q, key_part, low, high, log_ref[:, key_at])
+                weights = jnp.where(allowed, jnp.exp(raw - lse), 0.0)
+                dp = lax.dot_general(
+                    grad, values_ref[key_at, :], turned, preferred_element_type=F32
+                )
+                ds = (weights * (dp - delta)).astype(BF)
+                dq_ref[at, :] += jnp.dot(ds, key_part, preferred_element_type=F32) * scaling
+                dk_all[key_at, :] += (
+                    lax.dot_general(ds, q, across, preferred_element_type=F32) * scaling
+                )
+                dv_all[key_at, :] += lax.dot_general(
+                    weights.astype(BF), grad, across, preferred_element_type=F32
+                )
+
+            strips(2 * tokens, work, tokens)
+
+        def arrived(step):
+            if step == 0:
+                keep.wait()
+                dk_all[...] = jnp.zeros_like(dk_all)
+                dv_all[...] = jnp.zeros_like(dv_all)
+            da_load(step).start()
+            if step > 0:
+                attend_back(step - 1)
+
+        def pair(n):
+            return pltpu.make_async_remote_copy(
+                src_ref=pair_out.at[n],
+                dst_ref=pair_in.at[n],
+                send_sem=pair_send.at[n],
+                recv_sem=pair_recv.at[n],
+                device_id=sibling,
+                device_id_type=MESH,
+            )
 
         def after_terms():
             h_load.wait()
             m_load.wait()
-            grads(0, 3)
-
-        between = [
-            lambda: grads(3, 5),
-            lambda: grads(5, 6),
-            lambda: grads(6, 7),
-            lambda: grads(7, 8),
-            lambda: send(7),
-        ]
+            for _ in range(GRADS_FIRST):
+                next_part()
+
         gu_load.wait()
-        settle = reduce_plane(me, terms, rows, scratch[:N_REDUCE], produce, finish, after_terms)
+        settle = reduce_plane(
+            me,
+            terms,
+            rows,
+            scratch[:N_REDUCE],
+            TURNS_FFN_BACK[0],
+            produce,
+            finish,
+            after_terms,
+            tick,
+        )
         view = gather_view(full_ref, rows)
         keep = pltpu.make_async_copy(shard, view(me[0] * 4 + me[1] * 2 + me[2]), local)
         keep.start()
-        gather_plane(me, shard, view, scratch[N_REDUCE:], lambda step: between[step]())
-        keep.wait()
+        gather_plane(
+            me,
+            shard,
+            view,
+            scratch[N_REDUCE:],
+            TURNS_FFN_BACK[1],
+            arrived=arrived,
+            tick=tick,
+        )
+        while len(begun) < 8 + BACK_LAG:
+            next_part()
+        trickle.flush()
+        attend_back(3)
+        pair_out[0] = dk_all[tokens:, :].astype(BF)
+        pair_out[1] = dv_all[tokens:, :].astype(BF)
+        pair(0).start()
+        pair(1).start()
         settle()
+        for n, (ref, source_ref) in enumerate(((dk_ref, dk_all), (dv_ref, dv_all))):
+            pair(n).wait()
+            ref[...] = source_ref[:tokens, :] + pair_in[n].astype(F32)
         for t in range(8):
             core_copy(t).wait_send()
         pltpu.make_async_copy(to_ctx.at[0], in_ref.at[ctx], rest_sem.at[0]).wait()
-        for t in range(1, 8):
-            if t <= EARLY:
+        for n, t in enumerate(DEAL_ORDER):
+            if n < EARLY:
                 grad_landed(me, in_ref, grad_send, grad_recv, t)
-                grad_copy(me, to_ctx.at[t], in_ref, grad_send, grad_recv, t).wait_send()
+                for copy in grad_copies(me, to_ctx.at[t], in_ref, grad_send, grad_recv, t):
+                    copy.wait_send()
             else:
                 pltpu.make_async_copy(
-                    to_ctx.at[t], rest_ref.at[t - EARLY - 1], rest_sem.at[t - EARLY]
+                    to_ctx.at[t], rest_ref.at[n - EARLY], rest_sem.at[n - EARLY + 1]
                 ).wait()
 
     shape = jax.ShapeDtypeStruct
@@ -1332,9 +1646,12 @@
             shape((8, width), F32),
             shape((8, 3, part, part), BF),
             shape((7 - EARLY, 3, part, part), BF),
+            shape((tokens, HD), F32),
+            shape((tokens, HD), F32),
+            shape((tokens, HD), F32),
         ),
-        [*[ANY] * 7, VMEM, VMEM, VMEM],
-        (ANY, VMEM, VMEM, ANY, ANY),
+        [*[ANY] * 8, *[VMEM] * 12],
+        (ANY, VMEM, VMEM, ANY, ANY, VMEM, VMEM, VMEM),
         [
             vmem((tokens, width), BF),
             vmem((tokens, width), BF),
@@ -1346,60 +1663,86 @@
             vmem((tokens, 2 * hidden), BF),
             vmem((tokens, width), BF),
             vmem((rows, width), BF),
-            vmem((2, 3, part, part), F32),
             vmem((8, 3, part, part), BF),
             vmem((8, 3, part, part), BF),
             vmem((8, 3, part, part), BF),
-            DMA((4, 4)),
+            vmem((2, group, width), BF),
+            vmem((2 * tokens, HD), F32),
+            vmem((2 * tokens, HD), F32),
+            vmem((2, tokens, HD), BF),
+            vmem((2, tokens, HD), BF),
+            DMA((5, 4)),
             DMA,
             DMA((8,)),
             DMA((8,)),
+            DMA((8, 3)),
+            DMA((8, 3)),
             DMA((8,)),
-            DMA((8,)),
-            DMA((8,)),
+            DMA((2,)),
+            DMA((2,)),
+            DMA((2,)),
             *reduce_scratch(rows, width),
             *GATHER_SEMS,
         ],
-    )(grad_ffn, source, gu_w, down_w, for_gate, for_up, mixed, cotangent, branch, gain)
+    )(
+        grad_ffn,
+        source,
+        gu_w,
+        *down_w,
+        for_gate,
+        for_up,
+        mixed,
+        cotangent,
+        branch,
+        gain,
+        *attention,
+    )
 
 
 def write_results(early, late, wall, outputs, input_grad, gains):
     part = early.shape[2]
 
     def body(early_ref, late_ref, wall_ref, out_ref, in_ref, gain_ref, *results):
-        (out_to, in_to, gq, gk, gv, go, gg, gu, gd, gains_to) = results
-        c = pl.program_id(0)
-        ctx = lax.axis_index("z") * 2 + lax.axis_index("y")
-        t = lax.rem(ctx + 8 - c, 8)
-
-        @pl.when(c == 0)
+        (out_to, in_to, gq, gk, gv, go, gg, gu, gd, *gains_to) = results
+        n = pl.program_id(0)
+
+        @pl.when(n == 0)
         def _():
             out_to[...] = out_ref[...]
             in_to[...] = in_ref[...]
-            gains_to[...] = gain_ref[...]
+            for i, ref in enumerate(gains_to):
+                ref[...] = gain_ref[i : i + 1, :]
 
         for i, ref in enumerate((gq, gk, gv, go)):
             ref[...] = wall_ref[0, i].astype(F32)
 
-        @pl.when(t <= EARLY)
+        @pl.when(n <= EARLY)
         def _():
             for i, ref in enumerate((gg, gu, gd)):
                 ref[...] = early_ref[0, i].astype(F32)
 
-        @pl.when(t > EARLY)
+        @pl.when(n > EARLY)
         def _():
             for i, ref in enumerate((gg, gu, gd)):
                 ref[...] = late_ref[0, i].astype(F32)
 
     shape = jax.ShapeDtypeStruct
     spec = pl.BlockSpec
-    blob = spec((1, 3, part, part), lambda c: (c, 0, 0, 0))
+
+    def source(n):
+        ctx = lax.axis_index("z") * 2 + lax.axis_index("y")
+        odd = lax.rem(n, 2)
+        t = odd * (4 + n // 2) + (1 - odd) * (n // 2)
+        return lax.rem(ctx + 8 - t, 8)
+
     rows, columns = outputs.shape
-    whole = spec((rows, columns), lambda c: (0, 0))
-    in_row = spec((HD, HD), lambda c: (c % 2, c // 2))
-    in_column = spec((HD, HD), lambda c: (c // 2, c % 2))
-    side = spec((part, part), lambda c: (0, c))
-    gain_spec = spec(gains.shape, lambda c: (0, 0))
+    whole = spec((rows, columns), lambda n: (0, 0))
+    in_row = spec((HD, HD), lambda n: (source(n) % 2, source(n) // 2))
+    in_column = spec((HD, HD), lambda n: (source(n) // 2, source(n) % 2))
+    side = spec((part, part), lambda n: (0, source(n)))
+    gain_spec = spec(gains.shape, lambda n: (0, 0))
+    gain_row = spec((1, gains.shape[1]), lambda n: (0, 0))
+    blob = (1, 3, part, part)
     return pl.pallas_call(
         body,
         name="write_results",
@@ -1414,12 +1757,12 @@
             shape((part, 8 * part), F32),
             shape((part, 8 * part), F32),
             shape((8 * part, part), F32),
-            shape(gains.shape, F32),
+            *[shape((1, gains.shape[1]), F32)] * 4,
         ),
         in_specs=[
-            blob,
-            blob,
-            spec((1, 4, HD, HD), lambda c: (c, 0, 0, 0)),
+            spec(blob, lambda n: (source(jnp.minimum(n, EARLY)), 0, 0, 0)),
+            spec(blob, lambda n: (source(jnp.maximum(n, EARLY + 1)), 0, 0, 0)),
+            spec((1, 4, HD, HD), lambda n: (source(n), 0, 0, 0)),
             whole,
             whole,
             gain_spec,
@@ -1433,8 +1776,8 @@
             in_column,
             side,
             side,
-            spec((part, part), lambda c: (c, 0)),
-            gain_spec,
+            spec((part, part), lambda n: (source(n), 0)),
+            *[gain_row] * 4,
         ),
         compiler_params=pltpu.CompilerParams(vmem_limit_bytes=BIG_VMEM),
     )(early, late, wall, outputs, input_grad, gains)
@@ -1465,18 +1808,12 @@
     full_in,
     query,
     key,
-    query_rot,
-    keys,
-    values,
     attended,
-    lse,
+    grads_rotated,
     tables,
-    bounds,
-    logical,
     scales,
-    head_gains,
+    gains,
     qkv_w,
-    out_w,
     grad_own,
     attn_term,
     ffn_term,
@@ -1485,95 +1822,52 @@
     tokens, width = grad_attn.shape
     rows, group = tokens // 16, tokens // 4
     part = width // 4
-    scaling = 1.0 / math.sqrt(HD)
 
     def body(*refs):
         (da_any, x_any) = refs[:2]
-        (q_ref, k_ref, qrot_ref, keys_ref, values_ref, o_ref, lse_ref, cos_ref, sin_ref) = refs[2:11]
-        (low_ref, high_ref, log_ref, scale_ref, gain_ref, wqkv_ref, wout_ref) = refs[11:18]
-        (grad_ref, attn_ref, ffn_ref, left_ref) = refs[18:22]
-        (in_grad_ref, deal_in, gains_ref, ffn_in) = refs[22:26]
-        (da, xs, terms, do_ref, delta_ref, dq_ref, dk_ref, dv_ref) = refs[26:34]
-        (pair_out, pair_in, dqkv, slots, result) = refs[34:39]
-        (wall_grad, wall_out, wall_in, deal_out) = refs[39:43]
-        (gain_out, gain_in, gain_own, gain_slots) = refs[43:47]
-        (load_sem, pair_send, pair_recv, tot_send, tot_recv, out_send, out_recv) = refs[47:54]
-        (deal_send, deal_recv, gain_send, gain_recv, grad_send, grad_recv) = refs[54:60]
-        scratch = refs[60:]
+        (q_ref, k_ref, o_ref, dq_in, dk_in, dv_in, cos_ref, sin_ref) = refs[2:10]
+        (scale_ref, gain_ref, wqkv_ref) = refs[10:13]
+        (grad_ref, attn_ref, ffn_ref, left_ref) = refs[13:17]
+        (in_grad_ref, deal_in, gains_ref, ffn_in) = refs[17:21]
+        (da, xs, terms, dq_ref, dk_ref) = refs[21:26]
+        (dqkv, slots, result) = refs[26:29]
+        (qkv_grads, out_grads, wall_out, wall_in, deal_out) = refs[29:34]
+        (gain_out, gain_in, gain_own, gain_slots) = refs[34:38]
+        (load_sem, pair_send, pair_recv, tot_send, tot_recv, out_send, out_recv) = refs[38:45]
+        (deal_send, deal_recv, gain_send, gain_recv, grad_send, grad_recv) = refs[45:51]
+        scratch = refs[51:]
         me = z, y, x, k = place()
         ctx = own_tile(me)
         own = ctx * 2 + x
+        own_head = pl.ds(pl.multiple_of((x * 8 + ctx) * HD, HD), HD)
         sibling = (z, y, x, 1 - k)
 
-        da_loads = [
-            pltpu.make_async_copy(
-                da_any.at[g * group : (g + 1) * group, :],
-                da.at[g * group : (g + 1) * group, :],
-                load_sem.at[g],
-            )
-            for g in range(4)
-        ]
-        x_load = pltpu.make_async_copy(x_any, xs, load_sem.at[4])
-        for load in (*da_loads, x_load):
-            load.start()
+        da_load = pltpu.make_async_copy(da_any, da, load_sem.at[0])
+        x_load = pltpu.make_async_copy(x_any, xs, load_sem.at[1])
+        x_load.start()
+        da_load.start()
         close_greet(me)
-        for t in range(EARLY + 1, 8):
-            grad_copy(me, left_ref.at[t - EARLY - 1], ffn_in, grad_send, grad_recv, t).start()
+
+        trickle = Trickle()
+
+        def left_copies(n):
+            return grad_copies(me, left_ref.at[n - EARLY], ffn_in, grad_send, grad_recv, DEAL_ORDER[n])
+
+        for n in range(EARLY, 7):
+            trickle.add([copy.start for copy in left_copies(n)])
+        trickle.tick(CLOSE_FIRST)
 
         def pair(n):
             return pltpu.make_async_remote_copy(
-                src_ref=(pair_out.at[0], pair_out.at[1], wall_out, gain_out)[n],
-                dst_ref=(pair_in.at[0], pair_in.at[1], wall_in, gain_in)[n],
+                src_ref=wall_out.at[n] if n < 8 else gain_out,
+                dst_ref=wall_in.at[n] if n < 8 else gain_in,
                 send_sem=pair_send.at[n],
                 recv_sem=pair_recv.at[n],
                 device_id=sibling,
                 device_id_type=MESH,
             )
 
-        for g in range(4):
-            at = slice(g * group, (g + 1) * group)
-            da_loads[g].wait()
-            do = lax.dot_general(
-                da[at, :], wout_ref[...], (((1,), (1,)), ((), ())), preferred_element_type=F32
-            ).astype(BF)
-            do_ref[at, :] = do
-            delta_ref[at, :] = jnp.sum(do.astype(F32) * o_ref[at, :], axis=1, keepdims=True)
-
         across = (((0,), (0,)), ((), ()))
-        for half in (1, 0):
-            key_at = slice(half * tokens, (half + 1) * tokens)
-            dk_ref[...] = jnp.zeros_like(dk_ref)
-            dv_ref[...] = jnp.zeros_like(dv_ref)
-
-            def work(at, half=half, key_at=key_at):
-                q, g, key_part = qrot_ref[at, :], do_ref[at, :], keys_ref[key_at, :]
-                raw, allowed = masked_scores(
-                    q, key_part, low_ref[at, :], high_ref[at, :], log_ref[:, key_at]
-                )
-                weights = jnp.where(allowed, jnp.exp(raw - lse_ref[at, :]), 0.0)
-                dp = lax.dot_general(
-                    g, values_ref[key_at, :], (((1,), (1,)), ((), ())), preferred_element_type=F32
-                )
-                ds = (weights * (dp - delta_ref[at, :])).astype(BF)
-                dq = jnp.dot(ds, key_part, preferred_element_type=F32) * scaling
-                if half == 1:
-                    dq_ref[at, :] = dq
-                else:
-                    dq_ref[at, :] += dq
-                dk_ref[...] += (
-                    lax.dot_general(ds, q, across, preferred_element_type=F32) * scaling
-                )
-                dv_ref[...] += lax.dot_general(
-                    weights.astype(BF), g, across, preferred_element_type=F32
-                )
-
-            strips(tokens, work, group)
-            if half == 1:
-                pair_out[0] = dk_ref[...].astype(BF)
-                pair_out[1] = dv_ref[...].astype(BF)
-                pair(0).start()
-                pair(1).start()
-
         eye = eye_mask()
 
         def normed_grad(values, piece):
@@ -1584,23 +1878,20 @@
             for i in range(8):
                 piece = slice(i * HD, (i + 1) * HD)
                 factor = row_to_column(scale_ref[side * 8 + i : side * 8 + i + 1, :], eye)
-                back = normed_grad(source(piece), piece)
+                back = normed_grad(source[piece, :], piece)
                 term = back * proj[piece, :] * factor
                 for j in range(0, HD, 8):
                     gain_sum = gain_sum + term[j : j + 8, :]
-                weighted = back * gain_ref[side : side + 1, :]
+                weighted = back * gain_ref[side : side + 1, own_head]
                 grads[piece, :] = weighted
                 dot = jnp.sum(weighted * proj[piece, :], axis=1, keepdims=True)
                 slots[own, side * 8 + i : side * 8 + i + 1, :] = column_to_row(dot, eye)
             return jnp.sum(gain_sum, axis=0, keepdims=True)
 
-        query_gain = side_dots(0, lambda piece: dq_ref[piece, :], dq_ref, q_ref)
-        pair(0).wait_recv()
-        pair(1).wait_recv()
-        key_gain = side_dots(
-            1, lambda piece: dk_ref[piece, :] + pair_in[0, piece, :].astype(F32), dk_ref, k_ref
-        )
-        dqkv[:, 2 * HD :] = (dv_ref[...] + pair_in[1].astype(F32)).astype(BF)
+        query_gain = side_dots(0, dq_in, dq_ref, q_ref)
+        key_gain = side_dots(1, dk_in, dk_ref, k_ref)
+        sum_end = sum_begin(me, slots, tot_send, tot_recv)
+        dqkv[:, 2 * HD :] = dv_in[...].astype(BF)
 
         attn_sum = jnp.sum(attn_ref[...], axis=0, keepdims=True)
         ffn_sum = jnp.sum(ffn_ref[...], axis=0, keepdims=True)
@@ -1622,9 +1913,22 @@
                 target[x, 0:1, head_at] = query_gain
                 target[x, 1:2, head_at] = key_gain
 
-        pair(3).start()
-
-        total = sum_over_plane(me, slots, tot_send, tot_recv)
+        pair(8).start()
+
+        parts = (*DEAL_ORDER, 0)
+
+        def columns_of(n):
+            c = ctx + parts[n] - 8 * ((ctx + parts[n]) // 8)
+            return pl.ds(pl.multiple_of(c * 2 * HD, 2 * HD), 2 * HD)
+
+        attended_low = o_ref[...].astype(BF)
+        da_load.wait()
+        for n in range(8):
+            out_grads[n] = lax.dot_general(
+                attended_low, da[:, columns_of(n)], across, preferred_element_type=F32
+            )
+        total = sum_end()
+        trickle.tick(CLOSE_NEXT)
         for side, grads, proj in ((0, dq_ref, q_ref), (1, dk_ref, k_ref)):
             for i in range(8):
                 piece = slice(i * HD, (i + 1) * HD)
@@ -1662,11 +1966,12 @@
 
         number = ((z % 2) * 2 + y) * 2 + k
 
-        def deal(c):
+        def deal(n):
+            c = ctx + parts[n] - 8 * ((ctx + parts[n]) // 8)
             return pltpu.make_async_remote_copy(
-                src_ref=deal_out.at[c],
+                src_ref=deal_out.at[n],
                 dst_ref=deal_in.at[number],
-                send_sem=deal_send.at[c],
+                send_sem=deal_send.at[n],
                 recv_sem=deal_recv.at[number],
                 device_id=(c // 2, c % 2, x, head_core),
                 device_id_type=MESH,
@@ -1674,8 +1979,23 @@
 
         stays = k == head_core
 
+        def deal_start(n):
+            if n < 7:
+                deal(n).start()
+                return
+
+            @pl.when(jnp.logical_not(stays))
+            def _():
+                deal(n).start()
+
+            @pl.when(stays)
+            def _():
+                pltpu.make_async_copy(
+                    deal_out.at[n], deal_in.at[number], deal_recv.at[number]
+                ).start()
+
         def after_terms():
-            pair(3).wait_recv()
+            pair(8).wait_recv()
             gain_own[...] += gain_in[...]
             gain_slots[own] = gain_own[x]
 
@@ -1684,55 +2004,56 @@
                 return carry
 
             lax.fori_loop(1, 16, begin, 0)
-            x_load.wait()
-            for c in range(8):
-                grads = lax.dot_general(
-                    xs[:, c * 2 * HD : (c + 1) * 2 * HD],
-                    dqkv[...],
-                    across,
-                    preferred_element_type=F32,
+
+        x_load.wait()
+        begun = []
+
+        def halves(n, r):
+            rows_at = pl.ds(pl.multiple_of(r * HD, HD), HD)
+            for i in range(3):
+                yield i, qkv_grads[rows_at, i * HD : (i + 1) * HD]
+            yield 3, out_grads[n, :, rows_at]
+
+        def tick():
+            n = len(begun)
+            begun.append(n)
+            if n < 8:
+                qkv_grads[...] = lax.dot_general(
+                    xs[:, columns_of(n)], dqkv[...], across, preferred_element_type=F32
                 )
-                for i in range(3):
-                    for r in range(2):
-                        wall_grad[r, c, i] = grads[r * HD : (r + 1) * HD, i * HD : (i + 1) * HD]
-                out_grad = lax.dot_general(
-                    o_ref[...].astype(BF),
-                    da[:, c * 2 * HD : (c + 1) * 2 * HD],
-                    across,
-                    preferred_element_type=F32,
-                )
-                for r in range(2):
-                    wall_grad[r, c, 3] = out_grad[:, r * HD : (r + 1) * HD]
-
-            def to_other(c, carry):
-                wall_out[c] = wall_grad[1 - k, c].astype(BF)
-                return carry
-
-            lax.fori_loop(0, 8, to_other, 0)
-            pair(2).start()
-            pair(2).wait_recv()
-
-            def to_owner(c, carry):
-                deal_out[c] = (wall_grad[k, c] + wall_in[c].astype(F32)).astype(BF)
-                return carry
-
-            lax.fori_loop(0, 8, to_owner, 0)
-            for c in range(8):
-
-                @pl.when(jnp.logical_not(stays & (ctx == c)))
-                def _(c=c):
-                    deal(c).start()
-
-                @pl.when(stays & (ctx == c))
-                def _(c=c):
-                    pltpu.make_async_copy(
-                        deal_out.at[c], deal_in.at[number], deal_recv.at[number]
-                    ).start()
+                for i, value in halves(n, 1 - k):
+                    wall_out[n, i] = value.astype(BF)
+                for i, value in halves(n, k):
+                    deal_out[n, i] = value.astype(BF)
+                pair(n).start()
+            if CLOSE_LAG <= n < 8 + CLOSE_LAG:
+                last = n - CLOSE_LAG
+                pair(last).wait_recv()
+                deal_out[last] = (deal_out[last].astype(F32) + wall_in[last].astype(F32)).astype(BF)
+                deals.add([lambda: deal_start(last)])
+            deals.tick()
+            trickle.tick(CLOSE_RATE)
+
+        deals = Trickle()
 
         def finish(strip, total):
             result[strip] = (grad_ref[strip] + total).astype(BF)
 
-        settle = reduce_plane(me, terms, rows, scratch, produce, finish, after_terms)
+        settle = reduce_plane(
+            me,
+            terms,
+            rows,
+            scratch,
+            TURNS_CLOSE,
+            produce,
+            finish,
+            after_terms,
+            tick,
+        )
+        while len(begun) < 8 + CLOSE_LAG:
+            tick()
+        deals.flush()
+        trickle.flush()
         copies, own_copy = hand_out_copies(me, result, in_grad_ref, out_send, out_recv)
         for copy in copies:
             copy.start()
@@ -1762,19 +2083,19 @@
         own_copy.wait()
         for copy in copies:
             copy.wait()
-        for c in range(8):
-
-            @pl.when(jnp.logical_not(stays & (ctx == c)))
-            def _(c=c):
-                deal(c).wait_send()
-
-        for n in range(4):
+        for n in range(7):
+            deal(n).wait_send()
+
+        @pl.when(jnp.logical_not(stays))
+        def _():
+            deal(7).wait_send()
+
+        for n in range(9):
             pair(n).wait_send()
-        for t in range(EARLY + 1, 8):
-            grad_landed(me, ffn_in, grad_send, grad_recv, t)
-            grad_copy(
-                me, left_ref.at[t - EARLY - 1], ffn_in, grad_send, grad_recv, t
-            ).wait_send()
+        for n in range(EARLY, 7):
+            grad_landed(me, ffn_in, grad_send, grad_recv, DEAL_ORDER[n])
+            for copy in left_copies(n):
+                copy.wait_send()
 
     shape = jax.ShapeDtypeStruct
     vmem = pltpu.VMEM
@@ -1788,23 +2109,19 @@
             shape((4, part), F32),
             shape((8, *grads_left.shape[1:]), BF),
         ),
-        [ANY, ANY, *[VMEM] * 19, ANY],
+        [ANY, ANY, *[VMEM] * 14, ANY],
         (ANY, ANY, VMEM, ANY),
         [
             vmem((tokens, width), BF),
             vmem((tokens, width), BF),
             vmem((tokens, width), BF),
-            vmem((tokens, HD), BF),
-            vmem((tokens, 1), F32),
             vmem((tokens, HD), F32),
             vmem((tokens, HD), F32),
-            vmem((tokens, HD), F32),
-            vmem((2, tokens, HD), BF),
-            vmem((2, tokens, HD), BF),
             vmem((tokens, 3 * HD), BF),
             vmem((16, 16, HD), F32),
             vmem((rows, width), BF),
-            vmem((2, 8, 4, HD, HD), F32),
+            vmem((2 * HD, 3 * HD), F32),
+            vmem((8, HD, 2 * HD), F32),
             vmem((8, 4, HD, HD), BF),
             vmem((8, 4, HD, HD), BF),
             vmem((8, 4, HD, HD), BF),
@@ -1812,9 +2129,9 @@
             vmem((2, 4, part), F32),
             vmem((2, 4, part), F32),
             vmem((16, 4, part), F32),
-            DMA((5,)),
-            DMA((4,)),
-            DMA((4,)),
+            DMA((2,)),
+            DMA((9,)),
+            DMA((9,)),
             DMA((16,)),
             DMA((16,)),
             DMA((3,)),
@@ -1823,8 +2140,8 @@
             DMA((8,)),
             DMA((16,)),
             DMA((16,)),
-            DMA((8,)),
-            DMA((8,)),
+            DMA((8, 3)),
+            DMA((8, 3)),
             *reduce_scratch(rows, width),
         ],
     )(
@@ -1832,33 +2149,16 @@
         full_in,
         query,
         key,
-        query_rot,
-        keys,
-        values,
         attended,
-        lse,
+        *grads_rotated,
         *tables,
-        *bounds,
-        logical,
         scales,
-        head_gains,
+        gains,
         qkv_w,
-        out_w,
         grad_own,
         attn_term,
         ffn_term,
         grads_left,
-    )
-
-
-def rotary_tables(offset):
-    half_dim = HD // 2
-    inverse = jnp.power(ROPE_THETA, -jnp.arange(half_dim, dtype=F32) * 2.0 / HD)
-    angles = offset.astype(F32)[:, None] * inverse[None, :]
-    cosine, sine_part = jnp.cos(angles), jnp.sin(angles)
-    return (
-        jnp.concatenate([cosine, cosine], axis=1),
-        jnp.concatenate([-sine_part, sine_part], axis=1),
     )
 
 
@@ -1879,41 +2179,33 @@
     lengths,
     block_order,
 ):
-    z, y, x, k = place()
-    ctx = z * 2 + y
-    tok_rows, width_part = inputs.shape
-    plane_rows = tok_rows // 2
-    tokens = 8 * plane_rows
-
-    order = block_order.reshape(8, 2, -1)
-    block_rows = plane_rows // order.shape[2]
-
-    def logical_of(core):
-        blocks = lax.dynamic_index_in_dim(order, core, 1, keepdims=False).reshape(-1)
-        return (
-            blocks[:, None] * block_rows + jnp.arange(block_rows, dtype=jnp.int32)[None, :]
-        ).reshape(-1)
-
-    logical_own, logical_other = logical_of(k), logical_of(1 - k)
-    offset_own = sequence_tables(logical_own, lengths)[1]
-    tables = rotary_tables(offset_own)
-    low = (logical_own - offset_own)[:, None]
-    high = logical_own[:, None]
-    logical_keys = jnp.concatenate([logical_own, logical_other])[None, :]
-
-    gains = jnp.stack([query_gain, key_gain, attn_gain, ffn_gain])
-    full_in, source_own, own_cot, qkv_w, out_w, gains_full, gu_stage, d_stage, query_proj, key_proj, value_low = open_layer(
-        inputs, cotangent, w_query, w_key, w_value, w_out, w_gate, w_up, w_down, gains
-    )
-    head = x * 8 + ctx
-    attn_gain_row, ffn_gain_row = gains_full[2:3], gains_full[3:4]
-    head_gains = lax.dynamic_slice_in_dim(gains_full[:2], head * HD, HD, 1)
+    steps = np.arange(HD // 2, dtype=np.float64) * 2.0 / HD
+    frequency = np.tile(np.power(ROPE_THETA, -steps), 2)[None, :].astype(np.float32)
+    full_in, source_own, own_cot, qkv_w, out_w, gains_full, gu_stage, down_own, query_proj, key_proj, value_low, cosine, sine, low, high, logical_keys = open_layer(
+        inputs,
+        cotangent,
+        w_query,
+        w_key,
+        w_value,
+        w_out,
+        w_gate,
+        w_up,
+        w_down,
+        query_gain[None, :],
+        key_gain[None, :],
+        attn_gain[None, :],
+        ffn_gain[None, :],
+        block_order[None, :],
+        lengths[None, :],
+        jnp.asarray(frequency),
+    )
+    tables = (cosine, sine)
     (
         residual_full,
         residual_own,
         branch_own,
         gu_w,
-        down_w,
+        down_other,
         query_rot,
         keys_all,
         values_all,
@@ -1929,52 +2221,44 @@
         logical_keys,
         source_own,
         out_w,
-        head_gains,
-        attn_gain_row,
+        gains_full,
         gu_stage,
-        d_stage,
+        down_own,
     )
     grad_ffn, outputs, ffn_gain_term, for_gate, for_up, mixed = ffn_forward(
-        residual_full, gu_w, down_w, residual_own, own_cot, ffn_gain_row
-    )
-    grad_attn, grad_own, attn_gain_term, ffn_early, ffn_left = ffn_backward(
+        residual_full, gu_w, (down_own, down_other), residual_own, own_cot, gains_full
+    )
+    grad_attn, grad_own, attn_gain_term, ffn_early, ffn_left, *grads_rotated = ffn_backward(
         grad_ffn,
         residual_full,
         gu_w,
-        down_w,
+        (down_own, down_other),
         for_gate,
         for_up,
         mixed,
         own_cot,
         branch_own,
-        attn_gain_row,
+        gains_full,
+        (out_w, query_rot, keys_all, values_all, attended, lse, low, high, logical_keys),
     )
     input_grad, wall_grads, gain_grads, ffn_late = attention_backward(
         grad_attn,
         full_in,
         query_proj,
         key_proj,
-        query_rot,
-        keys_all,
-        values_all,
         attended,
-        lse,
+        grads_rotated,
         tables,
-        (low, high),
-        logical_keys,
         scales,
-        head_gains,
+        gains_full,
         qkv_w,
-        out_w,
         grad_own,
         attn_gain_term,
         ffn_gain_term,
         ffn_left,
     )
-    *results, gains_out = write_results(
-        ffn_early, ffn_late, wall_grads, outputs, input_grad, gain_grads
-    )
-    return (*results, *gains_out)
+    results = write_results(ffn_early, ffn_late, wall_grads, outputs, input_grad, gain_grads)
+    return (*results[:9], *[row[0] for row in results[9:]])
 
 
 def full_rows(piece):

time: 550 us -> 498 us (0.905)
  Pallas kernels: 531 us -> 491 us
  local copies, waits for them, and re-layouts: 7.63 us -> 0 us
  other arithmetic: 7.01 us -> 0 us
    pallas_call x1, Pallas kernels: 103 us -> 75.3 us  [attention_backward(): comm_call(body, 'attention_backward', 5, (shape((rows * 4, part), BF), sh...]
    pallas_call x1, Pallas kernels: 138 us -> 116 us  [attention_forward(): comm_call(body, 'attention_forward', 1, (shape((tokens, width), BF), shap...]
    pallas_call x1, Pallas kernels: 70.3 us -> 77.6 us  [open_layer(): comm_call(body, 'open_layer', 0, (shape((tokens, width), BF), shape((quar...]
where the time goes in v4:
time: 498 us; the launch traced here: 492 us
  Pallas kernels  491 us (99%)
    pallas_call x1, Pallas kernels, ffn_backward(): comm_call(body, 'ffn_backward', 4, (shape((tokens, width), BF), shape((ro...  125 us
    pallas_call x1, Pallas kernels, attention_forward(): comm_call(body, 'attention_forward', 1, (shape((tokens, width), BF), shap...  116 us
    pallas_call x1, Pallas kernels, ffn_forward(): comm_call(body, 'ffn_forward', 3, (shape((tokens, width), BF), shape((row...  88.7 us
    pallas_call x1, Pallas kernels, open_layer(): comm_call(body, 'open_layer', 0, (shape((tokens, width), BF), shape((quar...  77.6 us
    pallas_call x1, Pallas kernels, attention_backward(): comm_call(body, 'attention_backward', 5, (shape((rows * 4, part), BF), sh...  75.3 us

profile of v4, /device:TPU:1, one launch (start us, length us, event | category | flops | bytes accessed | tf_op | source)
XLA Modules:
  0.0 492.4 jit_solution(2636655486522144013)
XLA Ops:
  0.7 77.6 %open_layer.1 = (bf16[1024,2048]{1,0:T(8,128)(2,1)}, bf16[64,2048]{1,0:T(8,128)(2,1)}, bf16[64,2048]{1,0:T(8,128)(2,1)}, bf16[3,2048,128]{2,1,0:T(8,128)(2,1)}, ...) custom-call(bf16[256,512]{1,0:T(8,128)(2,1)} %refs_0_.1, ...), custom_call_target="tpu_custom_call" | custom-call | tf_op jit(solution)/shard_map/open_layer/pallas_call | solution.py:901
  78.3 116.3 %attention_forward.1 = (bf16[1024,2048]{1,0:T(8,128)(2,1)}, f32[64,2048]{1,0:T(8,128)}, f32[64,2048]{1,0:T(8,128)}, bf16[2,2048,512]{2,1,0:T(8,128)(2,1)}, bf16[...) custom-call(f32[1024,128]{1,0:T(8,128)} %get-tuple-element.71.refs_0, ...), custom_call_target="tpu_custom_call" | custom-call | tf_op jit(solution)/shard_map/attention_forward/pallas_call | solution.py:1209
  194.6 88.7 %ffn_forward.1 = (bf16[1024,2048]{1,0:T(8,128)(2,1)}, bf16[256,512]{1,0:T(8,128)(2,1)}, f32[8,2048]{1,0:T(8,128)}, f32[1024,512]{1,0:T(8,128)}, f32[1024,512]{1,0:T(8,128)}, /*index=5*/bf16[1024,512]{1,0:T(8,128)(2,1)}) custom-call(bf16[1024,2048]{1,0:T(8,128)(2,1)} %get-tuple-element.84.refs_0_.refs_1_, ...), custom_call_target="tpu_custom_call" | custom-call | tf_op jit(solution)/shard_map/ffn_forward/pallas_call | solution.py:1318
  283.3 125.2 %ffn_backward.1 = (bf16[1024,2048]{1,0:T(8,128)(2,1)}, f32[64,2048]{1,0:T(8,128)}, f32[8,2048]{1,0:T(8,128)}, bf16[8,3,256,256]{3,2,1,0:T(8,128)(2,1)}, bf16[2,3...) custom-call(bf16[1024,2048]{1,0:T(8,128)(2,1)} %get-tuple-element.89.refs_0_, ...), custom_call_target="tpu_custom_call" | custom-call | tf_op jit(solution)/shard_map/ffn_backward/pallas_call | solution.py:1639
  408.5 75.3 %attention_backward.1 = (bf16[256,512]{1,0:T(8,128)(2,1)}, bf16[8,4,128,128]{3,2,1,0:T(8,128)(2,1)}, f32[4,512]{1,0:T(4,128)}, bf16[8,3,256,256]{3,2,1,0:T(8,128)(2,1)}) custom-call(bf16[1024,2048]{1,0:T(8,128)(2,1)} %get-tuple-element.100.refs_0_, bf16[1024,2048]{1,0:T(8,128)(2,1)} %get-tuple-element.101.refs_1_, ...), custom_call_target="tpu_custom_call" | custom-call | tf_op jit(solution)/shard_map/attention_backward/pallas_call | solution.py:2102
  483.9 8.1 %write_results.1 = (bf16[256,512]{1,0:T(8,128)(2,1)}, bf16[256,512]{1,0:T(8,128)(2,1)}, f32[256,512]{1,0:T(8,128)}, f32[256,512]{1,0:T(8,128)}, f32[256,512]{1,0...) custom-call(bf16[8,3,256,256]{3,2,1,0:T(8,128)(2,1)} %get-tuple-elem, ...), custom_call_target="tpu_custom_call" | custom-call | tf_op jit(solution)/shard_map/write_results/pallas_call | solution.py:1746

commit v5 on v4

--- a/solution.py
+++ b/solution.py
@@ -99,6 +99,7 @@
 
 
 DEAL_ORDER = (4, 1, 5, 2, 6, 3, 7)
+OPEN_DEAL = 0
 OPEN_RATE = 2
 DEALT_FIRST = 5
 FORWARD_RATE = 1
@@ -106,8 +107,9 @@
 CLOSE_FIRST = 0
 CLOSE_NEXT = 4
 SUM_LAG = 1
+EARLY_LAYERS = True
 BACK_LAG = 1
-CLOSE_LAG = 3
+CLOSE_LAG = 2
 CLOSE_RATE = 1
 
 
@@ -134,8 +136,9 @@
     sems,
     turns,
     between=lambda step: None,
-    arrived=lambda step: None,
+    arrived=None,
     tick=lambda: None,
+    early=False,
 ):
     z, y, x, k = me
     recv, up_send, down_send, a_send, b_send = sems
@@ -160,7 +163,8 @@
         zp = near_first(step, z)
         landed(slot(zp, a, 1 - b))
         landed(slot(zp, 1 - a, 1 - b))
-        arrived(step)
+        if arrived is not None:
+            arrived(step)
 
     for step in range(5):
         if step < 4:
@@ -191,9 +195,10 @@
             copy(view(index), index, b_send.at[3 + step], dev_b).start()
             tick()
         between(step)
-        if step >= 2:
+        if step >= 2 and early:
             layer_landed(step - 2)
-    layer_landed(3)
+    for step in ((3,) if early else range(4)):
+        layer_landed(step)
     for step in range(4):
         a, b, slot, dev_a, dev_b = axes[step]
         zp = near_first(step, z)
@@ -465,19 +470,42 @@
     return back, term[:8] + term[8:]
 
 
-def comm_call(body, name, number, out_shape, in_specs, out_specs, scratch, cost=None):
-    return pl.pallas_call(
-        body,
-        name=name,
-        out_shape=out_shape,
-        in_specs=in_specs,
-        out_specs=out_specs,
-        scratch_shapes=scratch,
-        cost_estimate=cost,
-        compiler_params=pltpu.CompilerParams(
-            collective_id=number, has_side_effects=True, vmem_limit_bytes=BIG_VMEM
-        ),
-    )
+def comm_call(body, name, number, out_shape, in_specs, out_specs, scratch, lift=True):
+    lifted = [i for i, spec in enumerate(in_specs) if spec is VMEM] if lift else []
+
+    def with_loads(*refs):
+        refs = list(refs)
+        sems = refs.pop() if lifted else None
+        held = refs[len(refs) - len(lifted) :]
+        refs = refs[: len(refs) - len(lifted)]
+        copies = []
+        for n, i in enumerate(lifted):
+            copies.append(pltpu.make_async_copy(refs[i], held[n], sems.at[n]))
+            refs[i] = held[n]
+        for copy in copies:
+            copy.start()
+
+        def loaded():
+            for copy in copies:
+                copy.wait()
+
+        body(*refs, loaded=loaded)
+
+    def call(*args):
+        extra = [pltpu.VMEM(args[i].shape, args[i].dtype) for i in lifted]
+        return pl.pallas_call(
+            with_loads,
+            name=name,
+            out_shape=out_shape,
+            in_specs=[ANY if i in lifted else spec for i, spec in enumerate(in_specs)],
+            out_specs=out_specs,
+            scratch_shapes=[*scratch, *extra, *([DMA((len(lifted),))] if lifted else [])],
+            compiler_params=pltpu.CompilerParams(
+                collective_id=number, has_side_effects=True, vmem_limit_bytes=BIG_VMEM
+            ),
+        )(*args)
+
+    return call
 
 
 def same_x_greet(me):
@@ -546,7 +574,7 @@
     hidden = w_gate.shape[1]
     down = hidden // 8
 
-    def body(*refs):
+    def body(*refs, loaded):
         (in_ref, cot_ref, wq_ref, wk_ref, wv_ref, wo_ref, wg_ref, wu_ref, wd_ref) = refs[:9]
         gain_parts = refs[9:13]
         (order_ref, lengths_ref, frequency_ref) = refs[13:16]
@@ -582,6 +610,7 @@
         for load in loads:
             load.start()
         same_x_greet(me)
+        loaded()
 
         def pair_copy(src, dst, number):
             columns = pl.ds(pl.multiple_of(k * part, part), part)
@@ -686,6 +715,10 @@
                 out_stage[s] = out_raw[s].astype(BF)
 
             strips(2 * rows, round_out, 32)
+            if OPEN_DEAL == 0:
+                begin_deal()
+
+        def begin_deal():
             trickle.add([lambda e=e: deal_start(e) for e in range(8)])
 
         def deal_start(e):
@@ -814,21 +847,22 @@
 
         between = [
             deal_all,
-            lambda: (cot_begin(), round_down(), deal_down()),
+            lambda: (cot_begin(), round_down()),
             lambda: (round_up(0), round_up(1)),
             positions,
             lambda: None,
         ]
-        gather_plane(
-            me,
-            shard,
-            view,
-            gather_sems,
-            TURNS_OPEN,
-            lambda step: between[step](),
-            tick=lambda: trickle.tick(OPEN_RATE),
-        )
-        trickle.flush()
+
+        def open_between(step):
+            if 0 < step == OPEN_DEAL:
+                begin_deal()
+            if step == max(OPEN_DEAL, 1):
+                if step == 1:
+                    between[1]()
+                deal_down()
+                if step == 1:
+                    return
+            between[step]()
 
         def deal_wait(c):
             at = slice(c * 2 * HD, c * 2 * HD + HD)
@@ -853,27 +887,39 @@
                 for i, ref in enumerate((wqkv_ref.at[:, at, :], wout_ref.at[:, at]))
             ]
 
-        for c in range(8):
-            deal_wait(c)
-            for copy in share(c, k):
-                copy.start()
-        own_local.wait()
+        def project_layer(step):
+            if step == 0:
+                trickle.flush()
+                own_local.wait()
+                for c in range(8):
+                    deal_wait(c)
+                    for copy in share(c, k):
+                        copy.start()
+                for c in range(8):
+                    for copy in share(c, 1 - k):
+                        copy.wait_recv()
+            at = pl.ds(pl.multiple_of(near_first(step, z) * 2 * half, 2 * half), 2 * half)
+            tile = full_ref[at, :]
+            q_ref[at, :] = jnp.dot(tile, wqkv_ref[0], preferred_element_type=F32)
+            k_ref[at, :] = jnp.dot(tile, wqkv_ref[1], preferred_element_type=F32)
+            v_ref[at, :] = jnp.dot(tile, wqkv_ref[2], preferred_element_type=F32).astype(BF)
+
+        gather_plane(
+            me,
+            shard,
+            view,
+            gather_sems,
+            TURNS_OPEN,
+            open_between,
+            project_layer,
+            lambda: trickle.tick(OPEN_RATE),
+        )
+
         full_keep = pltpu.make_async_copy(full_ref, full_out, keep_sem.at[3])
         full_keep.start()
         own_rows = pl.ds(pl.multiple_of(own_slot * quarter, quarter), quarter)
         own_keep = pltpu.make_async_copy(full_ref.at[own_rows, :], own_out, keep_sem.at[4])
         own_keep.start()
-        for c in range(8):
-            for copy in share(c, 1 - k):
-                copy.wait_recv()
-
-        def project(s):
-            tile = full_ref[s, :]
-            q_ref[s, :] = jnp.dot(tile, wqkv_ref[0], preferred_element_type=F32)
-            k_ref[s, :] = jnp.dot(tile, wqkv_ref[1], preferred_element_type=F32)
-            v_ref[s, :] = jnp.dot(tile, wqkv_ref[2], preferred_element_type=F32).astype(BF)
-
-        strips(tokens, project, 256)
         for e in range(8):
 
             @pl.when(jnp.logical_not(stays & (own_e == e)))
@@ -951,6 +997,7 @@
             *GATHER_SEMS,
             pltpu.VMEM((4, part), F32),
         ],
+        lift=False,
     )(
         inputs,
         cotangent,
@@ -1037,7 +1084,7 @@
     hidden = gu_stage.shape[2] // 8
     part = width // 8
 
-    def body(*refs):
+    def body(*refs, loaded):
         (q_in, k_in, v_in, cos_ref, sin_ref, low_ref, high_ref, log_ref, source_ref, wout_ref, gain_ref) = refs[:11]
         (gu_ref, d_ref) = refs[11:13]
         (full_ref, own_ref, branch_ref, wgu_ref, d_other_ref, qrot_ref, keys_ref, values_ref, o_ref, lse_ref, scale_ref) = refs[13:24]
@@ -1047,10 +1094,11 @@
         me = z, y, x, k = place()
         ctx = own_tile(me)
         head_at = pl.ds(pl.multiple_of((x * 8 + ctx) * HD, HD), HD)
-        query_gain, key_gain = gain_ref[0:1, head_at], gain_ref[1:2, head_at]
         sibling = (z, y, x, 1 - k)
         barrier = pltpu.get_barrier_semaphore()
         plane_greet_all(me, [sibling])
+        loaded()
+        query_gain, key_gain = gain_ref[0:1, head_at], gain_ref[1:2, head_at]
 
         def pair(src, dst, n):
             return pltpu.make_async_remote_copy(
@@ -1129,10 +1177,10 @@
             )
             raw = jnp.where(allowed, raw, MASKED)
             top = jnp.max(raw, axis=1, keepdims=True)
-            weights = jnp.where(allowed, jnp.exp(raw - top), 0.0)
+            weights = jnp.exp(raw - top)
             total_weight = jnp.sum(weights, axis=1, keepdims=True)
-            weights = (weights / total_weight).astype(BF)
-            out = jnp.dot(weights, values_ref[...], preferred_element_type=F32)
+            out = jnp.dot(weights.astype(BF), values_ref[...], preferred_element_type=F32)
+            out = out * (1.0 / total_weight)
             o_ref[at, :] = out
             lse_ref[at, :] = top + jnp.log(total_weight)
             terms[at, :] = jnp.dot(
@@ -1250,11 +1298,12 @@
     rows, group = tokens // 16, tokens // 4
     hidden = 2 * down_w[0].shape[0]
 
-    def body(*refs):
+    def body(*refs, loaded):
         (h_any, gu_any, d_any, d_any2, res_ref, cot_ref, gain_ref) = refs[:7]
-        (full_ref, out_ref, gg_ref, for_gate_ref, for_up_ref, m_ref) = refs[7:13]
+        (full_ref, out_ref, gg_ref, for_gate_out, for_up_out, m_out) = refs[7:13]
         (hs, gu, dw, terms, shard, result, load_sem, local, out_send, out_recv) = refs[13:23]
-        scratch = refs[23:]
+        (for_gate_ref, for_up_ref, m_ref, leave_sem) = refs[23:27]
+        scratch = refs[27:]
         me = z, y, x, k = place()
 
         def h_load(zp):
@@ -1272,8 +1321,17 @@
         for zp in order[1:]:
             h_load(zp).start()
         greet_plane(me, pair_devices(me))
+        loaded()
         gg_ref[...] = jnp.zeros_like(gg_ref)
         gu_load.wait()
+
+        def leave(zp):
+            at = pl.ds(pl.multiple_of(zp * group, group), group)
+            pairs = ((for_gate_ref, for_gate_out), (for_up_ref, for_up_out), (m_ref, m_out))
+            return [
+                pltpu.make_async_copy(src.at[at, :], dst.at[at, :], leave_sem.at[i, zp])
+                for i, (src, dst) in enumerate(pairs)
+            ]
 
         def produce(zp):
             at = pl.ds(pl.multiple_of(zp * group, group), group)
@@ -1287,6 +1345,8 @@
             for_gate_ref[at, :] = up * sig * (1.0 + gate * (1.0 - sig))
             for_up_ref[at, :] = silu
             m_ref[at, :] = mixed
+            for copy in leave(zp):
+                copy.start()
             terms[at, :] = jnp.dot(mixed, dw[...], preferred_element_type=F32).astype(BF)
 
         def finish(strip, total):
@@ -1310,6 +1370,9 @@
         gather_plane(me, shard, view, scratch[N_REDUCE:], EVEN)
         keep.wait()
         settle()
+        for zp in range(4):
+            for copy in leave(zp):
+                copy.wait()
         own.wait()
         for copy in copies:
             copy.wait()
@@ -1328,7 +1391,7 @@
             shape((tokens, hidden), BF),
         ),
         [ANY, ANY, ANY, ANY, VMEM, VMEM, VMEM],
-        (ANY, ANY, VMEM, VMEM, VMEM, VMEM),
+        (ANY, ANY, VMEM, ANY, ANY, ANY),
         [
             pltpu.VMEM((tokens, width), BF),
             pltpu.VMEM((2, width, hidden), BF),
@@ -1340,6 +1403,10 @@
             DMA,
             DMA((3,)),
             DMA((4,)),
+            pltpu.VMEM((tokens, hidden), F32),
+            pltpu.VMEM((tokens, hidden), F32),
+            pltpu.VMEM((tokens, hidden), BF),
+            DMA((3, 4)),
             *reduce_scratch(rows, width),
             *GATHER_SEMS,
         ],
@@ -1347,7 +1414,7 @@
 
 
 EARLY = 5
-GRADS_FIRST = 6
+GRADS_FIRST = 3
 
 
 def grad_copies(me, src, dst, send, recv, t):
@@ -1408,7 +1475,7 @@
     turned = (((1,), (1,)), ((), ()))
     scaling = 1.0 / math.sqrt(HD)
 
-    def body(*refs):
+    def body(*refs, loaded):
         (df_any, h_any, gu_any, d_any, d_any2, fg_any, fu_any, m_any, cot_ref, branch_ref, gain_ref) = refs[:11]
         (wout_ref, qrot_ref, keys_ref, values_ref, o_ref, lse_ref, low_ref, high_ref, log_ref) = refs[11:20]
         (full_ref, own_ref, gg_ref, in_ref, rest_ref, dq_ref, dk_ref, dv_ref) = refs[20:28]
@@ -1443,6 +1510,7 @@
         m_load.start()
         sibling = (z, y, x, 1 - k)
         ctx_greet(me, [sibling])
+        loaded()
         gg_ref[...] = jnp.zeros_like(gg_ref)
         d_load.wait()
         d_load2.wait()
@@ -1608,6 +1676,7 @@
             TURNS_FFN_BACK[1],
             arrived=arrived,
             tick=tick,
+            early=EARLY_LAYERS,
         )
         while len(begun) < 8 + BACK_LAG:
             next_part()
@@ -1823,7 +1892,7 @@
     rows, group = tokens // 16, tokens // 4
     part = width // 4
 
-    def body(*refs):
+    def body(*refs, loaded):
         (da_any, x_any) = refs[:2]
         (q_ref, k_ref, o_ref, dq_in, dk_in, dv_in, cos_ref, sin_ref) = refs[2:10]
         (scale_ref, gain_ref, wqkv_ref) = refs[10:13]
@@ -1847,6 +1916,7 @@
         x_load.start()
         da_load.start()
         close_greet(me)
+        loaded()
 
         trickle = Trickle()
 

time: 498 us -> 483 us (0.970)
  Pallas kernels: 491 us -> 476 us
    pallas_call x5, Pallas kernels: 483 us -> 468 us  [call(): pl.pallas_call(with_loads, name=name, out_shape=out_shape, in_specs=[ANY...]
where the time goes in v5:
time: 483 us; the launch traced here: 477 us
  Pallas kernels  476 us (99%)
    pallas_call x5, Pallas kernels, call(): pl.pallas_call(with_loads, name=name, out_shape=out_shape, in_specs=[ANY...  468 us

profile of v5, /device:TPU:1, one launch (start us, length us, event | category | flops | bytes accessed | tf_op | source)
XLA Modules:
  0.0 476.9 jit_solution(8577981362172765854)
XLA Ops:
  0.7 73.1 %open_layer.1 = (bf16[1024,2048]{1,0:T(8,128)(2,1)}, bf16[64,2048]{1,0:T(8,128)(2,1)}, bf16[64,2048]{1,0:T(8,128)(2,1)}, bf16[3,2048,128]{2,1,0:T(8,128)(2,1)}, ...) custom-call(bf16[256,512]{1,0:T(8,128)(2,1)} %refs_0_.1, ...), custom_call_target="tpu_custom_call" | custom-call | tf_op jit(solution)/shard_map/open_layer/pallas_call | solution.py:496
  73.7 113.0 %attention_forward.1 = (bf16[1024,2048]{1,0:T(8,128)(2,1)}, f32[64,2048]{1,0:T(8,128)}, f32[64,2048]{1,0:T(8,128)}, bf16[2,2048,512]{2,1,0:T(8,128)(2,1)}, bf16[...) custom-call(f32[1024,128]{1,0:T(8,128)} %get-tuple-element.71.refs_0, ...), custom_call_target="tpu_custom_call" | custom-call | tf_op jit(solution)/shard_map/attention_forward/pallas_call | solution.py:496
  186.8 83.2 %ffn_forward.1 = (bf16[1024,2048]{1,0:T(8,128)(2,1)}, bf16[256,512]{1,0:T(8,128)(2,1)}, f32[8,2048]{1,0:T(8,128)}, f32[1024,512]{1,0:T(8,128)}, f32[1024,512]{1,0:T(8,128)}, /*index=5*/bf16[1024,512]{1,0:T(8,128)(2,1)}) custom-call(bf16[1024,2048]{1,0:T(8,128)(2,1)} %get-tuple-element.84.refs_0_.refs_1_, ...), custom_call_target="tpu_custom_call" | custom-call | tf_op jit(solution)/shard_map/ffn_forward/pallas_call | solution.py:496
  270.0 123.2 %ffn_backward.1 = (bf16[1024,2048]{1,0:T(8,128)(2,1)}, f32[64,2048]{1,0:T(8,128)}, f32[8,2048]{1,0:T(8,128)}, bf16[8,3,256,256]{3,2,1,0:T(8,128)(2,1)}, bf16[2,3...) custom-call(bf16[1024,2048]{1,0:T(8,128)(2,1)} %get-tuple-element.89.refs_0_, ...), custom_call_target="tpu_custom_call" | custom-call | tf_op jit(solution)/shard_map/ffn_backward/pallas_call | solution.py:496
  393.1 75.2 %attention_backward.1 = (bf16[256,512]{1,0:T(8,128)(2,1)}, bf16[8,4,128,128]{3,2,1,0:T(8,128)(2,1)}, f32[4,512]{1,0:T(4,128)}, bf16[8,3,256,256]{3,2,1,0:T(8,128)(2,1)}) custom-call(bf16[1024,2048]{1,0:T(8,128)(2,1)} %get-tuple-element.100.refs_0_, bf16[1024,2048]{1,0:T(8,128)(2,1)} %get-tuple-element.101.refs_1_, ...), custom_call_target="tpu_custom_call" | custom-call | tf_op jit(solution)/shard_map/attention_backward/pallas_call | solution.py:496
  468.3 8.1 %write_results.1 = (bf16[256,512]{1,0:T(8,128)(2,1)}, bf16[256,512]{1,0:T(8,128)(2,1)}, f32[256,512]{1,0:T(8,128)}, f32[256,512]{1,0:T(8,128)}, f32[256,512]{1,0...) custom-call(bf16[8,3,256,256]{3,2,1,0:T(8,128)(2,1)} %get-tuple-elem, ...), custom_call_target="tpu_custom_call" | custom-call | tf_op jit(solution)/shard_map/write_results/pallas_call | solution.py:1815

commit v6 on v5

--- a/solution.py
+++ b/solution.py
@@ -103,6 +103,8 @@
 OPEN_RATE = 2
 DEALT_FIRST = 5
 FORWARD_RATE = 1
+FORWARD_EVERY = 1
+BACK_EVERY = 1
 BACK_RATE = 1
 CLOSE_FIRST = 0
 CLOSE_NEXT = 4
@@ -116,11 +118,15 @@
 class Trickle:
     def __init__(self):
         self.waiting = []
+        self.calls = 0
 
     def add(self, copies):
         self.waiting.extend(copies)
 
-    def tick(self, count=1):
+    def tick(self, count=1, every=1):
+        self.calls += 1
+        if self.calls % every:
+            return
         for start in self.waiting[:count]:
             start()
         self.waiting = self.waiting[count:]
@@ -472,34 +478,50 @@
 
 def comm_call(body, name, number, out_shape, in_specs, out_specs, scratch, lift=True):
     lifted = [i for i, spec in enumerate(in_specs) if spec is VMEM] if lift else []
-
-    def with_loads(*refs):
+    leaving = [i for i, spec in enumerate(out_specs) if spec is VMEM]
+    first_out = len(in_specs)
+
+    def with_copies(*refs):
         refs = list(refs)
-        sems = refs.pop() if lifted else None
-        held = refs[len(refs) - len(lifted) :]
-        refs = refs[: len(refs) - len(lifted)]
-        copies = []
+        sems = refs.pop()
+        count = len(lifted) + len(leaving)
+        held = refs[len(refs) - count :]
+        refs = refs[: len(refs) - count]
+        loads, stores, begun = [], [], []
         for n, i in enumerate(lifted):
-            copies.append(pltpu.make_async_copy(refs[i], held[n], sems.at[n]))
+            loads.append(pltpu.make_async_copy(refs[i], held[n], sems.at[n]))
             refs[i] = held[n]
-        for copy in copies:
+        for n, i in enumerate(leaving, len(lifted)):
+            stores.append((held[n], pltpu.make_async_copy(held[n], refs[first_out + i], sems.at[n])))
+            refs[first_out + i] = held[n]
+        for copy in loads:
             copy.start()
 
         def loaded():
-            for copy in copies:
+            for copy in loads:
                 copy.wait()
 
-        body(*refs, loaded=loaded)
+        def leave(*done):
+            for ref, copy in stores:
+                if any(ref is other for other in done):
+                    copy.start()
+                    begun.append(ref)
+
+        body(*refs, loaded=loaded, leave=leave)
+        leave(*[ref for ref, _ in stores if not any(ref is other for other in begun)])
+        for _, copy in stores:
+            copy.wait()
 
     def call(*args):
         extra = [pltpu.VMEM(args[i].shape, args[i].dtype) for i in lifted]
+        extra += [pltpu.VMEM(out_shape[i].shape, out_shape[i].dtype) for i in leaving]
         return pl.pallas_call(
-            with_loads,
+            with_copies,
             name=name,
             out_shape=out_shape,
             in_specs=[ANY if i in lifted else spec for i, spec in enumerate(in_specs)],
-            out_specs=out_specs,
-            scratch_shapes=[*scratch, *extra, *([DMA((len(lifted),))] if lifted else [])],
+            out_specs=tuple(ANY for _ in out_specs),
+            scratch_shapes=[*scratch, *extra, DMA((len(extra),))],
             compiler_params=pltpu.CompilerParams(
                 collective_id=number, has_side_effects=True, vmem_limit_bytes=BIG_VMEM
             ),
@@ -574,7 +596,7 @@
     hidden = w_gate.shape[1]
     down = hidden // 8
 
-    def body(*refs, loaded):
+    def body(*refs, loaded, leave):
         (in_ref, cot_ref, wq_ref, wk_ref, wv_ref, wo_ref, wg_ref, wu_ref, wd_ref) = refs[:9]
         gain_parts = refs[9:13]
         (order_ref, lengths_ref, frequency_ref) = refs[13:16]
@@ -844,6 +866,7 @@
                 sine = jnp.sin(angles)
                 left = lax.broadcasted_iota(jnp.int32, (HD, HD), 1) < HD // 2
                 sin_ref[piece, :] = jnp.where(left, -sine, sine)
+            leave(cos_ref, sin_ref, low_ref, high_ref, log_ref)
 
         between = [
             deal_all,
@@ -898,6 +921,7 @@
                 for c in range(8):
                     for copy in share(c, 1 - k):
                         copy.wait_recv()
+                leave(wqkv_ref, wout_ref)
             at = pl.ds(pl.multiple_of(near_first(step, z) * 2 * half, 2 * half), 2 * half)
             tile = full_ref[at, :]
             q_ref[at, :] = jnp.dot(tile, wqkv_ref[0], preferred_element_type=F32)
@@ -1084,7 +1108,7 @@
     hidden = gu_stage.shape[2] // 8
     part = width // 8
 
-    def body(*refs, loaded):
+    def body(*refs, loaded, leave):
         (q_in, k_in, v_in, cos_ref, sin_ref, low_ref, high_ref, log_ref, source_ref, wout_ref, gain_ref) = refs[:11]
         (gu_ref, d_ref) = refs[11:13]
         (full_ref, own_ref, branch_ref, wgu_ref, d_other_ref, qrot_ref, keys_ref, values_ref, o_ref, lse_ref, scale_ref) = refs[13:24]
@@ -1201,7 +1225,8 @@
             TURNS_ATTENTION[0],
             produce,
             finish,
-            tick=lambda: trickle.tick(FORWARD_RATE),
+            lambda: leave(qrot_ref, keys_ref, values_ref, o_ref, lse_ref, scale_ref),
+            lambda: trickle.tick(FORWARD_RATE, FORWARD_EVERY),
         )
         view = gather_view(full_ref, rows)
         keep = pltpu.make_async_copy(shard, view(own), local)
@@ -1236,7 +1261,8 @@
             view,
             rest[N_REDUCE:],
             TURNS_ATTENTION[1],
-            tick=lambda: trickle.tick(FORWARD_RATE),
+            lambda step: leave(own_ref, branch_ref) if step == 0 else None,
+            tick=lambda: trickle.tick(FORWARD_RATE, FORWARD_EVERY),
         )
         trickle.flush()
         ffn_own.wait()
@@ -1298,7 +1324,7 @@
     rows, group = tokens // 16, tokens // 4
     hidden = 2 * down_w[0].shape[0]
 
-    def body(*refs, loaded):
+    def body(*refs, loaded, leave):
         (h_any, gu_any, d_any, d_any2, res_ref, cot_ref, gain_ref) = refs[:7]
         (full_ref, out_ref, gg_ref, for_gate_out, for_up_out, m_out) = refs[7:13]
         (hs, gu, dw, terms, shard, result, load_sem, local, out_send, out_recv) = refs[13:23]
@@ -1475,7 +1501,7 @@
     turned = (((1,), (1,)), ((), ()))
     scaling = 1.0 / math.sqrt(HD)
 
-    def body(*refs, loaded):
+    def body(*refs, loaded, leave):
         (df_any, h_any, gu_any, d_any, d_any2, fg_any, fu_any, m_any, cot_ref, branch_ref, gain_ref) = refs[:11]
         (wout_ref, qrot_ref, keys_ref, values_ref, o_ref, lse_ref, low_ref, high_ref, log_ref) = refs[11:20]
         (full_ref, own_ref, gg_ref, in_ref, rest_ref, dq_ref, dk_ref, dv_ref) = refs[20:28]
@@ -1594,7 +1620,7 @@
         def tick():
             if begun:
                 next_part()
-            trickle.tick(BACK_RATE)
+            trickle.tick(BACK_RATE, BACK_EVERY)
 
         def da_load(step):
             at = pl.ds(pl.multiple_of(near_first(step, z) * group, group), group)
@@ -1674,7 +1700,8 @@
             view,
             scratch[N_REDUCE:],
             TURNS_FFN_BACK[1],
-            arrived=arrived,
+            lambda step: leave(own_ref, gg_ref) if step == 0 else None,
+            arrived,
             tick=tick,
             early=EARLY_LAYERS,
         )
@@ -1892,7 +1919,7 @@
     rows, group = tokens // 16, tokens // 4
     part = width // 4
 
-    def body(*refs, loaded):
+    def body(*refs, loaded, leave):
         (da_any, x_any) = refs[:2]
         (q_ref, k_ref, o_ref, dq_in, dk_in, dv_in, cos_ref, sin_ref) = refs[2:10]
         (scale_ref, gain_ref, wqkv_ref) = refs[10:13]

time: 483 us -> 480 us (level)
  no operation moved by 1% of the time
where the time goes in v6:
time: 480 us; the launch traced here: 474 us
  Pallas kernels  472 us (98%)
    pallas_call x5, Pallas kernels, call(): pl.pallas_call(with_copies, name=name, out_shape=out_shape, in_specs=[ANY...  464 us

profile of v6, /device:TPU:1, one launch (start us, length us, event | category | flops | bytes accessed | tf_op | source)
XLA Modules:
  0.0 473.6 jit_solution(11846672550811046864)
XLA Ops:
  0.7 71.9 %open_layer.1 = (bf16[1024,2048]{1,0:T(8,128)(2,1)}, bf16[64,2048]{1,0:T(8,128)(2,1)}, bf16[64,2048]{1,0:T(8,128)(2,1)}, bf16[3,2048,128]{2,1,0:T(8,128)(2,1)}, ...) custom-call(bf16[256,512]{1,0:T(8,128)(2,1)} %refs_0_.1, ...), custom_call_target="tpu_custom_call" | custom-call | tf_op jit(solution)/shard_map/open_layer/pallas_call | solution.py:518
  72.6 110.9 %attention_forward.1 = (bf16[1024,2048]{1,0:T(8,128)(2,1)}, f32[64,2048]{1,0:T(8,128)}, f32[64,2048]{1,0:T(8,128)}, bf16[2,2048,512]{2,1,0:T(8,128)(2,1)}, bf16[...) custom-call(f32[1024,128]{1,0:T(8,128)} %get-tuple-element.71.refs_0, ...), custom_call_target="tpu_custom_call" | custom-call | tf_op jit(solution)/shard_map/attention_forward/pallas_call | solution.py:518
  183.4 83.9 %ffn_forward.1 = (bf16[1024,2048]{1,0:T(8,128)(2,1)}, bf16[256,512]{1,0:T(8,128)(2,1)}, f32[8,2048]{1,0:T(8,128)}, f32[1024,512]{1,0:T(8,128)}, f32[1024,512]{1,0:T(8,128)}, /*index=5*/bf16[1024,512]{1,0:T(8,128)(2,1)}) custom-call(bf16[1024,2048]{1,0:T(8,128)(2,1)} %get-tuple-element.84.refs_0_.refs_1_, ...), custom_call_target="tpu_custom_call" | custom-call | tf_op jit(solution)/shard_map/ffn_forward/pallas_call | solution.py:518
  267.4 123.4 %ffn_backward.1 = (bf16[1024,2048]{1,0:T(8,128)(2,1)}, f32[64,2048]{1,0:T(8,128)}, f32[8,2048]{1,0:T(8,128)}, bf16[8,3,256,256]{3,2,1,0:T(8,128)(2,1)}, bf16[2,3...) custom-call(bf16[1024,2048]{1,0:T(8,128)(2,1)} %get-tuple-element.89.refs_0_, ...), custom_call_target="tpu_custom_call" | custom-call | tf_op jit(solution)/shard_map/ffn_backward/pallas_call | solution.py:518
  390.8 74.2 %attention_backward.1 = (bf16[256,512]{1,0:T(8,128)(2,1)}, bf16[8,4,128,128]{3,2,1,0:T(8,128)(2,1)}, f32[4,512]{1,0:T(4,128)}, bf16[8,3,256,256]{3,2,1,0:T(8,128)(2,1)}) custom-call(bf16[1024,2048]{1,0:T(8,128)(2,1)} %get-tuple-element.100.refs_0_, bf16[1024,2048]{1,0:T(8,128)(2,1)} %get-tuple-element.101.refs_1_, ...), custom_call_target="tpu_custom_call" | custom-call | tf_op jit(solution)/shard_map/attention_backward/pallas_call | solution.py:518
  465.1 8.1 %write_results.1 = (bf16[256,512]{1,0:T(8,128)(2,1)}, bf16[256,512]{1,0:T(8,128)(2,1)}, f32[256,512]{1,0:T(8,128)}, f32[256,512]{1,0:T(8,128)}, f32[256,512]{1,0...) custom-call(bf16[8,3,256,256]{3,2,1,0:T(8,128)(2,1)} %get-tuple-elem, ...), custom_call_target="tpu_custom_call" | custom-call | tf_op jit(solution)/shard_map/write_results/pallas_call | solution.py:1842

commit v7 on v6

--- a/solution.py
+++ b/solution.py
@@ -1797,52 +1797,67 @@
 
 def write_results(early, late, wall, outputs, input_grad, gains):
     part = early.shape[2]
-
-    def body(early_ref, late_ref, wall_ref, out_ref, in_ref, gain_ref, *results):
-        (out_to, in_to, gq, gk, gv, go, gg, gu, gd, *gains_to) = results
-        n = pl.program_id(0)
-
-        @pl.when(n == 0)
-        def _():
-            out_to[...] = out_ref[...]
-            in_to[...] = in_ref[...]
-            for i, ref in enumerate(gains_to):
-                ref[...] = gain_ref[i : i + 1, :]
-
-        for i, ref in enumerate((gq, gk, gv, go)):
-            ref[...] = wall_ref[0, i].astype(F32)
-
-        @pl.when(n <= EARLY)
-        def _():
-            for i, ref in enumerate((gg, gu, gd)):
-                ref[...] = early_ref[0, i].astype(F32)
-
-        @pl.when(n > EARLY)
-        def _():
-            for i, ref in enumerate((gg, gu, gd)):
-                ref[...] = late_ref[0, i].astype(F32)
+    rows, columns = outputs.shape
+
+    def body(*refs):
+        (early_ref, late_ref, wall_ref, out_ref, in_ref, gain_ref) = refs[:6]
+        (out_to, in_to, gq, gk, gv, go, gg, gu, gd) = refs[6:15]
+        gains_to = refs[15:19]
+        (blob, wall_in, wide, wall_wide, out_wide, load_sem, store_sem, wall_sem) = refs[19:]
+        ctx = lax.axis_index("z") * 2 + lax.axis_index("y")
+        loads, stores = [], []
+        for n, t in enumerate((0, *DEAL_ORDER)):
+            c = lax.rem(ctx + 8 - t, 8)
+            source = early_ref if n <= EARLY else late_ref
+            loads.append(pltpu.make_async_copy(source.at[c], blob.at[n], load_sem.at[n]))
+            at = pl.ds(pl.multiple_of(c * part, part), part)
+            ends = (gg.at[:, at], gu.at[:, at], gd.at[at, :])
+            stores.append(
+                [
+                    pltpu.make_async_copy(wide.at[n, i], end, store_sem.at[n, i])
+                    for i, end in enumerate(ends)
+                ]
+            )
+        wall_load = pltpu.make_async_copy(wall_ref, wall_in, wall_sem.at[0])
+        for copy in (*loads, wall_load):
+            copy.start()
+        for i, ref in enumerate(gains_to):
+            ref[...] = gain_ref[i : i + 1, :]
+        out_to[...] = out_ref[...]
+        in_to[...] = in_ref[...]
+        for n in range(8):
+            loads[n].wait()
+            for i in range(3):
+
+                def work(strip, n=n, i=i):
+                    wide[n, i, strip] = blob[n, i, strip].astype(F32)
+
+                strips(part, work, 64)
+                stores[n][i].start()
+        wall_load.wait()
+        for n in range(8):
+            j, r = n // 2, n % 2
+            for i in range(3):
+                wall_wide[i, r * HD : (r + 1) * HD, j * HD : (j + 1) * HD] = wall_in[n, i].astype(F32)
+            out_wide[j * HD : (j + 1) * HD, r * HD : (r + 1) * HD] = wall_in[n, 3].astype(F32)
+        last = [
+            pltpu.make_async_copy(wall_wide.at[i], ref, wall_sem.at[1 + i])
+            for i, ref in enumerate((gq, gk, gv))
+        ]
+        last.append(pltpu.make_async_copy(out_wide, go, wall_sem.at[4]))
+        for copy in last:
+            copy.start()
+        for copy in last:
+            copy.wait()
+        for group in stores:
+            for copy in group:
+                copy.wait()
 
     shape = jax.ShapeDtypeStruct
-    spec = pl.BlockSpec
-
-    def source(n):
-        ctx = lax.axis_index("z") * 2 + lax.axis_index("y")
-        odd = lax.rem(n, 2)
-        t = odd * (4 + n // 2) + (1 - odd) * (n // 2)
-        return lax.rem(ctx + 8 - t, 8)
-
-    rows, columns = outputs.shape
-    whole = spec((rows, columns), lambda n: (0, 0))
-    in_row = spec((HD, HD), lambda n: (source(n) % 2, source(n) // 2))
-    in_column = spec((HD, HD), lambda n: (source(n) // 2, source(n) % 2))
-    side = spec((part, part), lambda n: (0, source(n)))
-    gain_spec = spec(gains.shape, lambda n: (0, 0))
-    gain_row = spec((1, gains.shape[1]), lambda n: (0, 0))
-    blob = (1, 3, part, part)
+    vmem = pltpu.VMEM
     return pl.pallas_call(
         body,
         name="write_results",
-        grid=(8,),
         out_shape=(
             shape((rows, columns), BF),
             shape((rows, columns), BF),
@@ -1855,26 +1870,18 @@
             shape((8 * part, part), F32),
             *[shape((1, gains.shape[1]), F32)] * 4,
         ),
-        in_specs=[
-            spec(blob, lambda n: (source(jnp.minimum(n, EARLY)), 0, 0, 0)),
-            spec(blob, lambda n: (source(jnp.maximum(n, EARLY + 1)), 0, 0, 0)),
-            spec((1, 4, HD, HD), lambda n: (source(n), 0, 0, 0)),
-            whole,
-            whole,
-            gain_spec,
+        in_specs=[ANY, ANY, ANY, VMEM, VMEM, VMEM],
+        out_specs=(VMEM, VMEM, *[ANY] * 7, *[VMEM] * 4),
+        scratch_shapes=[
+            vmem((8, 3, part, part), BF),
+            vmem((8, 4, HD, HD), BF),
+            vmem((8, 3, part, part), F32),
+            vmem((3, 2 * HD, 4 * HD), F32),
+            vmem((4 * HD, 2 * HD), F32),
+            DMA((8,)),
+            DMA((8, 3)),
+            DMA((5,)),
         ],
-        out_specs=(
-            whole,
-            whole,
-            in_row,
-            in_row,
-            in_row,
-            in_column,
-            side,
-            side,
-            spec((part, part), lambda n: (source(n), 0)),
-            *[gain_row] * 4,
-        ),
         compiler_params=pltpu.CompilerParams(vmem_limit_bytes=BIG_VMEM),
     )(early, late, wall, outputs, input_grad, gains)
 

time: 480 us -> 478 us (level)
  no operation moved by 1% of the time
where the time goes in v7:
time: 478 us; the launch traced here: 472 us
  Pallas kernels  471 us (99%)
    pallas_call x5, Pallas kernels, call(): pl.pallas_call(with_copies, name=name, out_shape=out_shape, in_specs=[ANY...  464 us

profile of v7, /device:TPU:1, one launch (start us, length us, event | category | flops | bytes accessed | tf_op | source)
XLA Modules:
  0.0 472.0 jit_solution(10390115609846007514)
XLA Ops:
  0.7 71.9 %open_layer.1 = (bf16[1024,2048]{1,0:T(8,128)(2,1)}, bf16[64,2048]{1,0:T(8,128)(2,1)}, bf16[64,2048]{1,0:T(8,128)(2,1)}, bf16[3,2048,128]{2,1,0:T(8,128)(2,1)}, ...) custom-call(bf16[256,512]{1,0:T(8,128)(2,1)} %refs_0_.1, ...), custom_call_target="tpu_custom_call" | custom-call | tf_op jit(solution)/shard_map/open_layer/pallas_call | solution.py:518
  72.6 110.9 %attention_forward.1 = (bf16[1024,2048]{1,0:T(8,128)(2,1)}, f32[64,2048]{1,0:T(8,128)}, f32[64,2048]{1,0:T(8,128)}, bf16[2,2048,512]{2,1,0:T(8,128)(2,1)}, bf16[...) custom-call(f32[1024,128]{1,0:T(8,128)} %get-tuple-element.71.refs_0, ...), custom_call_target="tpu_custom_call" | custom-call | tf_op jit(solution)/shard_map/attention_forward/pallas_call | solution.py:518
  183.4 83.9 %ffn_forward.1 = (bf16[1024,2048]{1,0:T(8,128)(2,1)}, bf16[256,512]{1,0:T(8,128)(2,1)}, f32[8,2048]{1,0:T(8,128)}, f32[1024,512]{1,0:T(8,128)}, f32[1024,512]{1,0:T(8,128)}, /*index=5*/bf16[1024,512]{1,0:T(8,128)(2,1)}) custom-call(bf16[1024,2048]{1,0:T(8,128)(2,1)} %get-tuple-element.84.refs_0_.refs_1_, ...), custom_call_target="tpu_custom_call" | custom-call | tf_op jit(solution)/shard_map/ffn_forward/pallas_call | solution.py:518
  267.4 123.4 %ffn_backward.1 = (bf16[1024,2048]{1,0:T(8,128)(2,1)}, f32[64,2048]{1,0:T(8,128)}, f32[8,2048]{1,0:T(8,128)}, bf16[8,3,256,256]{3,2,1,0:T(8,128)(2,1)}, bf16[2,3...) custom-call(bf16[1024,2048]{1,0:T(8,128)(2,1)} %get-tuple-element.89.refs_0_, ...), custom_call_target="tpu_custom_call" | custom-call | tf_op jit(solution)/shard_map/ffn_backward/pallas_call | solution.py:518
  390.8 74.2 %attention_backward.1 = (bf16[256,512]{1,0:T(8,128)(2,1)}, bf16[8,4,128,128]{3,2,1,0:T(8,128)(2,1)}, f32[4,512]{1,0:T(4,128)}, bf16[8,3,256,256]{3,2,1,0:T(8,128)(2,1)}) custom-call(bf16[1024,2048]{1,0:T(8,128)(2,1)} %get-tuple-element.100.refs_0_, bf16[1024,2048]{1,0:T(8,128)(2,1)} %get-tuple-element.101.refs_1_, ...), custom_call_target="tpu_custom_call" | custom-call | tf_op jit(solution)/shard_map/attention_backward/pallas_call | solution.py:518
  465.1 6.5 %write_results.1 = (bf16[256,512]{1,0:T(8,128)(2,1)}, bf16[256,512]{1,0:T(8,128)(2,1)}, f32[256,512]{1,0:T(8,128)}, f32[256,512]{1,0:T(8,128)}, f32[256,512]{1,0...) custom-call(bf16[8,3,256,256]{3,2,1,0:T(8,128)(2,1)} %get-tuple-elem, ...), custom_call_target="tpu_custom_call" | custom-call | tf_op jit(solution)/shard_map/write_results/pallas_call | solution.py:1858

commit v8 on v7

--- a/solution.py
+++ b/solution.py
@@ -110,7 +110,7 @@
 CLOSE_NEXT = 4
 SUM_LAG = 1
 EARLY_LAYERS = True
-BACK_LAG = 1
+BACK_LAG = 2
 CLOSE_LAG = 2
 CLOSE_RATE = 1
 
@@ -1440,7 +1440,7 @@
 
 
 EARLY = 5
-GRADS_FIRST = 3
+GRADS_FIRST = 4
 
 
 def grad_copies(me, src, dst, send, recv, t):

time: 478 us -> 478 us (level)
  no operation moved by 1% of the time
where the time goes in v8:
time: 478 us; the launch traced here: 471 us
  Pallas kernels  470 us (98%)
    pallas_call x5, Pallas kernels, call(): pl.pallas_call(with_copies, name=name, out_shape=out_shape, in_specs=[ANY...  464 us

profile of v8, /device:TPU:1, one launch (start us, length us, event | category | flops | bytes accessed | tf_op | source)
XLA Modules:
  0.0 471.4 jit_solution(2638884954952988387)
XLA Ops:
  0.7 71.9 %open_layer.1 = (bf16[1024,2048]{1,0:T(8,128)(2,1)}, bf16[64,2048]{1,0:T(8,128)(2,1)}, bf16[64,2048]{1,0:T(8,128)(2,1)}, bf16[3,2048,128]{2,1,0:T(8,128)(2,1)}, ...) custom-call(bf16[256,512]{1,0:T(8,128)(2,1)} %refs_0_.1, ...), custom_call_target="tpu_custom_call" | custom-call | tf_op jit(solution)/shard_map/open_layer/pallas_call | solution.py:518
  72.6 110.8 %attention_forward.1 = (bf16[1024,2048]{1,0:T(8,128)(2,1)}, f32[64,2048]{1,0:T(8,128)}, f32[64,2048]{1,0:T(8,128)}, bf16[2,2048,512]{2,1,0:T(8,128)(2,1)}, bf16[...) custom-call(f32[1024,128]{1,0:T(8,128)} %get-tuple-element.71.refs_0, ...), custom_call_target="tpu_custom_call" | custom-call | tf_op jit(solution)/shard_map/attention_forward/pallas_call | solution.py:518
  183.4 84.2 %ffn_forward.1 = (bf16[1024,2048]{1,0:T(8,128)(2,1)}, bf16[256,512]{1,0:T(8,128)(2,1)}, f32[8,2048]{1,0:T(8,128)}, f32[1024,512]{1,0:T(8,128)}, f32[1024,512]{1,0:T(8,128)}, /*index=5*/bf16[1024,512]{1,0:T(8,128)(2,1)}) custom-call(bf16[1024,2048]{1,0:T(8,128)(2,1)} %get-tuple-element.84.refs_0_.refs_1_, ...), custom_call_target="tpu_custom_call" | custom-call | tf_op jit(solution)/shard_map/ffn_forward/pallas_call | solution.py:518
  267.7 122.9 %ffn_backward.1 = (bf16[1024,2048]{1,0:T(8,128)(2,1)}, f32[64,2048]{1,0:T(8,128)}, f32[8,2048]{1,0:T(8,128)}, bf16[8,3,256,256]{3,2,1,0:T(8,128)(2,1)}, bf16[2,3...) custom-call(bf16[1024,2048]{1,0:T(8,128)(2,1)} %get-tuple-element.89.refs_0_, ...), custom_call_target="tpu_custom_call" | custom-call | tf_op jit(solution)/shard_map/ffn_backward/pallas_call | solution.py:518
  390.6 74.0 %attention_backward.1 = (bf16[256,512]{1,0:T(8,128)(2,1)}, bf16[8,4,128,128]{3,2,1,0:T(8,128)(2,1)}, f32[4,512]{1,0:T(4,128)}, bf16[8,3,256,256]{3,2,1,0:T(8,128)(2,1)}) custom-call(bf16[1024,2048]{1,0:T(8,128)(2,1)} %get-tuple-element.100.refs_0_, bf16[1024,2048]{1,0:T(8,128)(2,1)} %get-tuple-element.101.refs_1_, ...), custom_call_target="tpu_custom_call" | custom-call | tf_op jit(solution)/shard_map/attention_backward/pallas_call | solution.py:518
  464.6 6.5 %write_results.1 = (bf16[256,512]{1,0:T(8,128)(2,1)}, bf16[256,512]{1,0:T(8,128)(2,1)}, f32[256,512]{1,0:T(8,128)}, f32[256,512]{1,0:T(8,128)}, f32[256,512]{1,0...) custom-call(bf16[8,3,256,256]{3,2,1,0:T(8,128)(2,1)} %get-tuple-elem, ...), custom_call_target="tpu_custom_call" | custom-call | tf_op jit(solution)/shard_map/write_results/pallas_call | solution.py:1858
